TPU v7x, 128 devices: a whole 4x4x4 slice. The times are simulated.
128 devices in a mesh: depth: 16 (over z_lo, x, core), rows: 8 (over z_hi, y).
Axes of the slice: x: 4, y: 4, z: 4 (z_hi: 2, z_lo: 2; z = z_hi * 2 + z_lo), core: 2. Of those that a mesh axis runs over, the one named last changes fastest.
Arguments:
- x_now: float32 [2, 16, 2048, 2048], P(None, 'depth', 'rows'), may hold values from -150 to 150
- x_prev: float32 [2, 16, 2048, 2048], P(None, 'depth', 'rows'), may hold values from -6 to 6
- hologram: float32 [2, 2048, 2048], P(None, 'rows'), may hold values from -48 to 48
- depths: float32 [16], P('depth'), may hold values from 150 to 600
Outputs:
- x_next: float32 [2, 16, 2048, 2048], P(None, 'depth', 'rows')
All inputs are finite; a program needn't handle non-finite values.
Results may differ from a plain program's by a relative error of at most 0.00016.
Values sent between devices are 32-bit elements; how exact they have to be, the bound alone decides.
No kernel may reach another device: no remote copies, remote signals or barrier semaphores. Data moves between devices by JAX's collectives and lax.ppermute only.
A program may use at most 192 MiB of HBM per device.

v0:
```python
import math

import jax
import jax.numpy as jnp
from jax import lax
from jax.sharding import PartitionSpec as P

TV_ITERS = 2


ALPHA_TWIST = 1.8
BETA_TWIST = 1.2
LAMBDA_TV = 0.2
STEP_TV = 1.0 / 12.0
EPSILON = 1e-06
WAVENUMBER = 4.0 * math.pi
HIGHEST = lax.Precision.HIGHEST


def from_behind(x, axis, by):
    count = lax.axis_size(axis)
    pairs = [(i, i + by) for i in range(count) if 0 <= i + by < count]
    return lax.ppermute(x, axis, pairs)


def phase_rate(qx_grid, qy_grid):
    square = qx_grid * qx_grid + qy_grid * qy_grid
    return -square / (WAVENUMBER + jnp.sqrt(WAVENUMBER * WAVENUMBER - square))


def split_length(total):
    inner = min(total, 128)
    return (total // inner, inner)


def storage_freq(storage, total):
    outer, inner = split_length(total)
    freq = storage // inner + outer * (storage % inner)
    signed = jnp.where(freq < total // 2, freq, freq - total)
    return signed.astype(jnp.float32) * (2.0 * math.pi / total)


def dft_tables(length, sign):
    index = jnp.arange(length, dtype=jnp.int32)
    product = index[:, None] * index[None, :] % length
    angle = product.astype(jnp.float32) * (sign * 2.0 * math.pi / length)
    factor = 1.0 / math.sqrt(length)
    return (jnp.cos(angle) * factor, jnp.sin(angle) * factor)


def twiddle(outer, inner, total, sign):
    product = (
        jnp.arange(outer, dtype=jnp.int32)[:, None]
        * jnp.arange(inner, dtype=jnp.int32)[None, :]
        % total
    )
    angle = product.astype(jnp.float32) * (sign * 2.0 * math.pi / total)
    return (jnp.cos(angle), jnp.sin(angle))


def complex_einsum(form, left, right):

    def single(first, second):
        return jnp.einsum(form, first, second, precision=HIGHEST)

    return (
        single(left[0], right[0]) - single(left[1], right[1]),
        single(left[0], right[1]) + single(left[1], right[0]),
    )


def complex_times(left, right):
    return (left[0] * right[0] - left[1] * right[1], left[0] * right[1] + left[1] * right[0])


def forward_last(pair):
    total = pair[0].shape[-1]
    outer, inner = split_length(total)
    lead = pair[0].shape[:-1]
    shaped = (pair[0].reshape(lead + (outer, inner)), pair[1].reshape(lead + (outer, inner)))
    step = complex_einsum("...ij,ik->...kj", shaped, dft_tables(outer, -1.0))
    step = complex_times(step, twiddle(outer, inner, total, -1.0))
    step = complex_einsum("...kj,jl->...kl", step, dft_tables(inner, -1.0))
    return (step[0].reshape(lead + (total,)), step[1].reshape(lead + (total,)))


def inverse_last(pair):
    total = pair[0].shape[-1]
    outer, inner = split_length(total)
    lead = pair[0].shape[:-1]
    shaped = (pair[0].reshape(lead + (outer, inner)), pair[1].reshape(lead + (outer, inner)))
    step = complex_einsum("...kl,lj->...kj", shaped, dft_tables(inner, 1.0))
    step = complex_times(step, twiddle(outer, inner, total, 1.0))
    step = complex_einsum("...kj,ki->...ij", step, dft_tables(outer, 1.0))
    return (step[0].reshape(lead + (total,)), step[1].reshape(lead + (total,)))


def forward_first(pair):
    items, total, cols = pair[0].shape
    outer, inner = split_length(total)
    shaped = (
        pair[0].reshape(items, outer, inner, cols),
        pair[1].reshape(items, outer, inner, cols),
    )
    step = complex_einsum("aijc,ik->akjc", shaped, dft_tables(outer, -1.0))
    turn = twiddle(outer, inner, total, -1.0)
    step = complex_times(step, (turn[0][:, :, None], turn[1][:, :, None]))
    step = complex_einsum("akjc,jl->aklc", step, dft_tables(inner, -1.0))
    return (step[0].reshape(items, total, cols), step[1].reshape(items, total, cols))


def inverse_first(pair):
    items, total, cols = pair[0].shape
    outer, inner = split_length(total)
    shaped = (
        pair[0].reshape(items, outer, inner, cols),
        pair[1].reshape(items, outer, inner, cols),
    )
    step = complex_einsum("aklc,lj->akjc", shaped, dft_tables(inner, 1.0))
    turn = twiddle(outer, inner, total, 1.0)
    step = complex_times(step, (turn[0][:, :, None], turn[1][:, :, None]))
    step = complex_einsum("akjc,ki->aijc", step, dft_tables(outer, 1.0))
    return (step[0].reshape(items, total, cols), step[1].reshape(items, total, cols))


def back_to_space(back_re, back_im, x_now, planes):
    column_done = inverse_first((back_re, back_im))
    spatial = inverse_last(
        (
            lax.all_to_all(column_done[0], "rows", split_axis=1, concat_axis=2, tiled=True),
            lax.all_to_all(column_done[1], "rows", split_axis=1, concat_axis=2, tiled=True),
        )
    )
    return jnp.stack([x_now[0] + spatial[0] / planes, x_now[1] + spatial[1] / planes])


def denoise(field, strength, next_plane, prev_plane, next_row, prev_row, plane_keep, row_keep):

    def divergence(dual_z, dual_y, dual_x):
        part_z = dual_z - jnp.concatenate([prev_plane(dual_z), dual_z[:, :-1]], axis=1)
        part_y = dual_y - jnp.concatenate([prev_row(dual_y), dual_y[:, :, :-1]], axis=2)
        part_x = dual_x - jnp.concatenate(
            [jnp.zeros_like(dual_x[:, :, :, :1]), dual_x[:, :, :, :-1]], axis=3
        )
        return part_z + part_y + part_x

    scaled = field / strength
    duals = None
    for step in range(TV_ITERS):
        if step == 0:
            inner = -scaled
        else:
            inner = divergence(*duals) - scaled
        grad_z = jnp.where(
            plane_keep, jnp.concatenate([inner[:, 1:], next_plane(inner)], axis=1) - inner, 0.0
        )
        grad_y = jnp.where(
            row_keep, jnp.concatenate([inner[:, :, 1:], next_row(inner)], axis=2) - inner, 0.0
        )
        zero_col = jnp.zeros_like(inner[:, :, :, :1])
        grad_x = jnp.concatenate([inner[:, :, :, 1:] - inner[:, :, :, :-1], zero_col], axis=3)
        grad_z, grad_y, grad_x = (grad_z, grad_y, grad_x)
        denom = 1.0 + STEP_TV * jnp.sqrt(grad_z * grad_z + grad_y * grad_y + grad_x * grad_x)
        if step == 0:
            duals = (STEP_TV * grad_z / denom, STEP_TV * grad_y / denom, STEP_TV * grad_x / denom)
        else:
            duals = (
                (duals[0] + STEP_TV * grad_z) / denom,
                (duals[1] + STEP_TV * grad_y) / denom,
                (duals[2] + STEP_TV * grad_x) / denom,
            )
    return field - strength * divergence(*duals)


def shards(x_now, x_prev, hologram, depths):
    planes_loc = x_now.shape[1]
    rows_loc = x_now.shape[2]
    width = x_now.shape[3]
    depth_count = lax.axis_size("depth")
    row_count = lax.axis_size("rows")
    planes = planes_loc * depth_count
    cols_loc = width // row_count
    stacked = jnp.concatenate([x_now, hologram[:, None]], axis=1)
    row_done = forward_last((stacked[0], stacked[1]))
    spec_re, spec_im = forward_first(
        (
            lax.all_to_all(row_done[0], "rows", split_axis=2, concat_axis=1, tiled=True),
            lax.all_to_all(row_done[1], "rows", split_axis=2, concat_axis=1, tiled=True),
        )
    )
    obj_re = spec_re[:planes_loc]
    obj_im = spec_im[:planes_loc]
    holo_re = spec_re[planes_loc]
    holo_im = spec_im[planes_loc]
    col_store = lax.axis_index("rows") * cols_loc + jnp.arange(cols_loc, dtype=jnp.int32)
    row_store = jnp.arange(width, dtype=jnp.int32)
    rate = phase_rate(
        storage_freq(col_store, width)[None, :], storage_freq(row_store, width)[:, None]
    )
    phase = depths[:, None, None] * rate[None]
    trans_re = jnp.cos(phase)
    trans_im = jnp.sin(phase)
    local_re = jnp.sum(obj_re * trans_re - obj_im * trans_im, axis=0)
    local_im = jnp.sum(obj_re * trans_im + obj_im * trans_re, axis=0)
    sum_re, sum_im = lax.psum((local_re, local_im), "depth")
    resid_re = holo_re - sum_re
    resid_im = holo_im - sum_im
    back_re = trans_re * resid_re[None] + trans_im * resid_im[None]
    back_im = trans_re * resid_im[None] - trans_im * resid_re[None]
    field = back_to_space(back_re, back_im, x_now, planes)
    total = lax.psum(jnp.sum(field * field), ("depth", "rows"))
    mean_square = total / (2.0 * planes * width * width)
    strength = LAMBDA_TV * jnp.sqrt(mean_square + EPSILON)
    plane_global = lax.axis_index("depth") * planes_loc + jnp.arange(planes_loc, dtype=jnp.int32)
    row_global = lax.axis_index("rows") * rows_loc + jnp.arange(rows_loc, dtype=jnp.int32)
    plane_keep = (plane_global < planes - 1)[None, :, None, None]
    row_keep = (row_global < width - 1)[None, None, :, None]

    def next_plane(inner):
        return from_behind(inner, "depth", -1)

    def prev_plane(dual):
        return from_behind(dual, "depth", 1)

    def next_row(inner):
        return from_behind(inner[:, :, :1], "rows", -1)

    def prev_row(dual):
        return from_behind(dual[:, :, -1:], "rows", 1)

    denoised = denoise(
        field, strength, next_plane, prev_plane, next_row, prev_row, plane_keep, row_keep
    )
    return (1.0 - ALPHA_TWIST) * x_prev + (ALPHA_TWIST - BETA_TWIST) * x_now + BETA_TWIST * denoised


def solution(mesh):
    return jax.shard_map(
        shards,
        mesh=mesh,
        in_specs=(
            P(None, "depth", "rows", None),
            P(None, "depth", "rows", None),
            P(None, "rows", None),
            P("depth"),
        ),
        out_specs=P(None, "depth", "rows", None),
        check_vma=False,
    )
```

profile of v0, /device:TPU:32, one launch (start us, length us, event | category | flops | bytes accessed | tf_op | source)
XLA Modules:
  0.0 851.4 jit_solution(11265779304722274366)
XLA Ops:
  6.6 3.7 fusion
  12.2 4.1 fusion.3
  16.3 4.1 fusion.1
  20.5 4.3 fusion.61
  24.8 5.6 subtract_bitcast_fusion.2
  30.5 5.4 fusion.36
  35.9 5.5 fusion.48
  41.4 12.4 %copy.186 = f32[2,256,2048]{1,0,2:T(2,128)} copy(f32[2,256,2048]{1,2,0:T(8,128)S(1)} %bitcast.265) | data formatting | bytes 8388608 | tf_op jit(solution)/shard_map/reshape | solution.py:84
  53.7 6.9 all-to-all-start.1
  60.6 7.5 fusion.38
  68.2 5.3 fusion.45
  73.4 12.7 %copy.178 = f32[2,256,2048]{1,0,2:T(2,128)} copy(f32[2,256,2048]{1,2,0:T(8,128)S(1)} %bitcast.264) | data formatting | bytes 8388608 | tf_op jit(solution)/shard_map/reshape | solution.py:84
  86.1 25.5 %all-to-all-done.1 = f32[2,256,2048]{1,0,2:T(2,128)} async-done(((f32[2,256,2048]{1,0,2:T(2,128)}), f32[2,256,2048]{1,0,2:T(2,128)}, u32[]{:S(2)}, u32[]{:S(2)}) %all-to-all-start.1) | async-done | bytes 4194336 | tf_op jit(solution)/shard_map/all_to_all | solution.py:188
  111.6 17.1 %all-to-all-start = ((f32[2,256,2048]{1,0,2:T(2,128)}), f32[2,256,2048]{1,0,2:T(2,128)}, u32[]{:S(2)}, u32[]{:S(2)}) async-start(f32[2,256,2048]{1,0,2:T(2,128)} %copy.178), calls=%async_computation | async-start | bytes 8388608 | tf_op jit(solution)/shard_map/all_to_all | solution.py:187
  129.6 4.5 copy.187
  134.2 5.4 copy.188
  139.5 9.9 %fusion.28 = f32[16,2,128,256]{3,0,2,1:T(8,128)} fusion(f32[2,16,128,256]{3,2,1,0:T(8,128)} %bitcast.253), kind=kOutput, calls=%fused_computation.55 | convolution fusion | flops 201330432 | bytes 8388608 | tf_op jit(solution)/shard_map/aijc,ik->akjc/dot_general | solution.py:64
  149.4 6.5 fusion.30
  156.0 22.5 %all-to-all-done = f32[2,256,2048]{1,0,2:T(2,128)} async-done(((f32[2,256,2048]{1,0,2:T(2,128)}), f32[2,256,2048]{1,0,2:T(2,128)}, u32[]{:S(2)}, u32[]{:S(2)}) %all-to-all-start) | async-done | bytes 4194336 | tf_op jit(solution)/shard_map/all_to_all | solution.py:187
  178.5 4.5 copy.179
  183.0 5.5 copy.180
  188.6 9.5 %fusion.51 = f32[16,2,128,256]{3,0,2,1:T(8,128)S(1)} fusion(f32[16,2,128,256]{3,0,2,1:T(8,128)} %fusion.30, f32[2,16,128,256]{3,2,1,0:T(8,128)} %bitcast.246), kind=kOutput, calls=%fused_computation.76 | convolution fusion | flops 202379008 | bytes 12582912 | tf_op jit(solution)/shard_map/aijc,ik->akjc/dot_general | solution.py:64
  198.1 7.3 subtract_bitcast_fusion.1
  205.3 6.3 fusion.20
  211.6 6.8 fusion.22
  218.4 6.2 subtract_bitcast_fusion
  224.7 6.6 add_bitcast_fusion
  233.4 11.5 %fusion.76 = (f32[2048,256]{1,0:T(8,128)}, f32[2048,256]{1,0:T(8,128)}) fusion(f32[1,16,128,256]{3,2,1,0:T(8,128)S(1)} %get-tuple-element.30, f32[1,16,128,256]{3,2,1,0:T(8,128)S(1)} %get-tuple-element.32, f32[2048]{0:T(1024)S(1)} %fusion.146, f32[256]{0:T(256)S(1)} %fusion.173, f32[]{:T(128)} %bitcast.242), kind=kLoop, calls=%fused_computation.96 | loop fusion | flops 6291456 | bytes 8397828 | tf_op jit(solution)/shard_map/add | solution.py:204
  245.1 137.3 %all-reduce.7.cloned.1.call-done = (f32[2048,256]{1,0:T(8,128)}, f32[2048,256]{1,0:T(8,128)}) async-done(((f32[2048,256]{1,0:T(8,128)}, f32[2048,256]{1,0:T(8,128)}), (f32[2048,256]{1,0:T(8,128)}, f32[2048,256]{1,0:T(8,128)})) %all-reduce.7.cloned.1.call-update) | async-done | bytes 4194320 | tf_op jit(solution)/shard_map/psum | solution.py:205
  382.4 11.8 %multiply_subtract_fusion.1 = (f32[2048,256]{1,0:T(8,128)S(1)}, f32[2048,256]{1,0:T(8,128)S(1)}) fusion(f32[2048]{0:T(1024)S(1)} %fusion.146, f32[256]{0:T(256)S(1)} %fusion.173, f32[]{:T(128)} %bitcast.241, f32[2048,256]{1,0:T(8,128)} %get-tuple-element.5, f32[1,16,128,256]{3,2,1,0:T(8,128)} %get-tuple-element.31, f32[2048,256]{1,0:T(8,128)} %get-tuple-element.6, ...), kind=kLoop, calls=%fused_computation.105 | loop fusion | flops 7340032 | bytes 12592132 | tf_op jit(solution)/shard_map/sub | solution.py:209
  400.8 3.0 fusion.72
  403.8 3.1 fusion.87
  411.0 10.0 %copy.209 = f32[1,2048,256]{2,0,1:T(1,128)} copy(f32[1,2048,256]{2,1,0:T(8,128)S(1)} %bitcast.270) | data formatting | bytes 4194304 | tf_op jit(solution)/shard_map/reshape | solution.py:123
  421.0 6.6 all-to-all-start.2
  427.6 4.4 fusion.85
  432.0 2.9 fusion.96
  436.1 10.0 %copy.215 = f32[1,2048,256]{2,0,1:T(1,128)} copy(f32[1,2048,256]{2,1,0:T(8,128)S(1)} %bitcast.271) | data formatting | bytes 4194304 | tf_op jit(solution)/shard_map/reshape | solution.py:123
  446.1 9.2 %all-to-all-done.2 = f32[1,2048,256]{2,0,1:T(1,128)} async-done(((f32[1,2048,256]{2,0,1:T(1,128)}), f32[1,2048,256]{2,0,1:T(1,128)}, u32[]{:S(2)}, u32[]{:S(2)}) %all-to-all-start.2) | async-done | bytes 2097184 | tf_op jit(solution)/shard_map/all_to_all | solution.py:130
  455.4 4.5 all-to-all-start.3
  459.9 3.0 copy.254
  464.8 4.9 fusion.108
  469.7 4.9 fusion.123
  474.6 13.8 %all-to-all-done.3 = f32[1,2048,256]{2,0,1:T(1,128)} async-done(((f32[1,2048,256]{2,0,1:T(1,128)}), f32[1,2048,256]{2,0,1:T(1,128)}, u32[]{:S(2)}, u32[]{:S(2)}) %all-to-all-start.3) | async-done | bytes 2097184 | tf_op jit(solution)/shard_map/all_to_all | solution.py:131
  488.5 3.1 copy.255
  493.7 5.4 convolution_subtract_fusion
  499.1 3.9 multiply_subtract_fusion
  505.9 3.3 fusion.79
  509.2 3.0 multiply_bitcast_fusion.1
  512.2 4.3 multiply_bitcast_fusion
  520.8 4.2 slice_add_fusion.1
  528.1 67.5 %psum.23 = f32[]{:T(128)} all-reduce(f32[]{:T(128)} %multiply_reduce_fusion), channel_id=1, replica_groups=mesh['depth'=16,'rows'=8] {'depth','rows'}, use_global_device_ids=true, to_apply=%region_3.4 | all-reduce | flops 1 | bytes 8 | tf_op jit(solution)/shard_map/psum | solution.py:211
  596.3 4.2 fusion.105
  600.4 3.1 collective-permute-start
  606.0 4.6 slice_subtract_fusion.1
  610.7 5.1 slice.104
  615.8 34.3 %collective-permute-done = f32[2,1,256,2048]{3,2,1,0:T(8,128)} collective-permute-done((f32[2,1,256,2048]{3,2,1,0:T(8,128)}, f32[2,1,256,2048]{3,2,1,0:T(8,128)}, u32[]{:S(2)}, u32[]{:S(2)}) %collective-permute-start) | collective-permute-done | bytes 4194336 | tf_op jit(solution)/shard_map/ppermute | solution.py:23
  650.0 7.1 multiply_divide_fusion.2
  663.0 46.7 %collective-permute-done.2 = f32[2,1,256,2048]{3,2,1,0:T(8,128)S(1)} collective-permute-done((f32[2,1,256,2048]{3,2,1,0:T(8,128)S(1)}, f32[2,1,256,2048]{3,2,1,0:T(8,128)S(1)}, u32[]{:S(2)}, u32[]{:S(2)}) %collective-permute-start.2) | collective-permute-done | bytes 4194336 | tf_op jit(solution)/shard_map/ppermute | solution.py:23
  711.7 5.8 fusion.12
  720.8 3.2 slice_subtract_fusion
  726.4 39.3 %collective-permute-done.4 = f32[2,1,256,2048]{3,2,1,0:T(8,128)} collective-permute-done((f32[2,1,256,2048]{3,2,1,0:T(8,128)S(1)}, f32[2,1,256,2048]{3,2,1,0:T(8,128)}, u32[]{:S(2)}, u32[]{:S(2)}) %collective-permute-start.4) | collective-permute-done | bytes 4194336 | tf_op jit(solution)/shard_map/ppermute | solution.py:23
  765.6 12.4 %add_divide_fusion.2 = (f32[2,1,256,2048]{3,2,1,0:T(8,128)}, f32[2,1,256,2048]{3,2,1,0:T(8,128)}, f32[2,1,256,2048]{3,2,1,0:T(8,128)}) fusion(f32[2,1,256,2048]{3,2,1,0:T(8,128)} %copy-done.8, f32[2,1,256,2048]{3,2,1,0:T(8,128)} %collective-permute-done.4, f32[2,1,256,2048]{3,2,1,0:T(8,128)S(1)} %fusion.12, pred[]{:T(512)S(6)} %lt.181, ...), kind=kLoop, calls=%fused_computation.33 | loop fusion | flops 22020096 | bytes 41941248 | tf_op jit(solution)/shard_map/div | solution.py:168
  784.2 46.7 %collective-permute-done.6 = f32[2,1,256,2048]{3,2,1,0:T(8,128)S(1)} collective-permute-done((f32[2,1,256,2048]{3,2,1,0:T(8,128)}, f32[2,1,256,2048]{3,2,1,0:T(8,128)S(1)}, u32[]{:S(2)}, u32[]{:S(2)}) %collective-permute-start.6) | collective-permute-done | bytes 4194336 | tf_op jit(solution)/shard_map/ppermute | solution.py:23
  830.9 13.5 %fusion.19 = f32[2,1,256,2048]{3,2,1,0:T(8,128)} fusion(f32[2,1,256,2048]{3,2,1,0:T(8,128)} %get-tuple-element.9, f32[2,1,255,2048]{3,2,1,0:T(8,128)} %bitcast.245, f32[2,1,1,2048]{3,2,1,0:T(1,128)S(1)} %collective-permute-done.7, f32[2,1,256,2048]{3,2,1,0:T(8,128)} %get-tuple-element.8, f32[2,1,256,2047]{3,2,1,0:T(8,128)} %bitcast.255, ...), kind=kLoop, calls=%fused_computation.29 | loop fusion | flops 14680064 | bytes 41940996 | tf_op jit(solution)/shard_map/add | solution.py:234
  (67 shorter events, 52.5 us)
Async XLA Ops:
  30.4 5.4 copy-start.7
  30.4 5.4 copy-start.4
  53.7 57.9 %all-to-all-start.1 = ((f32[2,256,2048]{1,0,2:T(2,128)}), f32[2,256,2048]{1,0,2:T(2,128)}, u32[]{:S(2)}, u32[]{:S(2)}) async-start(f32[2,256,2048]{1,0,2:T(2,128)} %copy.186), calls=%async_computation.1 | async-start | bytes 8388608 | tf_op jit(solution)/shard_map/all_to_all | solution.py:188
  60.6 7.5 copy-start.5
  111.6 66.8 %all-to-all-start = ((f32[2,256,2048]{1,0,2:T(2,128)}), f32[2,256,2048]{1,0,2:T(2,128)}, u32[]{:S(2)}, u32[]{:S(2)}) async-start(f32[2,256,2048]{1,0,2:T(2,128)} %copy.178), calls=%async_computation | async-start | bytes 8388608 | tf_op jit(solution)/shard_map/all_to_all | solution.py:187
  128.7 253.7 %all-reduce.7.cloned.1.call-start = ((), (), s32[]{:S(2)}) async-start(), calls=%async_computation.4 | async-start | bytes 8388608 | tf_op jit(solution)/shard_map/psum | solution.py:205
  139.5 9.9 %copy-start.6 = (f32[2,8,256,256]{3,2,1,0:T(8,128)S(1)}, f32[2,8,256,256]{3,2,1,0:T(8,128)}, u32[]{:S(2)}) copy-start(f32[2,8,256,256]{3,2,1,0:T(8,128)} %copy.188) | copy-start | bytes 12582916
  188.5 9.5 %copy-start.3 = (f32[2,8,256,256]{3,2,1,0:T(8,128)S(1)}, f32[2,8,256,256]{3,2,1,0:T(8,128)}, u32[]{:S(2)}) copy-start(f32[2,8,256,256]{3,2,1,0:T(8,128)} %copy.180) | copy-start | bytes 12582916
  188.6 9.5 %copy-start.10 = (f32[16,2,128,256]{3,0,2,1:T(8,128)S(1)}, f32[16,2,128,256]{3,0,2,1:T(8,128)}, u32[]{:S(2)}) copy-start(f32[16,2,128,256]{3,0,2,1:T(8,128)} %fusion.28) | copy-start | bytes 12582916
  403.8 6.0 copy-start.9
  421.0 34.4 %all-to-all-start.2 = ((f32[1,2048,256]{2,0,1:T(1,128)}), f32[1,2048,256]{2,0,1:T(1,128)}, u32[]{:S(2)}, u32[]{:S(2)}) async-start(f32[1,2048,256]{2,0,1:T(1,128)} %copy.209), calls=%async_computation.2 | async-start | bytes 4194304 | tf_op jit(solution)/shard_map/all_to_all | solution.py:130
  455.4 33.1 %all-to-all-start.3 = ((f32[1,2048,256]{2,0,1:T(1,128)}), f32[1,2048,256]{2,0,1:T(1,128)}, u32[]{:S(2)}, u32[]{:S(2)}) async-start(f32[1,2048,256]{2,0,1:T(1,128)} %copy.215), calls=%async_computation.3 | async-start | bytes 4194304 | tf_op jit(solution)/shard_map/all_to_all | solution.py:131
  493.7 5.4 copy-start.11
  525.0 1.4 copy-start
  600.4 49.6 %collective-permute-start = (f32[2,1,256,2048]{3,2,1,0:T(8,128)}, f32[2,1,256,2048]{3,2,1,0:T(8,128)}, u32[]{:S(2)}, u32[]{:S(2)}) collective-permute-start(f32[2,1,256,2048]{3,2,1,0:T(8,128)} %fusion.105), channel_id=1, source_target_pairs={{8,0},{16,8},{24,16},{32,24},{40,32},{48,40},{56,48},{64,56},{72,6... | collective-permute-start | bytes 12582920 | tf_op jit(solution)/shard_map/ppermute | solution.py:23
  604.6 11.2 %collective-permute-start.1 = (f32[2,1,1,2048]{3,2,1,0:T(1,128)S(1)}, f32[2,1,1,2048]{3,2,1,0:T(1,128)S(1)}, u32[]{:S(2)}, u32[]{:S(2)}) collective-permute-start(f32[2,1,1,2048]{3,2,1,0:T(1,128)S(1)} %slice.105), channel_id=1, source_target_pairs={{1,0},{2,1},{3,2},{4,3},{5,4},{6,5},{7,6},{9,8},{10,9},{11,10},{12... | collective-permute-start | bytes 49160 | tf_op jit(solution)/shard_map/ppermute | solution.py:23
  610.6 39.4 %copy-start.1 = (f32[1,1,256,2048]{3,2,1,0:T(8,128)S(1)}, f32[1,1,256,2048]{3,2,1,0:T(8,128)}, u32[]{:S(2)}) copy-start(f32[1,1,256,2048]{3,2,1,0:T(8,128)} %copy-done) | copy-start | bytes 6291460
  657.2 52.5 %copy-start.8 = (f32[2,1,256,2048]{3,2,1,0:T(8,128)}, f32[2,1,256,2048]{3,2,1,0:T(8,128)S(1)}, u32[]{:S(2)}) copy-start(f32[2,1,256,2048]{3,2,1,0:T(8,128)S(1)} %get-tuple-element.10) | copy-start | bytes 12582916
  657.2 60.4 %copy-start.2 = (f32[2,1,256,2048]{3,2,1,0:T(8,128)}, f32[2,1,256,2048]{3,2,1,0:T(8,128)S(1)}, u32[]{:S(2)}) copy-start(f32[2,1,256,2048]{3,2,1,0:T(8,128)S(1)} %get-tuple-element.11) | copy-start | bytes 12582916
  657.2 52.5 %collective-permute-start.2 = (f32[2,1,256,2048]{3,2,1,0:T(8,128)S(1)}, f32[2,1,256,2048]{3,2,1,0:T(8,128)S(1)}, u32[]{:S(2)}, u32[]{:S(2)}) collective-permute-start(f32[2,1,256,2048]{3,2,1,0:T(8,128)S(1)} %get-tuple-element.10), channel_id=1, source_target_pairs={{0,8},{8,16},{16,24},{24,32},{32,40},{40,48},{48,56},{56,64},{64,7... | collective-permute-start | bytes 12582920 | tf_op jit(solution)/shard_map/ppermute | solution.py:23
  659.3 3.7 collective-permute-start.3
  709.7 2.0 copy-start.12
  717.6 48.0 %collective-permute-start.4 = (f32[2,1,256,2048]{3,2,1,0:T(8,128)S(1)}, f32[2,1,256,2048]{3,2,1,0:T(8,128)}, u32[]{:S(2)}, u32[]{:S(2)}) collective-permute-start(f32[2,1,256,2048]{3,2,1,0:T(8,128)S(1)} %fusion.12), channel_id=1, source_target_pairs={{8,0},{16,8},{24,16},{32,24},{40,32},{48,40},{56,48},{64,56},{72,6... | collective-permute-start | bytes 12582920 | tf_op jit(solution)/shard_map/ppermute | solution.py:23
  719.5 6.8 collective-permute-start.5
  778.1 52.8 %collective-permute-start.6 = (f32[2,1,256,2048]{3,2,1,0:T(8,128)}, f32[2,1,256,2048]{3,2,1,0:T(8,128)S(1)}, u32[]{:S(2)}, u32[]{:S(2)}) collective-permute-start(f32[2,1,256,2048]{3,2,1,0:T(8,128)} %get-tuple-element.7), channel_id=1, source_target_pairs={{0,8},{8,16},{16,24},{24,32},{32,40},{40,48},{48,56},{56,64},{64,7... | collective-permute-start | bytes 12582920 | tf_op jit(solution)/shard_map/ppermute | solution.py:23
  780.9 3.3 collective-permute-start.7
Sparse Core Ops, SparseCore 0:
  245.1 137.2 all-reduce.6
where the time goes:
time: 861 us; the launch traced here: 851 us
  waiting for transfers between devices  378 us (44%)
  matrix products  156 us (18%)
  local copies, waits for them, and re-layouts  98.9 us (11%)
  other arithmetic  83.9 us (10%)
  blocking collectives  67.5 us (8%)
  starting transfers between devices  51 us (6%)
  between operations  15.5 us (2%)
    ppermute x8, waiting for transfers between devices, from_behind(): return lax.ppermute(x, axis, pairs)  170 us
    dot_general x32, matrix products, single(): return jnp.einsum(form, first, second, precision=HIGHEST)  156 us
    psum x1, waiting for transfers between devices, shards(): sum_re, sum_im = lax.psum((local_re, local_im), 'depth')  137 us
    psum x1, blocking collectives, shards(): total = lax.psum(jnp.sum(field * field), ('depth', 'rows'))  67.5 us
    all_to_all x1, waiting for transfers between devices, shards(): lax.all_to_all(row_done[1], 'rows', split_axis=2, concat_axis=1, tiled=True)  25.5 us
    reshape x2, local copies, waits for them, and re-layouts, forward_last(): return (step[0].reshape(lead + (total,)), step[1].reshape(lead + (total,)))  25.1 us
    all_to_all x1, waiting for transfers between devices, shards(): lax.all_to_all(row_done[0], 'rows', split_axis=2, concat_axis=1, tiled=True)  22.5 us
  transfers between devices with their start and end apart: 13, of which 11 were waited for; matrix products, arithmetic and copies ran while one was open for 12% of the time, Pallas kernels for 0%

commit v1 on v0

v1 whole, which is shorter than its diff:
```python
import functools
import math

import jax
import jax.numpy as jnp
import ml_dtypes
import numpy as np
from jax import lax
from jax.experimental import pallas as pl
from jax.experimental.pallas import tpu as pltpu
from jax.sharding import PartitionSpec as P

ALPHA_TWIST = 1.8
BETA_TWIST = 1.2
LAMBDA_TV = 0.2
STEP_TV = 1.0 / 12.0
EPSILON = 1e-06
WAVENUMBER = 4.0 * math.pi

N = 2048
PLANES = 16
ROWS = 256
RADIX = 8
PART = 256
EXT = ROWS + 16
F32 = jnp.float32
BF16 = jnp.bfloat16
MIB = 1024 * 1024


def split_np(table):
    high = table.astype(np.float32).astype(ml_dtypes.bfloat16)
    low = (table - high.astype(np.float64)).astype(np.float32).astype(ml_dtypes.bfloat16)
    return high, low


def dft_blocks(scale):
    index = np.arange(PART)
    angle = 2.0 * np.pi * ((index[:, None] * index[None, :]) % PART) / PART
    cos = np.cos(angle) * scale
    sin = np.sin(angle) * scale
    forward = np.block([[cos, -sin], [sin, cos]])
    inverse = np.block([[cos, sin], [-sin, cos]])
    return forward, inverse


def twiddles():
    index = np.arange(PART)
    angle = 2.0 * np.pi * (np.arange(RADIX)[:, None] * index[None, :]) / N
    return np.stack([np.cos(angle), -np.sin(angle)], axis=1).astype(np.float32)


def dft4(a, b, c, d, sign):
    t0 = (a[0] + c[0], a[1] + c[1])
    t1 = (a[0] - c[0], a[1] - c[1])
    t2 = (b[0] + d[0], b[1] + d[1])
    t3 = (b[0] - d[0], b[1] - d[1])
    if sign > 0:
        turned = (-t3[1], t3[0])
    else:
        turned = (t3[1], -t3[0])
    return (
        (t0[0] + t2[0], t0[1] + t2[1]),
        (t1[0] + turned[0], t1[1] + turned[1]),
        (t0[0] - t2[0], t0[1] - t2[1]),
        (t1[0] - turned[0], t1[1] - turned[1]),
    )


def dft8(v, sign):
    even = dft4(v[0], v[2], v[4], v[6], sign)
    odd = dft4(v[1], v[3], v[5], v[7], sign)
    half = math.sqrt(0.5)
    o1, o2, o3 = odd[1], odd[2], odd[3]
    if sign > 0:
        w1 = ((o1[0] - o1[1]) * half, (o1[0] + o1[1]) * half)
        w2 = (-o2[1], o2[0])
        w3 = ((-o3[0] - o3[1]) * half, (o3[0] - o3[1]) * half)
    else:
        w1 = ((o1[0] + o1[1]) * half, (o1[1] - o1[0]) * half)
        w2 = (o2[1], -o2[0])
        w3 = ((o3[1] - o3[0]) * half, (-o3[0] - o3[1]) * half)
    turned = (odd[0], w1, w2, w3)
    low = [(even[k][0] + turned[k][0], even[k][1] + turned[k][1]) for k in range(4)]
    high = [(even[k][0] - turned[k][0], even[k][1] - turned[k][1]) for k in range(4)]
    return low + high


def split(x):
    high = x.astype(BF16)
    return high, (x - high.astype(F32)).astype(BF16)


def dot(a, b, contract):
    return lax.dot_general(a, b, (contract, ((), ())), preferred_element_type=F32)


def dot3(a_high, a_low, b_high, b_low, contract):
    return (
        dot(a_high, b_high, contract) + dot(a_high, b_low, contract) + dot(a_low, b_high, contract)
    )


NT = ((1,), (1,))
NN = ((1,), (0,))


def forward_radix(load, tw_ref, hi, lo, rows, half):
    lanes = slice(half * 128, half * 128 + 128)
    out = dft8([load(i) for i in range(RADIX)], -1)
    for k in range(RADIX):
        re, im = out[k]
        if k:
            c = tw_ref[k, 0:1, lanes]
            s = tw_ref[k, 1:2, lanes]
            re, im = re * c - im * s, re * s + im * c
        for part, value in ((0, re), (1, im)):
            high, low = split(value)
            at = slice(part * PART + half * 128, part * PART + half * 128 + 128)
            hi[k, rows, at] = high
            lo[k, rows, at] = low


def params(limit_mib):
    return pltpu.CompilerParams(vmem_limit_bytes=limit_mib * MIB)


def whole(shape):
    return pl.BlockSpec(shape, lambda *_: (0,) * len(shape))


def rows_body(x_ref, gh_ref, gl_ref, tw_ref, y_ref, ss_ref, hi, lo):
    k = pl.program_id(0)

    @pl.when(k == 0)
    def _():
        def chunk(t, total):
            rows = pl.ds(pl.multiple_of(t * 16, 16), 16)
            for half in range(2):

                def load(i):
                    at = slice(i * PART + half * 128, i * PART + half * 128 + 128)
                    return (x_ref[0, 0, rows, at], x_ref[1, 0, rows, at])

                patches = [load(i) for i in range(RADIX)]
                for re, im in patches:
                    total = total + (re * re + im * im)
                forward_radix(lambda i: patches[i], tw_ref, hi, lo, rows, half)
            return total

        ss_ref[...] = lax.fori_loop(0, ROWS // 16, chunk, jnp.zeros((16, 128), F32))

    gh, gl = gh_ref, gl_ref
    high, low = hi[k], lo[k]
    for part in range(2):
        at = slice(part * PART, part * PART + PART)
        out = dot3(gh[at, :], gl[at, :], high, low, NT)
        y_ref[0, :, part] = out.reshape(16, 16, ROWS)


def rows_forward(x_now, gt_high, gt_low, tw):
    return pl.pallas_call(
        rows_body,
        grid=(RADIX,),
        in_specs=[
            whole((2, 1, ROWS, N)),
            whole((2 * PART, 2 * PART)),
            whole((2 * PART, 2 * PART)),
            whole((RADIX, 2, PART)),
        ],
        out_specs=[
            pl.BlockSpec((1, 16, 2, 16, ROWS), lambda k: (k, 0, 0, 0, 0)),
            whole((16, 128)),
        ],
        out_shape=[
            jax.ShapeDtypeStruct((RADIX, 16, 2, 16, ROWS), F32),
            jax.ShapeDtypeStruct((16, 128), F32),
        ],
        scratch_shapes=[
            pltpu.VMEM((RADIX, ROWS, 2 * PART), BF16),
            pltpu.VMEM((RADIX, ROWS, 2 * PART), BF16),
        ],
        compiler_params=params(40),
        cost_estimate=pl.CostEstimate(
            flops=4 * 10**9, bytes_accessed=10 * MIB, transcendentals=0
        ),
        name="rows_forward",
    )(x_now, gt_high, gt_low, tw)


def holo_body(x_ref, gh_ref, gl_ref, tw_ref, y_ref, hi, lo):
    def chunk(t, carry):
        rows = pl.ds(pl.multiple_of(t * 16, 16), 16)
        for half in range(2):

            def load(i):
                at = slice(i * PART + half * 128, i * PART + half * 128 + 128)
                return (x_ref[0, rows, at], x_ref[1, rows, at])

            forward_radix(load, tw_ref, hi, lo, rows, half)
        return carry

    lax.fori_loop(0, ROWS // 16, chunk, 0)

    def per_k(k, carry):
        out = dot3(gh_ref[...], gl_ref[...], hi[k], lo[k], NT)
        y_ref[k] = out.reshape(2, 16, ROWS)
        return carry

    lax.fori_loop(0, RADIX, per_k, 0)


def holo_forward(hologram, gt_high, gt_low, tw):
    return pl.pallas_call(
        holo_body,
        out_shape=jax.ShapeDtypeStruct((RADIX, 2, 16, ROWS), F32),
        scratch_shapes=[
            pltpu.VMEM((RADIX, ROWS, 2 * PART), BF16),
            pltpu.VMEM((RADIX, ROWS, 2 * PART), BF16),
        ],
        in_specs=[pl.BlockSpec(memory_space=pltpu.VMEM)] * 4,
        out_specs=pl.BlockSpec(memory_space=pltpu.VMEM),
        compiler_params=params(40),
        cost_estimate=pl.CostEstimate(
            flops=4 * 10**8, bytes_accessed=5 * MIB, transcendentals=0
        ),
        name="holo_forward",
    )(hologram, gt_high, gt_low, tw)


def cos_sin(phase):
    turns = jnp.floor(phase * (2.0 / math.pi) + 0.5)
    rest = phase - turns * 1.5703125
    rest = rest - turns * 4.837512969970703e-4
    rest = rest - turns * 7.549789948768648e-8
    z = rest * rest
    sin = rest + rest * z * (
        -1.6666654611e-1 + z * (8.3321608736e-3 + z * -1.9515295891e-4)
    )
    cos = (
        1.0
        - 0.5 * z
        + z
        * z
        * (4.166664568298827e-2 + z * (-1.388731625493765e-3 + z * 2.443315711809948e-5))
    )
    quarter = turns.astype(jnp.int32) & 3
    odd = (quarter & 1) == 1
    base_cos = jnp.where(odd, sin, cos)
    base_sin = jnp.where(odd, cos, sin)
    out_cos = jnp.where((quarter == 1) | (quarter == 2), -base_cos, base_cos)
    out_sin = jnp.where(quarter >= 2, -base_sin, base_sin)
    return out_cos, out_sin


def transfer_body(depth_ref, rate_ref, t_ref):
    rate = rate_ref[0]
    for p in range(PLANES):
        cos, sin = cos_sin(depth_ref[0, p] * rate)
        rows = slice(p * 16, p * 16 + 16)
        t_ref[0, 0, rows, :] = cos
        t_ref[0, 1, rows, :] = sin


def transfer(depth_all, rate):
    return pl.pallas_call(
        transfer_body,
        grid=(RADIX,),
        in_specs=[
            pl.BlockSpec(memory_space=pltpu.SMEM),
            pl.BlockSpec((1, 16, PART), lambda k: (k, 0, 0)),
        ],
        out_specs=pl.BlockSpec((1, 2, PLANES * 16, PART), lambda k: (k, 0, 0, 0)),
        out_shape=jax.ShapeDtypeStruct((RADIX, 2, PLANES * 16, PART), F32),
        compiler_params=params(16),
        cost_estimate=pl.CostEstimate(
            flops=10**7, bytes_accessed=4 * MIB, transcendentals=0
        ),
        name="transfer",
    )(depth_all, rate)


COLS = PLANES * 16
WITH_HOLO = COLS + 16


def spectral_body(
    z_ref, h_ref, t_ref, gh_ref, gl_ref, ih_ref, il_ref, tw_ref, o_ref, norm_ref,
    hi, lo, spec, bhi, blo, back,
):
    k = pl.program_id(0)

    @pl.when(k == 0)
    def _():
        norm_ref[...] = jnp.zeros_like(norm_ref)

        def chunk(p, carry):
            rows = pl.ds(pl.multiple_of(p * 16, 16), 16)
            for half in range(2):
                at = slice(half * 128, half * 128 + 128)

                def load(i):
                    return (z_ref[i, p, 0, :, at], z_ref[i, p, 1, :, at])

                forward_radix(load, tw_ref, hi, lo, rows, half)
            return carry

        lax.fori_loop(0, PLANES, chunk, 0)
        for half in range(2):
            at = slice(half * 128, half * 128 + 128)

            def load_holo(i):
                return (h_ref[i, 0, :, at], h_ref[i, 1, :, at])

            forward_radix(load_holo, tw_ref, hi, lo, slice(COLS, WITH_HOLO), half)

    spec[...] = dot3(hi[k], lo[k], gh_ref[...], gl_ref[...], NN)

    for half in range(2):
        at = slice(half * 128, half * 128 + 128)
        at_im = slice(PART + half * 128, PART + half * 128 + 128)

        def gather(p, total):
            rows = pl.ds(pl.multiple_of(p * 16, 16), 16)
            xr, xi = spec[rows, at], spec[rows, at_im]
            tr, ti = t_ref[0, 0, rows, at], t_ref[0, 1, rows, at]
            return (total[0] + (tr * xr - ti * xi), total[1] + (tr * xi + ti * xr))

        zero = jnp.zeros((16, 128), F32)
        pred = lax.fori_loop(0, PLANES, gather, (zero, zero), unroll=4)
        holo = (spec[COLS:WITH_HOLO, at], spec[COLS:WITH_HOLO, at_im])
        res = (holo[0] - pred[0], holo[1] - pred[1])
        norm_ref[...] += res[0] * (holo[0] + pred[0]) + res[1] * (holo[1] + pred[1])

        def scatter(p, carry):
            rows = pl.ds(pl.multiple_of(p * 16, 16), 16)
            tr, ti = t_ref[0, 0, rows, at], t_ref[0, 1, rows, at]
            br = tr * res[0] + ti * res[1]
            bi = tr * res[1] - ti * res[0]
            for where, value in ((at, br), (at_im, bi)):
                high, low = split(value)
                bhi[rows, where] = high
                blo[rows, where] = low
            return carry

        lax.fori_loop(0, PLANES, scatter, 0, unroll=4)

    c = tw_ref[k, 0:1, :]
    s = tw_ref[k, 1:2, :]
    out = dot3(bhi[...], blo[...], ih_ref[...], il_ref[...], NN)
    re, im = out[:, :PART], out[:, PART:]
    back[k, 0] = re * c + im * s
    back[k, 1] = im * c - re * s

    @pl.when(k == RADIX - 1)
    def _():
        def chunk(p, carry):
            rows = pl.ds(pl.multiple_of(p * 16, 16), 16)
            for half in range(2):
                at = slice(half * 128, half * 128 + 128)
                out = dft8([(back[i, 0, rows, at], back[i, 1, rows, at]) for i in range(RADIX)], 1)
                for i in range(RADIX):
                    o_ref[i, p, 0, :, at] = out[i][0]
                    o_ref[i, p, 1, :, at] = out[i][1]
            return carry

        lax.fori_loop(0, PLANES, chunk, 0)


def spectral(z, holo, trans, g_high, g_low, i_high, i_low, tw):
    table = whole((2 * PART, 2 * PART))
    return pl.pallas_call(
        spectral_body,
        grid=(RADIX,),
        in_specs=[
            whole((RADIX, PLANES, 2, 16, PART)),
            whole((RADIX, 2, 16, PART)),
            pl.BlockSpec((1, 2, COLS, PART), lambda k: (k, 0, 0, 0)),
            table,
            table,
            table,
            table,
            whole((RADIX, 2, PART)),
        ],
        out_specs=[whole((RADIX, PLANES, 2, 16, PART)), whole((16, 128))],
        out_shape=[
            jax.ShapeDtypeStruct((RADIX, PLANES, 2, 16, PART), F32),
            jax.ShapeDtypeStruct((16, 128), F32),
        ],
        scratch_shapes=[
            pltpu.VMEM((RADIX, WITH_HOLO, 2 * PART), BF16),
            pltpu.VMEM((RADIX, WITH_HOLO, 2 * PART), BF16),
            pltpu.VMEM((WITH_HOLO, 2 * PART), F32),
            pltpu.VMEM((COLS, 2 * PART), BF16),
            pltpu.VMEM((COLS, 2 * PART), BF16),
            pltpu.VMEM((RADIX, 2, COLS, PART), F32),
        ],
        compiler_params=params(56),
        cost_estimate=pl.CostEstimate(
            flops=8 * 10**9, bytes_accessed=14 * MIB, transcendentals=0
        ),
        name="spectral",
    )(z, holo, trans, g_high, g_low, i_high, i_low, tw)


def rows_back_body(
    w_ref, x_ref, ih_ref, il_ref, tw_ref, re_ref, im_ref, top_ref, bot_ref, back
):
    k = pl.program_id(0)
    parts = [w_ref[0, :, c].reshape(PART, ROWS).T for c in range(2)]
    high, low = split(jnp.concatenate(parts, axis=1))
    out = dot3(high, low, ih_ref[...], il_ref[...], NN)
    c = tw_ref[k, 0:1, :]
    s = tw_ref[k, 1:2, :]
    re, im = out[:, :PART], out[:, PART:]
    back[k, 0] = re * c + im * s
    back[k, 1] = im * c - re * s

    @pl.when(k == RADIX - 1)
    def _():
        def chunk(t, carry):
            rows = pl.ds(pl.multiple_of(t * 16, 16), 16)
            for half in range(2):
                at = slice(half * 128, half * 128 + 128)
                out = dft8([(back[i, 0, rows, at], back[i, 1, rows, at]) for i in range(RADIX)], 1)
                for i in range(RADIX):
                    to = slice(i * PART + half * 128, i * PART + half * 128 + 128)
                    re_ref[rows, to] = x_ref[0, 0, rows, to] + out[i][0]
                    im_ref[rows, to] = x_ref[1, 0, rows, to] + out[i][1]
            return carry

        lax.fori_loop(0, ROWS // 16, chunk, 0)
        top_ref[0] = re_ref[0:8, :]
        top_ref[1] = im_ref[0:8, :]
        bot_ref[0] = re_ref[ROWS - 8 : ROWS, :]
        bot_ref[1] = im_ref[ROWS - 8 : ROWS, :]


def rows_back(w, x_now, i_high, i_low, tw):
    table = whole((2 * PART, 2 * PART))
    return pl.pallas_call(
        rows_back_body,
        grid=(RADIX,),
        in_specs=[
            pl.BlockSpec((1, 16, 2, 16, ROWS), lambda k: (k, 0, 0, 0, 0)),
            whole((2, 1, ROWS, N)),
            table,
            table,
            whole((RADIX, 2, PART)),
        ],
        out_specs=[whole((ROWS, N)), whole((ROWS, N)), whole((2, 8, N)), whole((2, 8, N))],
        out_shape=[
            jax.ShapeDtypeStruct((ROWS, N), F32),
            jax.ShapeDtypeStruct((ROWS, N), F32),
            jax.ShapeDtypeStruct((2, 8, N), F32),
            jax.ShapeDtypeStruct((2, 8, N), F32),
        ],
        scratch_shapes=[pltpu.VMEM((RADIX, 2, ROWS, PART), F32)],
        compiler_params=params(48),
        cost_estimate=pl.CostEstimate(
            flops=4 * 10**9, bytes_accessed=13 * MIB, transcendentals=0
        ),
        name="rows_back",
    )(w, x_now, i_high, i_low, tw)


TILES = EXT // 8


def below(x, after):
    row = lax.broadcasted_iota(jnp.int32, x.shape, 0)
    return pltpu.roll(jnp.where(row == 0, after, x), 7, 0)


def above(x, before):
    row = lax.broadcasted_iota(jnp.int32, x.shape, 0)
    return pltpu.roll(jnp.where(row == 7, before, x), 1, 0)


def right_of(x):
    return pltpu.roll(x, N - 1, 1)


def left_of(x):
    return pltpu.roll(x, 1, 1)


def weight(gz, gy, gx):
    return 1.0 / (1.0 + jnp.sqrt(gz * gz + gy * gy + gx * gx))


def masks(t, row_base):
    row = lax.broadcasted_iota(jnp.int32, (8, N), 0) + (row_base + t * 8 - 8)
    col = lax.broadcasted_iota(jnp.int32, (8, N), 1)
    return (row >= 0) & (row < N - 1), col < N - 1


def tv_first_body(
    comp, num_ref, at_ref, own, nxt, prv, own_h, nxt_h, prv_h, inner_ref, dual_ref, ext, sems
):
    copies = []
    for which, (main, halo) in enumerate(((own, own_h), (nxt, nxt_h), (prv, prv_h))):
        copies += [
            pltpu.make_async_copy(
                main, ext.at[which, pl.ds(8, ROWS), :], sems.at[which, 0]
            ),
            pltpu.make_async_copy(
                halo.at[0, comp], ext.at[which, pl.ds(0, 8), :], sems.at[which, 1]
            ),
            pltpu.make_async_copy(
                halo.at[1, comp], ext.at[which, pl.ds(ROWS + 8, 8), :], sems.at[which, 2]
            ),
        ]
    for copy in copies:
        copy.start()
    for copy in copies:
        copy.wait()
    scale = num_ref[0]
    inverse = num_ref[1]
    keep_next = num_ref[2]
    keep_prev = num_ref[3]
    row_base = at_ref[0]

    def tile(t, before):
        rows = pl.ds(pl.multiple_of(t * 8, 8), 8)
        later = pl.ds(pl.multiple_of(jnp.minimum(t + 1, TILES - 1) * 8, 8), 8)
        row_ok, col_ok = masks(t, row_base)
        u = ext[0, rows, :]
        q = ext[2, rows, :]
        gz = (ext[1, rows, :] - u) * (scale * keep_next)
        gy = jnp.where(row_ok, (below(u, ext[0, later, :]) - u) * scale, 0.0)
        gx = jnp.where(col_ok, (right_of(u) - u) * scale, 0.0)
        w = weight(gz, gy, gx)
        dz, dy, dx = gz * w, gy * w, gx * w
        gz = (u - q) * (scale * keep_prev)
        gy = jnp.where(row_ok, (below(q, ext[2, later, :]) - q) * scale, 0.0)
        gx = jnp.where(col_ok, (right_of(q) - q) * scale, 0.0)
        dq = gz * weight(gz, gy, gx)
        div = (dz - dq) + (dy - above(dy, before)) + (dx - left_of(dx))
        inner_ref[rows, :] = (div + u * inverse) * STEP_TV
        dual_ref[0, rows, :] = dz
        dual_ref[1, rows, :] = dy
        dual_ref[2, rows, :] = dx
        dual_ref[3, rows, :] = dq
        return dy

    lax.fori_loop(0, TILES, tile, jnp.zeros((8, N), F32))


def tv_first(comp, numbers, place, own, nxt, prv, own_h, nxt_h, prv_h):
    smem = pl.BlockSpec(memory_space=pltpu.SMEM)
    anywhere = pl.BlockSpec(memory_space=pl.ANY)
    vmem = pl.BlockSpec(memory_space=pltpu.VMEM)
    return pl.pallas_call(
        functools.partial(tv_first_body, comp),
        in_specs=[smem, smem] + [anywhere] * 6,
        out_specs=[vmem, vmem],
        out_shape=[
            jax.ShapeDtypeStruct((EXT, N), F32),
            jax.ShapeDtypeStruct((4, EXT, N), F32),
        ],
        scratch_shapes=[
            pltpu.VMEM((3, EXT, N), F32),
            pltpu.SemaphoreType.DMA((3, 3)),
        ],
        compiler_params=params(40),
        cost_estimate=pl.CostEstimate(
            flops=10**8, bytes_accessed=17 * MIB, transcendentals=2 * 10**6
        ),
        name="tv_first",
    )(numbers, place, own, nxt, prv, own_h, nxt_h, prv_h)


def tv_second_body(
    comp, num_ref, at_ref, own, nxt, prv, dual, parts, x_prev, x_now, *rest
):
    out_ref = rest[-1]
    strength = num_ref[4]
    keep_next = num_ref[2]
    keep_prev = num_ref[3]
    row_base = at_ref[0]

    def duals(t):
        rows = pl.ds(pl.multiple_of(t * 8, 8), 8)
        later = pl.ds(pl.multiple_of(t * 8 + 8, 8), 8)
        row_ok, col_ok = masks(t, row_base)
        u = own[rows, :]
        gz = (nxt[rows, :] - u) * keep_next
        gy = jnp.where(row_ok, below(u, own[later, :]) - u, 0.0)
        gx = jnp.where(col_ok, right_of(u) - u, 0.0)
        w = weight(gz, gy, gx)
        return rows, later, row_ok, col_ok, u, gz, gy, gx, w

    _, _, _, _, _, _, gy0, _, w0 = duals(0)
    first = (dual[1, 0:8, :] + gy0) * w0

    def tile(t, before):
        rows, later, row_ok, col_ok, u, gz, gy, gx, w = duals(t)
        dz = (dual[0, rows, :] + gz) * w
        dy = (dual[1, rows, :] + gy) * w
        dx = (dual[2, rows, :] + gx) * w
        q = prv[rows, :]
        gz = (u - q) * keep_prev
        gy = jnp.where(row_ok, below(q, prv[later, :]) - q, 0.0)
        gx = jnp.where(col_ok, right_of(q) - q, 0.0)
        dq = (dual[3, rows, :] + gz) * weight(gz, gy, gx)
        div = (dz - dq) + (dy - above(dy, before)) + (dx - left_of(dx))
        main = pl.ds(pl.multiple_of(t * 8 - 8, 8), 8)
        denoised = parts[main, :] - strength * div
        out_ref[0, 0, main, :] = (
            (1.0 - ALPHA_TWIST) * x_prev[0, 0, main, :]
            + (ALPHA_TWIST - BETA_TWIST) * x_now[0, 0, main, :]
            + BETA_TWIST * denoised
        )
        return dy

    lax.fori_loop(1, TILES - 1, tile, first)


def tv_second(comp, numbers, place, own, nxt, prv, dual, parts, x_prev, x_now, into):
    smem = pl.BlockSpec(memory_space=pltpu.SMEM)
    anywhere = pl.BlockSpec(memory_space=pl.ANY)
    block = pl.BlockSpec((1, 1, ROWS, N), lambda i: (comp, 0, 0, 0))
    args = [numbers, place, own, nxt, prv, dual, parts, x_prev, x_now]
    specs = [
        smem,
        smem,
        whole((EXT, N)),
        whole((EXT, N)),
        whole((EXT, N)),
        whole((4, EXT, N)),
        whole((ROWS, N)),
        block,
        block,
    ]
    aliases = {}
    if into is not None:
        args.append(into)
        specs.append(anywhere)
        aliases = {len(args) - 1: 0}
    return pl.pallas_call(
        functools.partial(tv_second_body, comp),
        grid=(1,),
        in_specs=specs,
        out_specs=block,
        out_shape=jax.ShapeDtypeStruct((2, 1, ROWS, N), F32),
        input_output_aliases=aliases,
        compiler_params=params(60),
        cost_estimate=pl.CostEstimate(
            flops=10**8, bytes_accessed=23 * MIB, transcendentals=2 * 10**6
        ),
        name="tv_second",
    )(*args)


def from_behind(x, axis, by):
    count = lax.axis_size(axis)
    pairs = [(i, i + by) for i in range(count) if 0 <= i + by < count]
    return lax.ppermute(x, axis, pairs)


def swap_sum(x, axis, bits):
    count = lax.axis_size(axis)
    for bit in bits:
        x = x + lax.ppermute(x, axis, [(i, i ^ bit) for i in range(count)])
    return x


def signed_freq(freq):
    signed = jnp.where(freq < N // 2, freq, freq - N)
    return signed.astype(F32) * (2.0 * math.pi / N)


def phase_rate(qx_grid, qy_grid):
    square = qx_grid * qx_grid + qy_grid * qy_grid
    return -square / (WAVENUMBER + jnp.sqrt(WAVENUMBER * WAVENUMBER - square))


def shards(x_now, x_prev, hologram, depths):
    d = lax.axis_index("depth")
    r = lax.axis_index("rows")
    forward, inverse = dft_blocks(1.0 / math.sqrt(N))
    g_high, g_low = split_np(forward)
    i_high, i_low = split_np(inverse)
    p_high, p_low = split_np(inverse / PLANES)
    t_high, t_low = split_np(forward.T)
    pick = np.stack([t_high, t_low]).reshape(2, 2, 16, 16, 2 * PART)
    pick = np.ascontiguousarray(pick.transpose(2, 0, 1, 3, 4)).reshape(16, 2, 32, 2 * PART)
    tw = jnp.asarray(twiddles())

    chosen = lax.dynamic_index_in_dim(jnp.asarray(pick), d, 0, keepdims=False)
    holo = holo_forward(hologram, chosen[0], chosen[1], tw)
    holo = lax.all_to_all(holo, "rows", 0, 0, tiled=True)

    lane = lax.broadcasted_iota(jnp.int32, (1, 128), 1)
    depth_all = swap_sum(jnp.where(lane == d, depths[0], 0.0), "depth", (1, 2, 4, 8))
    kx = r + RADIX * (16 * d + jnp.arange(16, dtype=jnp.int32))
    ky = (
        jnp.arange(RADIX, dtype=jnp.int32)[:, None]
        + RADIX * jnp.arange(PART, dtype=jnp.int32)[None, :]
    )
    rate = phase_rate(signed_freq(kx)[None, :, None], signed_freq(ky)[:, None, :])
    trans = transfer(depth_all, rate)

    sent, squares = rows_forward(x_now, jnp.asarray(t_high), jnp.asarray(t_low), tw)
    both = ("rows", "depth")
    got = lax.all_to_all(sent.reshape(128, 2, 16, ROWS), both, 0, 0, tiled=True)
    back, cross = spectral(
        got.reshape(RADIX, PLANES, 2, 16, ROWS),
        holo,
        trans,
        jnp.asarray(g_high),
        jnp.asarray(g_low),
        jnp.asarray(i_high),
        jnp.asarray(i_low),
        tw,
    )
    ret = lax.all_to_all(back.reshape(128, 2, 16, ROWS), both, 0, 0, tiled=True)

    total = jnp.sum(squares) + jnp.sum(cross) / PLANES
    total = jnp.full((1, 128), total)
    total = swap_sum(swap_sum(total, "rows", (1, 2, 4)), "depth", (1, 2, 4, 8))[0, 0]
    mean_square = jnp.maximum(total, 0.0) / (2.0 * PLANES * N * N)
    strength = LAMBDA_TV * jnp.sqrt(mean_square + EPSILON)
    numbers = jnp.stack(
        [
            -STEP_TV / strength,
            -1.0 / strength,
            (d < PLANES - 1).astype(F32),
            (d > 0).astype(F32),
            strength,
        ]
    )
    place = jnp.stack([r * ROWS])

    re, im, top, bot = rows_back(
        ret.reshape(RADIX, PLANES, 2, 16, ROWS), x_now, jnp.asarray(p_high), jnp.asarray(p_low), tw
    )
    own = (re, im)
    halo = jnp.stack([from_behind(bot, "rows", 1), from_behind(top, "rows", -1)])
    nxt = [from_behind(own[0], "depth", -1)]
    prv = [from_behind(own[0], "depth", 1)]
    halo_next = from_behind(halo, "depth", -1)
    halo_prev = from_behind(halo, "depth", 1)
    nxt.append(from_behind(own[1], "depth", -1))
    prv.append(from_behind(own[1], "depth", 1))

    out = None
    firsts = [
        tv_first(c, numbers, place, own[c], nxt[c], prv[c], halo, halo_next, halo_prev)
        for c in range(2)
    ]
    for c in range(2):
        inner, dual = firsts[c]
        out = tv_second(
            c,
            numbers,
            place,
            inner,
            from_behind(inner, "depth", -1),
            from_behind(inner, "depth", 1),
            dual,
            own[c],
            x_prev,
            x_now,
            out,
        )
    return out


def solution(mesh):
    return jax.shard_map(
        shards,
        mesh=mesh,
        in_specs=(
            P(None, "depth", "rows", None),
            P(None, "depth", "rows", None),
            P(None, "rows", None),
            P("depth"),
        ),
        out_specs=P(None, "depth", "rows", None),
        check_vma=False,
    )
```

time: 861 us -> 369 us (0.43)
  waiting for transfers between devices: 378 us -> 121 us
  matrix products: 156 us -> 0 us
  Pallas kernels: 0 us -> 104 us
  local copies, waits for them, and re-layouts: 98.9 us -> 12.1 us
  other arithmetic: 83.9 us -> 1.47 us
  between operations: 15.5 us -> 2.43 us
  starting transfers between devices: 51 us -> 63.4 us
    dot_general x32 -> x0, matrix products: 156 us -> none  [single(): return jnp.einsum(form, first, second, precision=HIGHEST)]
    psum x1 -> x0, waiting for transfers between devices: 137 us -> none  [shards(): sum_re, sum_im = lax.psum((local_re, local_im), 'depth')]
    ppermute x8 -> x12, waiting for transfers between devices: 170 us -> 35.1 us  [from_behind(): return lax.ppermute(x, axis, pairs)]
    pallas_call x0 -> x9, Pallas kernels: none -> 104 us  [the longest x2 30.1 us: tv_second(): pl.pallas_call(functools.partial(tv_second_body, comp), grid=(1,), in_spe...]
    ppermute x0 -> x11, waiting for transfers between devices: none -> 86 us  [swap_sum(): x = x + lax.ppermute(x, axis, [(i, i ^ bit) for i in range(count)])]
    all_to_all x4 -> x2, waiting for transfers between devices: 71.1 us -> 0.01 us  [the longest x1 0.01 us: shards(): holo = lax.all_to_all(holo, 'rows', 0, 0, tiled=True)]
    psum x1 -> x0, blocking collectives: 67.5 us -> none  [shards(): total = lax.psum(jnp.sum(field * field), ('depth', 'rows'))]
    all_to_all x0 -> x1, blocking collectives: none -> 60.1 us  [shards(): ret = lax.all_to_all(back.reshape(128, 2, 16, ROWS), both, 0, 0, tiled=True)]
  transfers between devices with their start and end apart: 13 -> 25, of which waited for: 11 -> 19; matrix products, arithmetic and copies ran while one was open for 12% -> 0% of each run, Pallas kernels for 0% -> 15%
where the time goes in v1:
time: 369 us; the launch traced here: 364 us
  waiting for transfers between devices  121 us (33%)
  Pallas kernels  104 us (28%)
  starting transfers between devices  63.4 us (17%)
  blocking collectives  60.1 us (16%)
  local copies, waits for them, and re-layouts  12.1 us (3%)
    ppermute x11, waiting for transfers between devices, swap_sum(): x = x + lax.ppermute(x, axis, [(i, i ^ bit) for i in range(count)])  86 us
    all_to_all x1, blocking collectives, shards(): ret = lax.all_to_all(back.reshape(128, 2, 16, ROWS), both, 0, 0, tiled=True)  60.1 us
    ppermute x12, waiting for transfers between devices, from_behind(): return lax.ppermute(x, axis, pairs)  35.1 us
    ppermute x12, starting transfers between devices, from_behind(): return lax.ppermute(x, axis, pairs)  34.2 us
    pallas_call x2, Pallas kernels, tv_second(): pl.pallas_call(functools.partial(tv_second_body, comp), grid=(1,), in_spe...  30.1 us
    pallas_call x2, Pallas kernels, tv_first(): pl.pallas_call(functools.partial(tv_first_body, comp), in_specs=[smem, sm...  28 us
    pallas_call x1, Pallas kernels, spectral(): pl.pallas_call(spectral_body, grid=(RADIX,), in_specs=[whole((RADIX, PLAN...  19.4 us
    ppermute x11, starting transfers between devices, swap_sum(): x = x + lax.ppermute(x, axis, [(i, i ^ bit) for i in range(count)])  11.3 us
  transfers between devices with their start and end apart: 25, of which 19 were waited for; matrix products, arithmetic and copies ran while one was open for 0% of the time, Pallas kernels for 15%

profile of v1, /device:TPU:32, one launch (start us, length us, event | category | flops | bytes accessed | tf_op | source)
XLA Modules:
  0.0 364.4 jit_solution(10230270931407695526)
XLA Ops:
  0.0 0.8 dynamic-slice_bitcast_fusion
  0.8 2.2 copy-done.2
  3.0 0.7 copy-done.6
  3.7 5.1 %holo_forward.1 = f32[8,2,16,256]{3,2,1,0:T(8,128)} custom-call(f32[2,256,2048]{2,1,0:T(8,128)S(1)} %copy-done.2, bf16[32,512]{1,0:T(8,128)(2,1)S(1)} %get-tuple-element.30.gh_ref, bf16[32,512]{1,0:T(8,128)(2,1)S(1)} %get-tuple-element.29.gl_ref, f32[8,2,256]{2,1,0:T(2,128)S(1)} %copy-done.6), custom_call_target="tpu_custom_call" | custom-call | flops 400000000 | bytes 5242880 | tf_op jit(solution)/shard_map/holo_forward/pallas_call | solution.py:214
  8.8 6.9 %all-to-all-start.1 = ((f32[8,2,16,256]{3,2,1,0:T(8,128)}), f32[8,2,16,256]{3,2,1,0:T(8,128)S(1)}, u32[]{:S(2)}, u32[]{:S(2)}) async-start(f32[8,2,16,256]{3,2,1,0:T(8,128)} %holo_forward.1), calls=%async_computation.1 | async-start | bytes 524288 | tf_op jit(solution)/shard_map/all_to_all | solution.py:693
  15.7 2.2 copy-done
  17.9 6.8 %rows_forward.1 = (f32[8,16,2,16,256]{4,3,2,1,0:T(8,128)S(1)}, f32[16,128]{1,0:T(8,128)S(1)}) custom-call(f32[2,1,256,2048]{3,2,1,0:T(8,128)S(1)} %copy-done, bf16[512,512]{1,0:T(8,128)(2,1)S(1)} %copy-done.12, bf16[512,512]{1,0:T(8,128)(2,1)S(1)} %copy-done.13, f32[8,2,256]{2,1,0:T(2,128)S(1)} %copy-done.7), custom_call_target="tpu_custom_call" | custom-call | flops 4000000000 | bytes 10485760 | tf_op jit(solution)/shard_map/rows_forward/pallas_call | solution.py:162
  24.7 2.0 copy-done.3
  26.7 0.7 copy-done.17
  27.5 11.0 %all-to-all-start = ((f32[128,2,16,256]{3,2,1,0:T(8,128)}), f32[128,2,16,256]{3,2,1,0:T(8,128)}, u32[]{:S(2)}, u32[]{:S(2)}) async-start(f32[128,2,16,256]{3,2,1,0:T(8,128)} %bitcast.21), calls=%async_computation | async-start | bytes 8388608 | tf_op jit(solution)/shard_map/all_to_all | solution.py:707
  39.1 0.2 collective-permute-start
  39.4 1.0 collective-permute-done
  40.3 1.5 collective-permute-start.1
  41.8 43.0 %collective-permute-done.1 = f32[1,128]{1,0:T(1,128)S(1)} collective-permute-done((f32[1,128]{1,0:T(1,128)S(1)}, f32[1,128]{1,0:T(1,128)S(1)}, u32[]{:S(2)}, u32[]{:S(2)}) %collective-permute-start.1) | collective-permute-done | bytes 544 | tf_op jit(solution)/shard_map/ppermute | solution.py:665
  84.8 2.7 collective-permute-start.2
  87.6 2.3 collective-permute-done.2
  89.9 0.5 collective-permute-start.3
  90.4 0.1 fusion.rate_ref
  90.5 2.9 collective-permute-done.3
  93.4 3.5 transfer.1.t_ref
  96.9 2.0 copy-done.4
  99.0 19.4 %spectral.1 = (f32[8,16,2,16,256]{4,3,2,1,0:T(8,128)}, f32[16,128]{1,0:T(8,128)}) custom-call(f32[8,16,2,16,256]{4,3,2,1,0:T(8,128)} %bitcast.1.z_ref, f32[8,2,16,256]{3,2,1,0:T(8,128)} %copy-done.17, f32[8,2,256,256]{3,2,1,0:T(8,128)} %copy-done.4, bf16[512,512]{1,0:T(8,128)(2,1)} %constant.79.clone.gh_ref, bf16[512,512]{1,0:T(8,128)(2,1)} %constant.80.clone.gl_ref, ...), custom_call_target="tpu_custom_call" | custom-call | flops 8000000000 | bytes 14680064 | tf_op jit(solution)/shard_map/spectral/pallas_call | solution.py:372
  118.4 60.1 %all_to_all.15 = f32[128,2,16,256]{3,2,1,0:T(8,128)} all-to-all(f32[128,2,16,256]{3,2,1,0:T(8,128)} %bitcast.22), channel_id=1, replica_groups=mesh['depth'=16,'rows'=8] {'rows','depth'}, dimensions={0} | all-to-all | bytes 8388608 | tf_op jit(solution)/shard_map/all_to_all | solution.py:718
  178.6 10.9 %rows_back.1 = (f32[256,2048]{1,0:T(8,128)}, f32[256,2048]{1,0:T(8,128)S(1)}, f32[2,8,2048]{2,1,0:T(8,128)S(1)}, f32[2,8,2048]{2,1,0:T(8,128)S(1)}) custom-call(f32[8,16,2,16,256]{4,3,2,1,0:T(8,128)} %bitcast.23, f32[2,1,256,2048]{3,2,1,0:T(8,128)} %x_now.3, bf16[512,512]{1,0:T(8,128)(2,1)S(1)} %copy-done.10, bf16[512,512]{1,0:T(8,128)(2,1)S(1)} %copy-done.11, ...), custom_call_target="tpu_custom_call" | custom-call | flops 4000000000 | bytes 13631488 | tf_op jit(solution)/shard_map/rows_back/pallas_call | solution.py:441
  189.5 4.7 %collective-permute-start.19 = (f32[256,2048]{1,0:T(8,128)}, f32[256,2048]{1,0:T(8,128)}, u32[]{:S(2)}, u32[]{:S(2)}) collective-permute-start(f32[256,2048]{1,0:T(8,128)} %get-tuple-element.26.own.parts), channel_id=1, source_target_pairs={{8,0},{16,8},{24,16},{32,24},{40,32},{48,40},{56,48},{64,56},{72,6... | collective-permute-start | bytes 6291464 | tf_op jit(solution)/shard_map/ppermute | solution.py:659
  194.2 1.9 collective-permute-start.20
  196.2 5.8 %collective-permute-start.11 = (f32[256,2048]{1,0:T(8,128)S(1)}, f32[256,2048]{1,0:T(8,128)}, u32[]{:S(2)}, u32[]{:S(2)}) collective-permute-start(f32[256,2048]{1,0:T(8,128)S(1)} %get-tuple-element.21.own.parts), channel_id=1, source_target_pairs={{8,0},{16,8},{24,16},{32,24},{40,32},{48,40},{56,48},{64,56},{72,6... | collective-permute-start | bytes 6291464 | tf_op jit(solution)/shard_map/ppermute | solution.py:659
  201.9 1.9 collective-permute-start.12
  203.9 0.6 reduce_sum.18
  204.5 0.7 reduce_sum.19
  206.4 0.8 collective-permute-start.4
  207.2 2.8 collective-permute-done.4
  210.0 3.5 collective-permute-start.5
  213.6 1.5 collective-permute-done.5
  215.1 1.0 collective-permute-start.6
  216.1 4.1 %collective-permute-done.6 = f32[1,128]{1,0:T(1,128)S(1)} collective-permute-done((f32[1,128]{1,0:T(1,128)S(1)}, f32[1,128]{1,0:T(1,128)S(1)}, u32[]{:S(2)}, u32[]{:S(2)}) %collective-permute-start.6) | collective-permute-done | bytes 544 | tf_op jit(solution)/shard_map/ppermute | solution.py:665
  220.1 1.1 collective-permute-done.7
  221.3 19.8 %collective-permute-done.8 = f32[1,128]{1,0:T(1,128)S(1)} collective-permute-done((f32[1,128]{1,0:T(1,128)S(1)}, f32[1,128]{1,0:T(1,128)S(1)}, u32[]{:S(2)}, u32[]{:S(2)}) %collective-permute-start.8) | collective-permute-done | bytes 544 | tf_op jit(solution)/shard_map/ppermute | solution.py:665
  241.1 0.5 collective-permute-start.9
  241.6 4.6 %collective-permute-done.9 = f32[1,128]{1,0:T(1,128)S(1)} collective-permute-done((f32[1,128]{1,0:T(1,128)S(1)}, f32[1,128]{1,0:T(1,128)S(1)}, u32[]{:S(2)}, u32[]{:S(2)}) %collective-permute-start.9) | collective-permute-done | bytes 544 | tf_op jit(solution)/shard_map/ppermute | solution.py:665
  246.1 3.2 collective-permute-start.13
  249.3 2.8 collective-permute-done.13
  252.2 1.3 collective-permute-start.14
  253.5 6.0 %collective-permute-done.14 = f32[2,8,2048]{2,1,0:T(8,128)S(1)} collective-permute-done((f32[2,8,2048]{2,1,0:T(8,128)S(1)}, f32[2,8,2048]{2,1,0:T(8,128)S(1)}, u32[]{:S(2)}, u32[]{:S(2)}) %collective-permute-start.14) | collective-permute-done | bytes 131104 | tf_op jit(solution)/shard_map/ppermute | solution.py:659
  259.5 0.6 collective-permute-start.10
  260.1 2.9 collective-permute-done.10
  263.0 1.9 collective-permute-start.15
  264.9 3.9 %collective-permute-done.15.nxt_h = f32[2,2,8,2048]{3,2,1,0:T(8,128)S(1)} collective-permute-done((f32[2,2,8,2048]{3,2,1,0:T(8,128)S(1)}, f32[2,2,8,2048]{3,2,1,0:T(8,128)S(1)}, u32[]{:S(2)}, u32[]{:S(2)}) %collective-permute-start.15) | collective-permute-done | bytes 262176 | tf_op jit(solution)/shard_map/ppermute | solution.py:659
  268.8 1.9 collective-permute-start.16
  270.9 0.1 stack.43.num_ref
  271.0 7.8 %collective-permute-done.16.prv_h = f32[2,2,8,2048]{3,2,1,0:T(8,128)S(1)} collective-permute-done((f32[2,2,8,2048]{3,2,1,0:T(8,128)S(1)}, f32[2,2,8,2048]{3,2,1,0:T(8,128)S(1)}, u32[]{:S(2)}, u32[]{:S(2)}) %collective-permute-start.16) | collective-permute-done | bytes 262176 | tf_op jit(solution)/shard_map/ppermute | solution.py:659
  278.8 13.8 %tv_first.3 = (f32[272,2048]{1,0:T(8,128)S(1)}, f32[4,272,2048]{2,1,0:T(8,128)}) custom-call(f32[5]{0:T(128)S(1)} %stack.43.num_ref, s32[1]{0:T(128)} %bitcast.10.at_ref, f32[256,2048]{1,0:T(8,128)} %get-tuple-element.26.own.parts, f32[256,2048]{1,0:T(8,128)} %collective-permute-done.19.nxt, f32[256,2048]{1,0:T(8,128)} %collective-permute-done.20.prv, ...), custom_call_target="tpu_custom_call" | custom-call | flops 100000000 | bytes 17825792 | tf_op jit(solution)/shard_map/tv_first/pallas_call | solution.py:554
  292.6 1.9 collective-permute-start.21
  294.5 2.4 collective-permute-start.22
  297.0 14.1 %tv_first.2 = (f32[272,2048]{1,0:T(8,128)}, f32[4,272,2048]{2,1,0:T(8,128)}) custom-call(f32[5]{0:T(128)S(1)} %stack.43.num_ref, s32[1]{0:T(128)} %bitcast.10.at_ref, f32[256,2048]{1,0:T(8,128)S(1)} %get-tuple-element.21.own.parts, f32[256,2048]{1,0:T(8,128)} %collective-permute-done.11.nxt, f32[256,2048]{1,0:T(8,128)} %collective-permute-done.12.prv, ...), custom_call_target="tpu_custom_call" | custom-call | flops 100000000 | bytes 17825792 | tf_op jit(solution)/shard_map/tv_first/pallas_call | solution.py:554
  311.1 5.3 %collective-permute-start.17 = (f32[272,2048]{1,0:T(8,128)}, f32[272,2048]{1,0:T(8,128)S(1)}, u32[]{:S(2)}, u32[]{:S(2)}) collective-permute-start(f32[272,2048]{1,0:T(8,128)} %get-tuple-element.24.own), channel_id=1, source_target_pairs={{8,0},{16,8},{24,16},{32,24},{40,32},{48,40},{56,48},{64,56},{72,6... | collective-permute-start | bytes 6684680 | tf_op jit(solution)/shard_map/ppermute | solution.py:659
  316.4 1.9 collective-permute-start.18
  318.4 1.1 collective-permute-done.21.nxt
  319.5 5.9 %collective-permute-done.22.prv = f32[272,2048]{1,0:T(8,128)S(1)} collective-permute-done((f32[272,2048]{1,0:T(8,128)S(1)}, f32[272,2048]{1,0:T(8,128)S(1)}, u32[]{:S(2)}, u32[]{:S(2)}) %collective-permute-start.22) | collective-permute-done | bytes 2228256 | tf_op jit(solution)/shard_map/ppermute | solution.py:659
  325.4 1.4 copy-done.15
  326.8 15.0 %tv_second.2.rest_0_ = f32[2,1,256,2048]{3,2,1,0:T(8,128)} custom-call(f32[5]{0:T(128)} %copy-done.9, s32[1]{0:T(128)} %bitcast.10.at_ref, f32[272,2048]{1,0:T(8,128)} %copy-done.5, f32[272,2048]{1,0:T(8,128)} %copy-done.14, f32[272,2048]{1,0:T(8,128)} %copy-done.15, f32[4,272,2048]{2,1,0:T(8,128)} %get-tuple-element.28.dual, ...), custom_call_target="tpu_custom_call" | custom-call | flops 100000000 | bytes 24117248 | tf_op jit(solution)/shard_map/tv_second/pallas_call | solution.py:641
  341.8 1.6 collective-permute-done.17.nxt
  343.5 5.9 %collective-permute-done.18.prv = f32[272,2048]{1,0:T(8,128)} collective-permute-done((f32[272,2048]{1,0:T(8,128)}, f32[272,2048]{1,0:T(8,128)}, u32[]{:S(2)}, u32[]{:S(2)}) %collective-permute-start.18) | collective-permute-done | bytes 2228256 | tf_op jit(solution)/shard_map/ppermute | solution.py:659
  349.4 15.0 %tv_second.3 = f32[2,1,256,2048]{3,2,1,0:T(8,128)} custom-call(f32[5]{0:T(128)} %copy-done.9, s32[1]{0:T(128)} %bitcast.10.at_ref, f32[272,2048]{1,0:T(8,128)} %get-tuple-element.24.own, f32[272,2048]{1,0:T(8,128)} %copy-done.16, f32[272,2048]{1,0:T(8,128)} %collective-permute-done.18.prv, ...), custom_call_target="tpu_custom_call", output_to_operand_aliasing={{}: (9, {})} | custom-call | flops 100000000 | bytes 24117248 | tf_op jit(solution)/shard_map/tv_second/pallas_call | solution.py:641
  (56 shorter events, 0.2 us)
Async XLA Ops:
  0.0 15.7 %copy-start.7 = (f32[8,2,256]{2,1,0:T(2,128)S(1)}, f32[8,2,256]{2,1,0:T(2,128)}, u32[]{:S(2)}) copy-start(f32[8,2,256]{2,1,0:T(2,128)} %constant.75.clone.tw_ref) | copy-start | bytes 49156
  0.8 2.2 copy-start.2
  3.0 0.7 copy-start.6
  3.7 12.0 %copy-start.12 = (bf16[512,512]{1,0:T(8,128)(2,1)S(1)}, bf16[512,512]{1,0:T(8,128)(2,1)}, u32[]{:S(2)}) copy-start(bf16[512,512]{1,0:T(8,128)(2,1)} %constant.77.clone.gh_ref.ih_ref) | copy-start | bytes 1572868
  3.7 12.0 %copy-start.13 = (bf16[512,512]{1,0:T(8,128)(2,1)S(1)}, bf16[512,512]{1,0:T(8,128)(2,1)}, u32[]{:S(2)}) copy-start(bf16[512,512]{1,0:T(8,128)(2,1)} %constant.78.clone.gl_ref.il_ref) | copy-start | bytes 1572868
  8.8 17.9 %all-to-all-start.1 = ((f32[8,2,16,256]{3,2,1,0:T(8,128)}), f32[8,2,16,256]{3,2,1,0:T(8,128)S(1)}, u32[]{:S(2)}, u32[]{:S(2)}) async-start(f32[8,2,16,256]{3,2,1,0:T(8,128)} %holo_forward.1), calls=%async_computation.1 | async-start | bytes 524288 | tf_op jit(solution)/shard_map/all_to_all | solution.py:693
  15.7 2.2 copy-start
  24.7 2.0 copy-start.3
  26.7 0.7 copy-start.17
  27.5 71.5 %all-to-all-start = ((f32[128,2,16,256]{3,2,1,0:T(8,128)}), f32[128,2,16,256]{3,2,1,0:T(8,128)}, u32[]{:S(2)}, u32[]{:S(2)}) async-start(f32[128,2,16,256]{3,2,1,0:T(8,128)} %bitcast.21), calls=%async_computation | async-start | bytes 8388608 | tf_op jit(solution)/shard_map/all_to_all | solution.py:707
  39.1 1.2 collective-permute-start
  40.3 44.5 %collective-permute-start.1 = (f32[1,128]{1,0:T(1,128)S(1)}, f32[1,128]{1,0:T(1,128)S(1)}, u32[]{:S(2)}, u32[]{:S(2)}) collective-permute-start(f32[1,128]{1,0:T(1,128)S(1)} %fusion.10), channel_id=1, source_target_pairs={{0,16},{8,24},{16,0},{24,8},{32,48},{40,56},{48,32},{56,40},{64,80... | collective-permute-start | bytes 1544 | tf_op jit(solution)/shard_map/ppermute | solution.py:665
  84.8 5.0 %collective-permute-start.2 = (f32[1,128]{1,0:T(1,128)S(1)}, f32[1,128]{1,0:T(1,128)S(1)}, u32[]{:S(2)}, u32[]{:S(2)}) collective-permute-start(f32[1,128]{1,0:T(1,128)S(1)} %fusion.11), channel_id=1, source_target_pairs={{0,32},{8,40},{16,48},{24,56},{32,0},{40,8},{48,16},{56,24},{64,96... | collective-permute-start | bytes 1544 | tf_op jit(solution)/shard_map/ppermute | solution.py:665
  89.9 3.5 collective-permute-start.3
  96.9 2.0 copy-start.4
  118.4 60.2 %copy-start.8 = (f32[8,2,256]{2,1,0:T(2,128)S(1)}, f32[8,2,256]{2,1,0:T(2,128)}, u32[]{:S(2)}) copy-start(f32[8,2,256]{2,1,0:T(2,128)} %constant.75.clone.tw_ref) | copy-start | bytes 49156
  118.4 60.2 %copy-start.10 = (bf16[512,512]{1,0:T(8,128)(2,1)S(1)}, bf16[512,512]{1,0:T(8,128)(2,1)}, u32[]{:S(2)}) copy-start(bf16[512,512]{1,0:T(8,128)(2,1)} %constant.81.clone.ih_ref) | copy-start | bytes 1572868
  118.4 60.2 %copy-start.11 = (bf16[512,512]{1,0:T(8,128)(2,1)S(1)}, bf16[512,512]{1,0:T(8,128)(2,1)}, u32[]{:S(2)}) copy-start(bf16[512,512]{1,0:T(8,128)(2,1)} %constant.82.clone.il_ref) | copy-start | bytes 1572868
  178.5 25.9 %copy-start.18 = (f32[16,128]{1,0:T(8,128)S(1)}, f32[16,128]{1,0:T(8,128)}, u32[]{:S(2)}) copy-start(f32[16,128]{1,0:T(8,128)} %get-tuple-element.19) | copy-start | bytes 24580
  189.5 121.6 %copy-start.1 = (f32[256,2048]{1,0:T(8,128)}, f32[256,2048]{1,0:T(8,128)S(1)}, u32[]{:S(2)}) copy-start(f32[256,2048]{1,0:T(8,128)S(1)} %get-tuple-element.21.own.parts) | copy-start | bytes 6291460
  189.5 89.3 %collective-permute-start.19 = (f32[256,2048]{1,0:T(8,128)}, f32[256,2048]{1,0:T(8,128)}, u32[]{:S(2)}, u32[]{:S(2)}) collective-permute-start(f32[256,2048]{1,0:T(8,128)} %get-tuple-element.26.own.parts), channel_id=1, source_target_pairs={{8,0},{16,8},{24,16},{32,24},{40,32},{48,40},{56,48},{64,56},{72,6... | collective-permute-start | bytes 6291464 | tf_op jit(solution)/shard_map/ppermute | solution.py:659
  194.2 84.5 %collective-permute-start.20 = (f32[256,2048]{1,0:T(8,128)}, f32[256,2048]{1,0:T(8,128)}, u32[]{:S(2)}, u32[]{:S(2)}) collective-permute-start(f32[256,2048]{1,0:T(8,128)} %get-tuple-element.26.own.parts), channel_id=1, source_target_pairs={{0,8},{8,16},{16,24},{24,32},{32,40},{40,48},{48,56},{56,64},{64,7... | collective-permute-start | bytes 6291464 | tf_op jit(solution)/shard_map/ppermute | solution.py:659
  196.2 100.8 %collective-permute-start.11 = (f32[256,2048]{1,0:T(8,128)S(1)}, f32[256,2048]{1,0:T(8,128)}, u32[]{:S(2)}, u32[]{:S(2)}) collective-permute-start(f32[256,2048]{1,0:T(8,128)S(1)} %get-tuple-element.21.own.parts), channel_id=1, source_target_pairs={{8,0},{16,8},{24,16},{32,24},{40,32},{48,40},{56,48},{64,56},{72,6... | collective-permute-start | bytes 6291464 | tf_op jit(solution)/shard_map/ppermute | solution.py:659
  201.9 95.0 %collective-permute-start.12 = (f32[256,2048]{1,0:T(8,128)S(1)}, f32[256,2048]{1,0:T(8,128)}, u32[]{:S(2)}, u32[]{:S(2)}) collective-permute-start(f32[256,2048]{1,0:T(8,128)S(1)} %get-tuple-element.21.own.parts), channel_id=1, source_target_pairs={{0,8},{8,16},{16,24},{24,32},{32,40},{40,48},{48,56},{56,64},{64,7... | collective-permute-start | bytes 6291464 | tf_op jit(solution)/shard_map/ppermute | solution.py:659
  206.4 3.6 collective-permute-start.4
  210.0 5.0 %collective-permute-start.5 = (f32[1,128]{1,0:T(1,128)S(1)}, f32[1,128]{1,0:T(1,128)S(1)}, u32[]{:S(2)}, u32[]{:S(2)}) collective-permute-start(f32[1,128]{1,0:T(1,128)S(1)} %broadcast_add_fusion), channel_id=1, source_target_pairs={{0,2},{1,3},{2,0},{3,1},{4,6},{5,7},{6,4},{7,5},{8,10},{9,11},{10,... | collective-permute-start | bytes 1544 | tf_op jit(solution)/shard_map/ppermute | solution.py:665
  215.1 5.0 %collective-permute-start.6 = (f32[1,128]{1,0:T(1,128)S(1)}, f32[1,128]{1,0:T(1,128)S(1)}, u32[]{:S(2)}, u32[]{:S(2)}) collective-permute-start(f32[1,128]{1,0:T(1,128)S(1)} %fusion.9), channel_id=1, source_target_pairs={{0,4},{1,5},{2,6},{3,7},{4,0},{5,1},{6,2},{7,3},{8,12},{9,13},{10,... | collective-permute-start | bytes 1544 | tf_op jit(solution)/shard_map/ppermute | solution.py:665
  220.1 1.1 collective-permute-start.7
  221.3 19.8 %collective-permute-start.8 = (f32[1,128]{1,0:T(1,128)S(1)}, f32[1,128]{1,0:T(1,128)S(1)}, u32[]{:S(2)}, u32[]{:S(2)}) collective-permute-start(f32[1,128]{1,0:T(1,128)S(1)} %add.131), channel_id=1, source_target_pairs={{0,16},{8,24},{16,0},{24,8},{32,48},{40,56},{48,32},{56,40},{64,80... | collective-permute-start | bytes 1544 | tf_op jit(solution)/shard_map/ppermute | solution.py:665
  241.1 5.0 %collective-permute-start.9 = (f32[1,128]{1,0:T(1,128)S(1)}, f32[1,128]{1,0:T(1,128)S(1)}, u32[]{:S(2)}, u32[]{:S(2)}) collective-permute-start(f32[1,128]{1,0:T(1,128)S(1)} %add.132), channel_id=1, source_target_pairs={{0,32},{8,40},{16,48},{24,56},{32,0},{40,8},{48,16},{56,24},{64,96... | collective-permute-start | bytes 1544 | tf_op jit(solution)/shard_map/ppermute | solution.py:665
  246.1 6.0 %collective-permute-start.13 = (f32[2,8,2048]{2,1,0:T(8,128)S(1)}, f32[2,8,2048]{2,1,0:T(8,128)S(1)}, u32[]{:S(2)}, u32[]{:S(2)}) collective-permute-start(f32[2,8,2048]{2,1,0:T(8,128)S(1)} %get-tuple-element.22), channel_id=1, source_target_pairs={{0,1},{1,2},{2,3},{3,4},{4,5},{5,6},{6,7},{8,9},{9,10},{10,11},{11... | collective-permute-start | bytes 393224 | tf_op jit(solution)/shard_map/ppermute | solution.py:659
  252.2 7.3 %collective-permute-start.14 = (f32[2,8,2048]{2,1,0:T(8,128)S(1)}, f32[2,8,2048]{2,1,0:T(8,128)S(1)}, u32[]{:S(2)}, u32[]{:S(2)}) collective-permute-start(f32[2,8,2048]{2,1,0:T(8,128)S(1)} %get-tuple-element.23), channel_id=1, source_target_pairs={{1,0},{2,1},{3,2},{4,3},{5,4},{6,5},{7,6},{9,8},{10,9},{11,10},{12... | collective-permute-start | bytes 393224 | tf_op jit(solution)/shard_map/ppermute | solution.py:659
  259.5 3.5 collective-permute-start.10
  263.0 5.8 %collective-permute-start.15 = (f32[2,2,8,2048]{3,2,1,0:T(8,128)S(1)}, f32[2,2,8,2048]{3,2,1,0:T(8,128)S(1)}, u32[]{:S(2)}, u32[]{:S(2)}) collective-permute-start(f32[2,2,8,2048]{3,2,1,0:T(8,128)S(1)} %pad_maximum_fusion.own_h), channel_id=1, source_target_pairs={{8,0},{16,8},{24,16},{32,24},{40,32},{48,40},{56,48},{64,56},{72,6... | collective-permute-start | bytes 786440 | tf_op jit(solution)/shard_map/ppermute | solution.py:659
  268.8 10.0 %collective-permute-start.16 = (f32[2,2,8,2048]{3,2,1,0:T(8,128)S(1)}, f32[2,2,8,2048]{3,2,1,0:T(8,128)S(1)}, u32[]{:S(2)}, u32[]{:S(2)}) collective-permute-start(f32[2,2,8,2048]{3,2,1,0:T(8,128)S(1)} %pad_maximum_fusion.own_h), channel_id=1, source_target_pairs={{0,8},{8,16},{16,24},{24,32},{32,40},{40,48},{48,56},{56,64},{64,7... | collective-permute-start | bytes 786440 | tf_op jit(solution)/shard_map/ppermute | solution.py:659
  271.0 40.1 %copy-start.9 = (f32[5]{0:T(128)}, f32[5]{0:T(128)S(1)}, u32[]{:S(2)}) copy-start(f32[5]{0:T(128)S(1)} %stack.43.num_ref) | copy-start | bytes 64
  292.6 18.5 %copy-start.5 = (f32[272,2048]{1,0:T(8,128)}, f32[272,2048]{1,0:T(8,128)S(1)}, u32[]{:S(2)}) copy-start(f32[272,2048]{1,0:T(8,128)S(1)} %get-tuple-element.27.own) | copy-start | bytes 6684676
  292.6 26.9 %collective-permute-start.21 = (f32[272,2048]{1,0:T(8,128)S(1)}, f32[272,2048]{1,0:T(8,128)S(1)}, u32[]{:S(2)}, u32[]{:S(2)}) collective-permute-start(f32[272,2048]{1,0:T(8,128)S(1)} %get-tuple-element.27.own), channel_id=1, source_target_pairs={{8,0},{16,8},{24,16},{32,24},{40,32},{48,40},{56,48},{64,56},{72,6... | collective-permute-start | bytes 6684680 | tf_op jit(solution)/shard_map/ppermute | solution.py:659
  294.5 30.9 %collective-permute-start.22 = (f32[272,2048]{1,0:T(8,128)S(1)}, f32[272,2048]{1,0:T(8,128)S(1)}, u32[]{:S(2)}, u32[]{:S(2)}) collective-permute-start(f32[272,2048]{1,0:T(8,128)S(1)} %get-tuple-element.27.own), channel_id=1, source_target_pairs={{0,8},{8,16},{16,24},{24,32},{32,40},{40,48},{48,56},{56,64},{64,7... | collective-permute-start | bytes 6684680 | tf_op jit(solution)/shard_map/ppermute | solution.py:659
  311.1 32.3 %collective-permute-start.17 = (f32[272,2048]{1,0:T(8,128)}, f32[272,2048]{1,0:T(8,128)S(1)}, u32[]{:S(2)}, u32[]{:S(2)}) collective-permute-start(f32[272,2048]{1,0:T(8,128)} %get-tuple-element.24.own), channel_id=1, source_target_pairs={{8,0},{16,8},{24,16},{32,24},{40,32},{48,40},{56,48},{64,56},{72,6... | collective-permute-start | bytes 6684680 | tf_op jit(solution)/shard_map/ppermute | solution.py:659
  316.4 33.0 %collective-permute-start.18 = (f32[272,2048]{1,0:T(8,128)}, f32[272,2048]{1,0:T(8,128)}, u32[]{:S(2)}, u32[]{:S(2)}) collective-permute-start(f32[272,2048]{1,0:T(8,128)} %get-tuple-element.24.own), channel_id=1, source_target_pairs={{0,8},{8,16},{16,24},{24,32},{32,40},{40,48},{48,56},{56,64},{64,7... | collective-permute-start | bytes 6684680 | tf_op jit(solution)/shard_map/ppermute | solution.py:659
  319.5 5.9 %copy-start.14 = (f32[272,2048]{1,0:T(8,128)}, f32[272,2048]{1,0:T(8,128)S(1)}, u32[]{:S(2)}) copy-start(f32[272,2048]{1,0:T(8,128)S(1)} %collective-permute-done.21.nxt) | copy-start | bytes 6684676
  325.4 1.4 copy-start.15
  343.5 5.9 %copy-start.16 = (f32[272,2048]{1,0:T(8,128)}, f32[272,2048]{1,0:T(8,128)S(1)}, u32[]{:S(2)}) copy-start(f32[272,2048]{1,0:T(8,128)S(1)} %collective-permute-done.17.nxt) | copy-start | bytes 6684676

commit v2 on v1

--- a/solution.py
+++ b/solution.py
@@ -180,7 +180,7 @@
             pltpu.VMEM((RADIX, ROWS, 2 * PART), BF16),
             pltpu.VMEM((RADIX, ROWS, 2 * PART), BF16),
         ],
-        compiler_params=params(40),
+        compiler_params=params(62),
         cost_estimate=pl.CostEstimate(
             flops=4 * 10**9, bytes_accessed=10 * MIB, transcendentals=0
         ),
@@ -188,7 +188,7 @@
     )(x_now, gt_high, gt_low, tw)
 
 
-def holo_body(x_ref, gh_ref, gl_ref, tw_ref, y_ref, hi, lo):
+def holo_body(depth_ref, x_ref, gh_ref, gl_ref, tw_ref, y_ref, hi, lo):
     def chunk(t, carry):
         rows = pl.ds(pl.multiple_of(t * 16, 16), 16)
         for half in range(2):
@@ -201,31 +201,37 @@
         return carry
 
     lax.fori_loop(0, ROWS // 16, chunk, 0)
+    y_ref[...] = jnp.full(y_ref.shape, depth_ref[0], F32)
 
     def per_k(k, carry):
         out = dot3(gh_ref[...], gl_ref[...], hi[k], lo[k], NT)
-        y_ref[k] = out.reshape(2, 16, ROWS)
+        for part in range(2):
+            for half in range(2):
+                y_ref[k, :, part * 2 + half, :] = out[
+                    part * 16 : part * 16 + 16, half * 128 : half * 128 + 128
+                ]
         return carry
 
     lax.fori_loop(0, RADIX, per_k, 0)
 
 
-def holo_forward(hologram, gt_high, gt_low, tw):
+def holo_forward(depths, hologram, gt_high, gt_low, tw):
     return pl.pallas_call(
         holo_body,
-        out_shape=jax.ShapeDtypeStruct((RADIX, 2, 16, ROWS), F32),
+        out_shape=jax.ShapeDtypeStruct((RADIX, 16, 8, 128), F32),
         scratch_shapes=[
             pltpu.VMEM((RADIX, ROWS, 2 * PART), BF16),
             pltpu.VMEM((RADIX, ROWS, 2 * PART), BF16),
         ],
-        in_specs=[pl.BlockSpec(memory_space=pltpu.VMEM)] * 4,
+        in_specs=[pl.BlockSpec(memory_space=pltpu.SMEM)]
+        + [pl.BlockSpec(memory_space=pltpu.VMEM)] * 4,
         out_specs=pl.BlockSpec(memory_space=pltpu.VMEM),
-        compiler_params=params(40),
+        compiler_params=params(62),
         cost_estimate=pl.CostEstimate(
             flops=4 * 10**8, bytes_accessed=5 * MIB, transcendentals=0
         ),
         name="holo_forward",
-    )(hologram, gt_high, gt_low, tw)
+    )(depths, hologram, gt_high, gt_low, tw)
 
 
 def cos_sin(phase):
@@ -272,7 +278,7 @@
         ],
         out_specs=pl.BlockSpec((1, 2, PLANES * 16, PART), lambda k: (k, 0, 0, 0)),
         out_shape=jax.ShapeDtypeStruct((RADIX, 2, PLANES * 16, PART), F32),
-        compiler_params=params(16),
+        compiler_params=params(62),
         cost_estimate=pl.CostEstimate(
             flops=10**7, bytes_accessed=4 * MIB, transcendentals=0
         ),
@@ -281,11 +287,12 @@
 
 
 COLS = PLANES * 16
+MESSAGE = 72
 WITH_HOLO = COLS + 16
 
 
 def spectral_body(
-    z_ref, h_ref, t_ref, gh_ref, gl_ref, ih_ref, il_ref, tw_ref, o_ref, norm_ref,
+    z_ref, h_ref, t_ref, sq_ref, gh_ref, gl_ref, ih_ref, il_ref, tw_ref, o_ref, norm_ref,
     hi, lo, spec, bhi, blo, back,
 ):
     k = pl.program_id(0)
@@ -307,10 +314,9 @@
 
         lax.fori_loop(0, PLANES, chunk, 0)
         for half in range(2):
-            at = slice(half * 128, half * 128 + 128)
 
             def load_holo(i):
-                return (h_ref[i, 0, :, at], h_ref[i, 1, :, at])
+                return (h_ref[i, :, half, :], h_ref[i, :, 2 + half, :])
 
             forward_radix(load_holo, tw_ref, hi, lo, slice(COLS, WITH_HOLO), half)
 
@@ -354,40 +360,44 @@
 
     @pl.when(k == RADIX - 1)
     def _():
+        square = sq_ref[...] + norm_ref[...] * (1.0 / PLANES)
+        square = square[:8, :] + square[8:, :]
+
         def chunk(p, carry):
             rows = pl.ds(pl.multiple_of(p * 16, 16), 16)
+            for i in range(RADIX):
+                o_ref[i, p, 64:MESSAGE, :] = square
             for half in range(2):
                 at = slice(half * 128, half * 128 + 128)
                 out = dft8([(back[i, 0, rows, at], back[i, 1, rows, at]) for i in range(RADIX)], 1)
                 for i in range(RADIX):
-                    o_ref[i, p, 0, :, at] = out[i][0]
-                    o_ref[i, p, 1, :, at] = out[i][1]
+                    o_ref[i, p, half * 16 : half * 16 + 16, :] = out[i][0]
+                    o_ref[i, p, half * 16 + 32 : half * 16 + 48, :] = out[i][1]
             return carry
 
         lax.fori_loop(0, PLANES, chunk, 0)
 
 
-def spectral(z, holo, trans, g_high, g_low, i_high, i_low, tw):
+def spectral(z, holo, trans, squares, g_high, g_low, i_high, i_low, tw):
     table = whole((2 * PART, 2 * PART))
     return pl.pallas_call(
         spectral_body,
         grid=(RADIX,),
         in_specs=[
             whole((RADIX, PLANES, 2, 16, PART)),
-            whole((RADIX, 2, 16, PART)),
+            whole((RADIX, 16, 8, 128)),
             pl.BlockSpec((1, 2, COLS, PART), lambda k: (k, 0, 0, 0)),
+            whole((16, 128)),
             table,
             table,
             table,
             table,
             whole((RADIX, 2, PART)),
         ],
-        out_specs=[whole((RADIX, PLANES, 2, 16, PART)), whole((16, 128))],
-        out_shape=[
-            jax.ShapeDtypeStruct((RADIX, PLANES, 2, 16, PART), F32),
-            jax.ShapeDtypeStruct((16, 128), F32),
-        ],
+        out_specs=whole((RADIX, PLANES, MESSAGE, 128)),
+        out_shape=jax.ShapeDtypeStruct((RADIX, PLANES, MESSAGE, 128), F32),
         scratch_shapes=[
+            pltpu.VMEM((16, 128), F32),
             pltpu.VMEM((RADIX, WITH_HOLO, 2 * PART), BF16),
             pltpu.VMEM((RADIX, WITH_HOLO, 2 * PART), BF16),
             pltpu.VMEM((WITH_HOLO, 2 * PART), F32),
@@ -395,19 +405,27 @@
             pltpu.VMEM((COLS, 2 * PART), BF16),
             pltpu.VMEM((RADIX, 2, COLS, PART), F32),
         ],
-        compiler_params=params(56),
+        compiler_params=params(62),
         cost_estimate=pl.CostEstimate(
             flops=8 * 10**9, bytes_accessed=14 * MIB, transcendentals=0
         ),
         name="spectral",
-    )(z, holo, trans, g_high, g_low, i_high, i_low, tw)
+    )(z, holo, trans, squares, g_high, g_low, i_high, i_low, tw)
 
 
 def rows_back_body(
-    w_ref, x_ref, ih_ref, il_ref, tw_ref, re_ref, im_ref, top_ref, bot_ref, back
+    w_ref, x_ref, ih_ref, il_ref, tw_ref, re_ref, im_ref, top_ref, bot_ref, sum_ref, back
 ):
     k = pl.program_id(0)
-    parts = [w_ref[0, :, c].reshape(PART, ROWS).T for c in range(2)]
+    @pl.when(k == 0)
+    def _():
+        sum_ref[...] = jnp.zeros_like(sum_ref)
+
+    sum_ref[...] += jnp.sum(w_ref[0, :, 64:MESSAGE, :], axis=0)
+    parts = []
+    for c in range(2):
+        halves = [w_ref[0, :, c * 32 + h * 16 : c * 32 + h * 16 + 16, :] for h in range(2)]
+        parts.append(jnp.concatenate([h.reshape(PART, 128).T for h in halves], axis=0))
     high, low = split(jnp.concatenate(parts, axis=1))
     out = dot3(high, low, ih_ref[...], il_ref[...], NN)
     c = tw_ref[k, 0:1, :]
@@ -442,21 +460,28 @@
         rows_back_body,
         grid=(RADIX,),
         in_specs=[
-            pl.BlockSpec((1, 16, 2, 16, ROWS), lambda k: (k, 0, 0, 0, 0)),
+            pl.BlockSpec((1, 16, MESSAGE, 128), lambda k: (k, 0, 0, 0)),
             whole((2, 1, ROWS, N)),
             table,
             table,
             whole((RADIX, 2, PART)),
         ],
-        out_specs=[whole((ROWS, N)), whole((ROWS, N)), whole((2, 8, N)), whole((2, 8, N))],
+        out_specs=[
+            whole((ROWS, N)),
+            whole((ROWS, N)),
+            whole((2, 8, N)),
+            whole((2, 8, N)),
+            whole((8, 128)),
+        ],
         out_shape=[
             jax.ShapeDtypeStruct((ROWS, N), F32),
             jax.ShapeDtypeStruct((ROWS, N), F32),
             jax.ShapeDtypeStruct((2, 8, N), F32),
             jax.ShapeDtypeStruct((2, 8, N), F32),
+            jax.ShapeDtypeStruct((8, 128), F32),
         ],
         scratch_shapes=[pltpu.VMEM((RADIX, 2, ROWS, PART), F32)],
-        compiler_params=params(48),
+        compiler_params=params(62),
         cost_estimate=pl.CostEstimate(
             flops=4 * 10**9, bytes_accessed=13 * MIB, transcendentals=0
         ),
@@ -465,105 +490,191 @@
 
 
 TILES = EXT // 8
-
-
-def below(x, after):
+WIDE = 512
+STAGES = 4
+
+
+def shift_up(x, after):
     row = lax.broadcasted_iota(jnp.int32, x.shape, 0)
     return pltpu.roll(jnp.where(row == 0, after, x), 7, 0)
 
 
-def above(x, before):
+def shift_down(x, before):
     row = lax.broadcasted_iota(jnp.int32, x.shape, 0)
     return pltpu.roll(jnp.where(row == 7, before, x), 1, 0)
 
 
-def right_of(x):
-    return pltpu.roll(x, N - 1, 1)
-
-
-def left_of(x):
-    return pltpu.roll(x, 1, 1)
-
-
-def weight(gz, gy, gx):
-    return 1.0 / (1.0 + jnp.sqrt(gz * gz + gy * gy + gx * gx))
-
-
-def masks(t, row_base):
-    row = lax.broadcasted_iota(jnp.int32, (8, N), 0) + (row_base + t * 8 - 8)
-    col = lax.broadcasted_iota(jnp.int32, (8, N), 1)
-    return (row >= 0) & (row < N - 1), col < N - 1
+def from_right(x, after):
+    if after is None:
+        col = lax.broadcasted_iota(jnp.int32, x.shape, 1)
+        return jnp.where(col == WIDE - 1, x, pltpu.roll(x, WIDE - 1, 1))
+    return pltpu.roll(jnp.concatenate([x, after], axis=1), WIDE + 127, 1)[:, :WIDE]
+
+
+def from_left(x, before):
+    if before is None:
+        col = lax.broadcasted_iota(jnp.int32, x.shape, 1)
+        return jnp.where(col == 0, 0.0, pltpu.roll(x, 1, 1))
+    return pltpu.roll(jnp.concatenate([before, x], axis=1), 1, 1)[:, 128:]
+
+
+def reciprocal(x):
+    guess = pl.reciprocal(x, approx=True)
+    return guess * (2.0 - x * guess)
+
+
+def norm(gz, gy, gx):
+    square = gz * gz + gy * gy + gx * gx
+    return square * lax.rsqrt(square + 1e-30)
+
+
+def patch(ref, lead, rows, start):
+    at = slice(start, start + WIDE)
+    after = None
+    if start + WIDE < N:
+        after = ref[lead + (rows, slice(start + WIDE, start + WIDE + 128))]
+    return ref[lead + (rows, at)], after
 
 
 def tv_first_body(
-    comp, num_ref, at_ref, own, nxt, prv, own_h, nxt_h, prv_h, inner_ref, dual_ref, ext, sems
+    comp, num_ref, at_ref, own, nxt, prv, own_h, nxt_h, prv_h, inner_out, dual_out,
+    ext, inner, dual, in_sems, halo_sems, out_sems,
 ):
-    copies = []
+    size = ROWS // STAGES
+    mains = []
+    halos = []
     for which, (main, halo) in enumerate(((own, own_h), (nxt, nxt_h), (prv, prv_h))):
-        copies += [
-            pltpu.make_async_copy(
-                main, ext.at[which, pl.ds(8, ROWS), :], sems.at[which, 0]
-            ),
-            pltpu.make_async_copy(
-                halo.at[0, comp], ext.at[which, pl.ds(0, 8), :], sems.at[which, 1]
-            ),
-            pltpu.make_async_copy(
-                halo.at[1, comp], ext.at[which, pl.ds(ROWS + 8, 8), :], sems.at[which, 2]
-            ),
-        ]
-    for copy in copies:
-        copy.start()
-    for copy in copies:
-        copy.wait()
+        mains.append(
+            [
+                pltpu.make_async_copy(
+                    main.at[pl.ds(q * size, size), :],
+                    ext.at[which, pl.ds(8 + q * size, size), :],
+                    in_sems.at[which, q],
+                )
+                for q in range(STAGES)
+            ]
+        )
+        halos.append(
+            [
+                pltpu.make_async_copy(
+                    halo.at[end, comp],
+                    ext.at[which, pl.ds(end * (ROWS + 8), 8), :],
+                    halo_sems.at[which, end],
+                )
+                for end in range(2)
+            ]
+        )
+    for q in range(STAGES):
+        for which in range(3):
+            if q == 0:
+                halos[which][0].start()
+            mains[which][q].start()
+            if q == STAGES - 1:
+                halos[which][1].start()
     scale = num_ref[0]
     inverse = num_ref[1]
+    size_of = num_ref[5]
     keep_next = num_ref[2]
     keep_prev = num_ref[3]
-    row_base = at_ref[0]
-
-    def tile(t, before):
+    band = at_ref[0]
+
+    def tile(t, carry):
         rows = pl.ds(pl.multiple_of(t * 8, 8), 8)
         later = pl.ds(pl.multiple_of(jnp.minimum(t + 1, TILES - 1) * 8, 8), 8)
-        row_ok, col_ok = masks(t, row_base)
-        u = ext[0, rows, :]
-        q = ext[2, rows, :]
-        gz = (ext[1, rows, :] - u) * (scale * keep_next)
-        gy = jnp.where(row_ok, (below(u, ext[0, later, :]) - u) * scale, 0.0)
-        gx = jnp.where(col_ok, (right_of(u) - u) * scale, 0.0)
-        w = weight(gz, gy, gx)
-        dz, dy, dx = gz * w, gy * w, gx * w
-        gz = (u - q) * (scale * keep_prev)
-        gy = jnp.where(row_ok, (below(q, ext[2, later, :]) - q) * scale, 0.0)
-        gx = jnp.where(col_ok, (right_of(q) - q) * scale, 0.0)
-        dq = gz * weight(gz, gy, gx)
-        div = (dz - dq) + (dy - above(dy, before)) + (dx - left_of(dx))
-        inner_ref[rows, :] = (div + u * inverse) * STEP_TV
-        dual_ref[0, rows, :] = dz
-        dual_ref[1, rows, :] = dy
-        dual_ref[2, rows, :] = dx
-        dual_ref[3, rows, :] = dq
-        return dy
-
-    lax.fori_loop(0, TILES, tile, jnp.zeros((8, N), F32))
+        earlier = pl.ds(pl.multiple_of(jnp.maximum(t - 1, 0) * 8, 8), 8)
+        left = None
+        for start in range(0, N, WIDE):
+            at = slice(start, start + WIDE)
+            u, u_after = patch(ext, (0,), rows, start)
+            q, q_after = patch(ext, (2,), rows, start)
+            gz = (ext[1, rows, at] - u) * keep_next
+            gy = shift_up(u, ext[0, later, at]) - u
+            gx = from_right(u, u_after) - u
+            w = scale * reciprocal(1.0 + size_of * norm(gz, gy, gx))
+            dz, dy, dx = gz * w, gy * w, gx * w
+            gz = (u - q) * keep_prev
+            gy = shift_up(q, ext[2, later, at]) - q
+            gx = from_right(q, q_after) - q
+            dq = gz * (scale * reciprocal(1.0 + size_of * norm(gz, gy, gx)))
+            above = shift_down(dy, dual[1, earlier, at])
+            div = (dz - dq) + (dy - above) + (dx - from_left(dx, left))
+            left = dx[:, WIDE - 128 :]
+            inner[rows, at] = (div + u * inverse) * STEP_TV
+            dual[0, rows, at] = dz
+            dual[1, rows, at] = dy
+            dual[2, rows, at] = dx
+            dual[3, rows, at] = dq
+        return carry
+
+    outs = []
+    done = 0
+    for q in range(STAGES):
+        for which in range(3):
+            if q == 0:
+                halos[which][0].wait()
+            mains[which][q].wait()
+            if q == STAGES - 1:
+                halos[which][1].wait()
+        if q == 0:
+
+            @pl.when(band == 0)
+            def _():
+                for which in range(3):
+                    ext[which, 7:8, :] = ext[which, 8:9, :]
+
+        if q == STAGES - 1:
+
+            @pl.when(band == N // ROWS - 1)
+            def _():
+                for which in range(3):
+                    ext[which, ROWS + 8 : ROWS + 9, :] = ext[which, ROWS + 7 : ROWS + 8, :]
+
+        upto = TILES if q == STAGES - 1 else (q + 1) * size // 8
+        lax.fori_loop(done, upto, tile, 0)
+        if q == 0:
+
+            @pl.when(band == 0)
+            def _():
+                inner[7:8, :] = inner[8:9, :]
+
+        if q == STAGES - 1:
+
+            @pl.when(band == N // ROWS - 1)
+            def _():
+                inner[ROWS + 8 : ROWS + 9, :] = inner[ROWS + 7 : ROWS + 8, :]
+
+        span = pl.ds(done * 8, (upto - done) * 8)
+        outs += [
+            pltpu.make_async_copy(inner.at[span, :], inner_out.at[span, :], out_sems.at[0, q]),
+            pltpu.make_async_copy(dual.at[:, span, :], dual_out.at[:, span, :], out_sems.at[1, q]),
+        ]
+        outs[-2].start()
+        outs[-1].start()
+        done = upto
+    for copy in outs:
+        copy.wait()
 
 
 def tv_first(comp, numbers, place, own, nxt, prv, own_h, nxt_h, prv_h):
     smem = pl.BlockSpec(memory_space=pltpu.SMEM)
     anywhere = pl.BlockSpec(memory_space=pl.ANY)
-    vmem = pl.BlockSpec(memory_space=pltpu.VMEM)
     return pl.pallas_call(
         functools.partial(tv_first_body, comp),
         in_specs=[smem, smem] + [anywhere] * 6,
-        out_specs=[vmem, vmem],
+        out_specs=[anywhere, anywhere],
         out_shape=[
             jax.ShapeDtypeStruct((EXT, N), F32),
             jax.ShapeDtypeStruct((4, EXT, N), F32),
         ],
         scratch_shapes=[
             pltpu.VMEM((3, EXT, N), F32),
-            pltpu.SemaphoreType.DMA((3, 3)),
-        ],
-        compiler_params=params(40),
+            pltpu.VMEM((EXT, N), F32),
+            pltpu.VMEM((4, EXT, N), F32),
+            pltpu.SemaphoreType.DMA((3, STAGES)),
+            pltpu.SemaphoreType.DMA((3, 2)),
+            pltpu.SemaphoreType.DMA((2, STAGES)),
+        ],
+        compiler_params=params(62),
         cost_estimate=pl.CostEstimate(
             flops=10**8, bytes_accessed=17 * MIB, transcendentals=2 * 10**6
         ),
@@ -572,80 +683,113 @@
 
 
 def tv_second_body(
-    comp, num_ref, at_ref, own, nxt, prv, dual, parts, x_prev, x_now, *rest
+    comp, num_ref, own_in, nxt_in, prv_in, dual_in, parts_in, x_prev_in, x_now_in, *rest
 ):
-    out_ref = rest[-1]
+    out_ref, inner, dual, plain, below, sems, out_sems = rest[-7:]
+    size = ROWS // STAGES
+    copies = []
+    for q in range(STAGES):
+        first = 0 if q == 0 else q * size + 16
+        span = pl.ds(first, (q + 1) * size + 16 - first)
+        main = pl.ds(q * size, size)
+        pairs = [(ref.at[span, :], inner.at[i, span, :]) for i, ref in enumerate((own_in, nxt_in, prv_in))]
+        pairs += [
+            (dual_in.at[:, span, :], dual.at[:, span, :]),
+            (parts_in.at[main, :], plain.at[0, main, :]),
+            (x_prev_in.at[comp, 0, main, :], plain.at[1, main, :]),
+            (x_now_in.at[comp, 0, main, :], plain.at[2, main, :]),
+        ]
+        copies.append(
+            [pltpu.make_async_copy(a, b, sems.at[i, q]) for i, (a, b) in enumerate(pairs)]
+        )
+        for copy in copies[-1]:
+            copy.start()
     strength = num_ref[4]
     keep_next = num_ref[2]
     keep_prev = num_ref[3]
-    row_base = at_ref[0]
-
-    def duals(t):
+
+    def tile(t, carry):
         rows = pl.ds(pl.multiple_of(t * 8, 8), 8)
         later = pl.ds(pl.multiple_of(t * 8 + 8, 8), 8)
-        row_ok, col_ok = masks(t, row_base)
-        u = own[rows, :]
-        gz = (nxt[rows, :] - u) * keep_next
-        gy = jnp.where(row_ok, below(u, own[later, :]) - u, 0.0)
-        gx = jnp.where(col_ok, right_of(u) - u, 0.0)
-        w = weight(gz, gy, gx)
-        return rows, later, row_ok, col_ok, u, gz, gy, gx, w
-
-    _, _, _, _, _, _, gy0, _, w0 = duals(0)
-    first = (dual[1, 0:8, :] + gy0) * w0
-
-    def tile(t, before):
-        rows, later, row_ok, col_ok, u, gz, gy, gx, w = duals(t)
-        dz = (dual[0, rows, :] + gz) * w
-        dy = (dual[1, rows, :] + gy) * w
-        dx = (dual[2, rows, :] + gx) * w
-        q = prv[rows, :]
-        gz = (u - q) * keep_prev
-        gy = jnp.where(row_ok, below(q, prv[later, :]) - q, 0.0)
-        gx = jnp.where(col_ok, right_of(q) - q, 0.0)
-        dq = (dual[3, rows, :] + gz) * weight(gz, gy, gx)
-        div = (dz - dq) + (dy - above(dy, before)) + (dx - left_of(dx))
-        main = pl.ds(pl.multiple_of(t * 8 - 8, 8), 8)
-        denoised = parts[main, :] - strength * div
-        out_ref[0, 0, main, :] = (
-            (1.0 - ALPHA_TWIST) * x_prev[0, 0, main, :]
-            + (ALPHA_TWIST - BETA_TWIST) * x_now[0, 0, main, :]
-            + BETA_TWIST * denoised
+        main = pl.ds(pl.multiple_of(jnp.maximum(t - 1, 0) * 8, 8), 8)
+        left = None
+        for start in range(0, N, WIDE):
+            at = slice(start, start + WIDE)
+            u, u_after = patch(inner, (0,), rows, start)
+            q, q_after = patch(inner, (2,), rows, start)
+            gz = (inner[1, rows, at] - u) * keep_next
+            gy = shift_up(u, inner[0, later, at]) - u
+            gx = from_right(u, u_after) - u
+            w = reciprocal(1.0 + norm(gz, gy, gx))
+            dz = (dual[0, rows, at] + gz) * w
+            dy = (dual[1, rows, at] + gy) * w
+            dx = (dual[2, rows, at] + gx) * w
+            gz = (u - q) * keep_prev
+            gy = shift_up(q, inner[2, later, at]) - q
+            gx = from_right(q, q_after) - q
+            dq = (dual[3, rows, at] + gz) * reciprocal(1.0 + norm(gz, gy, gx))
+            above = shift_down(dy, below[:, at])
+            below[:, at] = dy
+            div = (dz - dq) + (dy - above) + (dx - from_left(dx, left))
+            left = dx[:, WIDE - 128 :]
+            denoised = plain[0, main, at] - strength * div
+            plain[1, main, at] = (
+                (1.0 - ALPHA_TWIST) * plain[1, main, at]
+                + (ALPHA_TWIST - BETA_TWIST) * plain[2, main, at]
+                + BETA_TWIST * denoised
+            )
+        return carry
+
+    def first_rows(start):
+        at = slice(start, start + WIDE)
+        u, u_after = patch(inner, (0,), slice(0, 8), start)
+        gz = (inner[1, 0:8, at] - u) * keep_next
+        gy = shift_up(u, inner[0, 8:16, at]) - u
+        gx = from_right(u, u_after) - u
+        below[:, at] = (dual[1, 0:8, at] + gy) * reciprocal(1.0 + norm(gz, gy, gx))
+
+    outs = []
+    for q in range(STAGES):
+        for copy in copies[q]:
+            copy.wait()
+        if q == 0:
+            for start in range(0, N, WIDE):
+                first_rows(start)
+        lax.fori_loop(1 + q * size // 8, 1 + (q + 1) * size // 8, tile, 0)
+        main = pl.ds(q * size, size)
+        outs.append(
+            pltpu.make_async_copy(
+                plain.at[1, main, :], out_ref.at[comp, 0, main, :], out_sems.at[q]
+            )
         )
-        return dy
-
-    lax.fori_loop(1, TILES - 1, tile, first)
-
-
-def tv_second(comp, numbers, place, own, nxt, prv, dual, parts, x_prev, x_now, into):
+        outs[-1].start()
+    for copy in outs:
+        copy.wait()
+
+
+def tv_second(comp, numbers, own, nxt, prv, dual, parts, x_prev, x_now, into):
     smem = pl.BlockSpec(memory_space=pltpu.SMEM)
     anywhere = pl.BlockSpec(memory_space=pl.ANY)
-    block = pl.BlockSpec((1, 1, ROWS, N), lambda i: (comp, 0, 0, 0))
-    args = [numbers, place, own, nxt, prv, dual, parts, x_prev, x_now]
-    specs = [
-        smem,
-        smem,
-        whole((EXT, N)),
-        whole((EXT, N)),
-        whole((EXT, N)),
-        whole((4, EXT, N)),
-        whole((ROWS, N)),
-        block,
-        block,
-    ]
+    args = [numbers, own, nxt, prv, dual, parts, x_prev, x_now]
     aliases = {}
     if into is not None:
         args.append(into)
-        specs.append(anywhere)
         aliases = {len(args) - 1: 0}
     return pl.pallas_call(
         functools.partial(tv_second_body, comp),
-        grid=(1,),
-        in_specs=specs,
-        out_specs=block,
+        in_specs=[smem] + [anywhere] * (len(args) - 1),
+        out_specs=anywhere,
         out_shape=jax.ShapeDtypeStruct((2, 1, ROWS, N), F32),
+        scratch_shapes=[
+            pltpu.VMEM((3, EXT, N), F32),
+            pltpu.VMEM((4, EXT, N), F32),
+            pltpu.VMEM((3, ROWS, N), F32),
+            pltpu.VMEM((8, N), F32),
+            pltpu.SemaphoreType.DMA((7, STAGES)),
+            pltpu.SemaphoreType.DMA((STAGES,)),
+        ],
         input_output_aliases=aliases,
-        compiler_params=params(60),
+        compiler_params=params(62),
         cost_estimate=pl.CostEstimate(
             flops=10**8, bytes_accessed=23 * MIB, transcendentals=2 * 10**6
         ),
@@ -659,11 +803,8 @@
     return lax.ppermute(x, axis, pairs)
 
 
-def swap_sum(x, axis, bits):
-    count = lax.axis_size(axis)
-    for bit in bits:
-        x = x + lax.ppermute(x, axis, [(i, i ^ bit) for i in range(count)])
-    return x
+def tie(x, *after):
+    return lax.optimization_barrier((x,) + after)[0]
 
 
 def signed_freq(freq):
@@ -685,15 +826,14 @@
     p_high, p_low = split_np(inverse / PLANES)
     t_high, t_low = split_np(forward.T)
     pick = np.stack([t_high, t_low]).reshape(2, 2, 16, 16, 2 * PART)
-    pick = np.ascontiguousarray(pick.transpose(2, 0, 1, 3, 4)).reshape(16, 2, 32, 2 * PART)
+    pick = np.ascontiguousarray(pick.transpose(3, 0, 1, 2, 4)).reshape(16, 2, 32, 2 * PART)
     tw = jnp.asarray(twiddles())
+    both = ("rows", "depth")
 
     chosen = lax.dynamic_index_in_dim(jnp.asarray(pick), d, 0, keepdims=False)
-    holo = holo_forward(hologram, chosen[0], chosen[1], tw)
-    holo = lax.all_to_all(holo, "rows", 0, 0, tiled=True)
-
-    lane = lax.broadcasted_iota(jnp.int32, (1, 128), 1)
-    depth_all = swap_sum(jnp.where(lane == d, depths[0], 0.0), "depth", (1, 2, 4, 8))
+    holo = holo_forward(depths, hologram, chosen[0], chosen[1], tw)
+    holo = lax.all_to_all(holo.reshape(128, 8, 128), both, 0, 0, tiled=True)
+    depth_all = holo[:PLANES, 4, 0].reshape(1, PLANES)
     kx = r + RADIX * (16 * d + jnp.arange(16, dtype=jnp.int32))
     ky = (
         jnp.arange(RADIX, dtype=jnp.int32)[:, None]
@@ -703,23 +843,28 @@
     trans = transfer(depth_all, rate)
 
     sent, squares = rows_forward(x_now, jnp.asarray(t_high), jnp.asarray(t_low), tw)
-    both = ("rows", "depth")
     got = lax.all_to_all(sent.reshape(128, 2, 16, ROWS), both, 0, 0, tiled=True)
-    back, cross = spectral(
+    back = spectral(
         got.reshape(RADIX, PLANES, 2, 16, ROWS),
-        holo,
+        holo.reshape(RADIX, PLANES, 8, 128),
         trans,
+        squares,
         jnp.asarray(g_high),
         jnp.asarray(g_low),
         jnp.asarray(i_high),
         jnp.asarray(i_low),
         tw,
     )
-    ret = lax.all_to_all(back.reshape(128, 2, 16, ROWS), both, 0, 0, tiled=True)
-
-    total = jnp.sum(squares) + jnp.sum(cross) / PLANES
-    total = jnp.full((1, 128), total)
-    total = swap_sum(swap_sum(total, "rows", (1, 2, 4)), "depth", (1, 2, 4, 8))[0, 0]
+    ret = lax.all_to_all(back.reshape(128, MESSAGE, 128), both, 0, 0, tiled=True)
+    re, im, top, bot, sums = rows_back(
+        ret.reshape(RADIX, PLANES, MESSAGE, 128),
+        x_now,
+        jnp.asarray(p_high),
+        jnp.asarray(p_low),
+        tw,
+    )
+
+    total = jnp.sum(sums)
     mean_square = jnp.maximum(total, 0.0) / (2.0 * PLANES * N * N)
     strength = LAMBDA_TV * jnp.sqrt(mean_square + EPSILON)
     numbers = jnp.stack(
@@ -729,43 +874,35 @@
             (d < PLANES - 1).astype(F32),
             (d > 0).astype(F32),
             strength,
+            STEP_TV / strength,
         ]
     )
-    place = jnp.stack([r * ROWS])
-
-    re, im, top, bot = rows_back(
-        ret.reshape(RADIX, PLANES, 2, 16, ROWS), x_now, jnp.asarray(p_high), jnp.asarray(p_low), tw
-    )
-    own = (re, im)
+    place = jnp.stack([r])
+
     halo = jnp.stack([from_behind(bot, "rows", 1), from_behind(top, "rows", -1)])
-    nxt = [from_behind(own[0], "depth", -1)]
-    prv = [from_behind(own[0], "depth", 1)]
+    own = [re, im]
+    nxt = [from_behind(re, "depth", -1)]
+    prv = [from_behind(re, "depth", 1)]
     halo_next = from_behind(halo, "depth", -1)
     halo_prev = from_behind(halo, "depth", 1)
+    own[1] = tie(im, nxt[0], prv[0], halo_next, halo_prev)
     nxt.append(from_behind(own[1], "depth", -1))
     prv.append(from_behind(own[1], "depth", 1))
 
-    out = None
-    firsts = [
-        tv_first(c, numbers, place, own[c], nxt[c], prv[c], halo, halo_next, halo_prev)
-        for c in range(2)
-    ]
-    for c in range(2):
-        inner, dual = firsts[c]
-        out = tv_second(
-            c,
-            numbers,
-            place,
-            inner,
-            from_behind(inner, "depth", -1),
-            from_behind(inner, "depth", 1),
-            dual,
-            own[c],
-            x_prev,
-            x_now,
-            out,
-        )
-    return out
+    inner_re, dual_re = tv_first(0, numbers, place, re, nxt[0], prv[0], halo, halo_next, halo_prev)
+    nxt_re = from_behind(inner_re, "depth", -1)
+    prv_re = from_behind(inner_re, "depth", 1)
+    inner_im, dual_im = tv_first(
+        1, numbers, place, own[1], nxt[1], prv[1], halo, halo_next, halo_prev
+    )
+    nxt_im = from_behind(inner_im, "depth", -1)
+    prv_im = from_behind(inner_im, "depth", 1)
+    out = tv_second(
+        0, numbers, inner_re, nxt_re, prv_re, dual_re, re, x_prev, x_now, None
+    )
+    return tv_second(
+        1, numbers, inner_im, nxt_im, prv_im, dual_im, own[1], x_prev, x_now, out
+    )
 
 
 def solution(mesh):

time: 369 us -> 321 us (0.87)
  waiting for transfers between devices: 121 us -> 93.3 us
  starting transfers between devices: 63.4 us -> 50.7 us
  local copies, waits for them, and re-layouts: 12.1 us -> 2.85 us
  blocking collectives: 60.1 us -> 66.8 us
    ppermute x11 -> x0, waiting for transfers between devices: 86 us -> none  [swap_sum(): x = x + lax.ppermute(x, axis, [(i, i ^ bit) for i in range(count)])]
    all_to_all x1, waiting for transfers between devices: 0.01 us -> 42.3 us  [shards(): got = lax.all_to_all(sent.reshape(128, 2, 16, ROWS), both, 0, 0, tiled=True)]
    ppermute x12, waiting for transfers between devices: 35.1 us -> 48.4 us  [from_behind(): return lax.ppermute(x, axis, pairs)]
    ppermute x11 -> x0, starting transfers between devices: 11.3 us -> none  [swap_sum(): x = x + lax.ppermute(x, axis, [(i, i ^ bit) for i in range(count)])]
    unnamed x38 -> x8, local copies, waits for them, and re-layouts: 11.3 us -> 0.02 us
    all_to_all x1, blocking collectives: 60.1 us -> 66.8 us  [shards(): lax.all_to_all(back.reshape(128, MESSAGE, 128), both, 0, 0, tiled=True)]
    pallas_call x2, Pallas kernels: 28 us -> 22.8 us  [tv_first(): pl.pallas_call(functools.partial(tv_first_body, comp), in_specs=[smem, sm...]
    pallas_call x3, Pallas kernels: 35.2 us -> 30.1 us  [the longest x2 22.6 us: tv_second(): pl.pallas_call(functools.partial(tv_second_body, comp), in_specs=[smem] +...]
  transfers between devices with their start and end apart: 25 -> 14, of which waited for: 19 -> 11; matrix products, arithmetic and copies ran while one was open for 0% -> 1% of each run, Pallas kernels for 15% -> 16%
where the time goes in v2:
time: 321 us; the launch traced here: 320 us
  Pallas kernels  102 us (32%)
  waiting for transfers between devices  93.3 us (29%)
  blocking collectives  66.8 us (21%)
  starting transfers between devices  50.7 us (16%)
    all_to_all x1, blocking collectives, shards(): lax.all_to_all(back.reshape(128, MESSAGE, 128), both, 0, 0, tiled=True)  66.8 us
    ppermute x12, waiting for transfers between devices, from_behind(): return lax.ppermute(x, axis, pairs)  48.4 us
    all_to_all x1, waiting for transfers between devices, shards(): got = lax.all_to_all(sent.reshape(128, 2, 16, ROWS), both, 0, 0, tiled=True)  42.3 us
    ppermute x12, starting transfers between devices, from_behind(): return lax.ppermute(x, axis, pairs)  32.9 us
    pallas_call x2, Pallas kernels, tv_first(): pl.pallas_call(functools.partial(tv_first_body, comp), in_specs=[smem, sm...  22.8 us
    pallas_call x2, Pallas kernels, tv_second(): pl.pallas_call(functools.partial(tv_second_body, comp), in_specs=[smem] +...  22.6 us
    pallas_call x1, Pallas kernels, spectral(): pl.pallas_call(spectral_body, grid=(RADIX,), in_specs=[whole((RADIX, PLAN...  20.1 us
    pallas_call x1, Pallas kernels, rows_back(): pl.pallas_call(rows_back_body, grid=(RADIX,), in_specs=[pl.BlockSpec((1,...  12.2 us
  transfers between devices with their start and end apart: 14, of which 11 were waited for; matrix products, arithmetic and copies ran while one was open for 1% of the time, Pallas kernels for 16%

profile of v2, /device:TPU:32, one launch (start us, length us, event | category | flops | bytes accessed | tf_op | source)
XLA Modules:
  0.0 319.6 jit_solution(7783195027966234925)
XLA Ops:
  0.7 1.4 dynamic-slice_bitcast_fusion
  2.1 7.5 %holo_forward.1 = f32[8,16,8,128]{3,2,1,0:T(8,128)} custom-call(f32[1]{0:T(128)S(6)} %copy.19.depth_ref, f32[2,256,2048]{2,1,0:T(8,128)} %x_ref.4, bf16[32,512]{1,0:T(8,128)(2,1)} %get-tuple-element.30.gh_ref, bf16[32,512]{1,0:T(8,128)(2,1)} %get-tuple-element.29.gl_ref, f32[8,2,256]{2,1,0:T(2,128)} %constant.68.clone.tw_ref), custom_call_target="tpu_custom_call" | custom-call | flops 400000000 | bytes 5242880 | tf_op jit(solution)/shard_map/holo_forward/pallas_call | solution.py:219
  9.6 10.2 %all-to-all-start.1 = ((f32[128,8,128]{2,1,0:T(8,128)}), f32[128,8,128]{2,1,0:T(8,128)S(1)}, u32[]{:S(2)}, u32[]{:S(2)}) async-start(f32[128,8,128]{2,1,0:T(8,128)} %bitcast.23), calls=%async_computation.1 | async-start | bytes 1048576 | tf_op jit(solution)/shard_map/all_to_all | solution.py:835
  19.8 10.6 %rows_forward.1 = (f32[8,16,2,16,256]{4,3,2,1,0:T(8,128)}, f32[16,128]{1,0:T(8,128)}) custom-call(f32[2,1,256,2048]{3,2,1,0:T(8,128)} %x_now_in.3, bf16[512,512]{1,0:T(8,128)(2,1)} %constant.70.clone.gh_ref.ih_ref, bf16[512,512]{1,0:T(8,128)(2,1)} %constant.71.clone.gl_ref.il_ref, f32[8,2,256]{2,1,0:T(2,128)} %constant.68.clone.tw_ref), custom_call_target="tpu_custom_call" | custom-call | flops 4000000000 | bytes 10485760 | tf_op jit(solution)/shard_map/rows_forward/pallas_call | solution.py:162
  30.4 2.6 all-to-all-done.1
  33.0 0.0 copy-start.3
  33.0 7.6 %all-to-all-start = ((f32[128,2,16,256]{3,2,1,0:T(8,128)}), f32[128,2,16,256]{3,2,1,0:T(8,128)}, u32[]{:S(2)}, u32[]{:S(2)}) async-start(f32[128,2,16,256]{3,2,1,0:T(8,128)} %bitcast.22), calls=%async_computation | async-start | bytes 8388608 | tf_op jit(solution)/shard_map/all_to_all | solution.py:846
  40.7 0.8 fusion.rate_ref
  41.5 0.0 copy-done.3
  41.5 0.8 slice_reduce_fusion
  42.3 6.3 %transfer.1.t_ref = f32[8,2,256,256]{3,2,1,0:T(8,128)} custom-call(f32[1,16]{1,0:T(1,128)} %bitcast.27, f32[8,16,256]{2,1,0:T(8,128)} %fusion.rate_ref), custom_call_target="tpu_custom_call" | custom-call | flops 10000000 | bytes 4194304 | tf_op jit(solution)/shard_map/transfer/pallas_call | solution.py:272
  48.5 42.3 %all-to-all-done = f32[128,2,16,256]{3,2,1,0:T(8,128)} async-done(((f32[128,2,16,256]{3,2,1,0:T(8,128)}), f32[128,2,16,256]{3,2,1,0:T(8,128)}, u32[]{:S(2)}, u32[]{:S(2)}) %all-to-all-start) | async-done | bytes 4194336 | tf_op jit(solution)/shard_map/all_to_all | solution.py:846
  90.8 20.1 %spectral.1 = f32[8,16,72,128]{3,2,1,0:T(8,128)} custom-call(f32[8,16,2,16,256]{4,3,2,1,0:T(8,128)} %bitcast.1.z_ref, f32[8,16,8,128]{3,2,1,0:T(8,128)} %bitcast.24, f32[8,2,256,256]{3,2,1,0:T(8,128)} %transfer.1.t_ref, f32[16,128]{1,0:T(8,128)} %get-tuple-element.18.sq_ref, bf16[512,512]{1,0:T(8,128)(2,1)} %constant.72.clone.gh_ref, ...), custom_call_target="tpu_custom_call" | custom-call | flops 8000000000 | bytes 14680064 | tf_op jit(solution)/shard_map/spectral/pallas_call | solution.py:383
  110.9 66.8 %all_to_all.15 = f32[128,72,128]{2,1,0:T(8,128)} all-to-all(f32[128,72,128]{2,1,0:T(8,128)} %bitcast.21), channel_id=1, replica_groups=mesh['depth'=16,'rows'=8] {'rows','depth'}, dimensions={0} | all-to-all | bytes 9437184 | tf_op jit(solution)/shard_map/all_to_all | solution.py:858
  177.8 12.2 %rows_back.1 = (f32[256,2048]{1,0:T(8,128)}, f32[256,2048]{1,0:T(8,128)}, f32[2,8,2048]{2,1,0:T(8,128)}, f32[2,8,2048]{2,1,0:T(8,128)}, f32[8,128]{1,0:T(8,128)}) custom-call(f32[8,16,72,128]{3,2,1,0:T(8,128)} %bitcast.20, f32[2,1,256,2048]{3,2,1,0:T(8,128)} %x_now_in.3, bf16[512,512]{1,0:T(8,128)(2,1)} %constant.74.clone.ih_ref, ...), custom_call_target="tpu_custom_call" | custom-call | flops 4000000000 | bytes 13631488 | tf_op jit(solution)/shard_map/rows_back/pallas_call | solution.py:459
  189.9 3.5 %collective-permute-start = (f32[256,2048]{1,0:T(8,128)}, f32[256,2048]{1,0:T(8,128)}, u32[]{:S(2)}, u32[]{:S(2)}) collective-permute-start(f32[256,2048]{1,0:T(8,128)} %get-tuple-element.21.own.parts_in), channel_id=1, source_target_pairs={{8,0},{16,8},{24,16},{32,24},{40,32},{48,40},{56,48},{64,56},{72,6... | collective-permute-start | bytes 6291464 | tf_op jit(solution)/shard_map/ppermute | solution.py:803
  193.5 1.9 collective-permute-start.1
  195.4 3.6 %collective-permute-start.2 = (f32[2,8,2048]{2,1,0:T(8,128)}, f32[2,8,2048]{2,1,0:T(8,128)S(1)}, u32[]{:S(2)}, u32[]{:S(2)}) collective-permute-start(f32[2,8,2048]{2,1,0:T(8,128)} %get-tuple-element.22), channel_id=1, source_target_pairs={{0,1},{1,2},{2,3},{3,4},{4,5},{5,6},{6,7},{8,9},{9,10},{10,11},{11... | collective-permute-start | bytes 393224 | tf_op jit(solution)/shard_map/ppermute | solution.py:803
  199.0 1.3 collective-permute-start.3
  200.3 1.5 collective-permute-done.2
  201.9 4.3 %collective-permute-done.3 = f32[2,8,2048]{2,1,0:T(8,128)S(1)} collective-permute-done((f32[2,8,2048]{2,1,0:T(8,128)}, f32[2,8,2048]{2,1,0:T(8,128)S(1)}, u32[]{:S(2)}, u32[]{:S(2)}) %collective-permute-start.3) | collective-permute-done | bytes 131104 | tf_op jit(solution)/shard_map/ppermute | solution.py:803
  206.1 0.0 copy-start
  206.2 4.7 %collective-permute-start.4 = (f32[2,2,8,2048]{3,2,1,0:T(8,128)S(1)}, f32[2,2,8,2048]{3,2,1,0:T(8,128)S(1)}, u32[]{:S(2)}, u32[]{:S(2)}) collective-permute-start(f32[2,2,8,2048]{3,2,1,0:T(8,128)S(1)} %pad_maximum_fusion.own_h), channel_id=1, source_target_pairs={{8,0},{16,8},{24,16},{32,24},{40,32},{48,40},{56,48},{64,56},{72,6... | collective-permute-start | bytes 786440 | tf_op jit(solution)/shard_map/ppermute | solution.py:803
  210.9 1.9 collective-permute-start.5
  212.8 10.0 %collective-permute-done.4.nxt_h = f32[2,2,8,2048]{3,2,1,0:T(8,128)S(1)} collective-permute-done((f32[2,2,8,2048]{3,2,1,0:T(8,128)S(1)}, f32[2,2,8,2048]{3,2,1,0:T(8,128)S(1)}, u32[]{:S(2)}, u32[]{:S(2)}) %collective-permute-start.4) | collective-permute-done | bytes 262176 | tf_op jit(solution)/shard_map/ppermute | solution.py:803
  222.8 0.0 copy-start.1
  222.8 6.0 %collective-permute-done.5.prv_h = f32[2,2,8,2048]{3,2,1,0:T(8,128)S(1)} collective-permute-done((f32[2,2,8,2048]{3,2,1,0:T(8,128)S(1)}, f32[2,2,8,2048]{3,2,1,0:T(8,128)S(1)}, u32[]{:S(2)}, u32[]{:S(2)}) %collective-permute-start.5) | collective-permute-done | bytes 262176 | tf_op jit(solution)/shard_map/ppermute | solution.py:803
  228.8 0.0 copy-start.2
  228.8 0.0 collective-permute-done.nxt
  228.8 0.0 collective-permute-done.1.prv
  228.8 1.9 collective-permute-start.6
  230.7 2.4 collective-permute-start.7
  233.1 1.3 reduce_sum.9
  235.3 0.7 stack.47.num_ref
  235.9 0.0 copy-done
  235.9 0.0 copy-done.1
  235.9 0.0 copy-done.2
  235.9 11.4 %tv_first.3 = (f32[272,2048]{1,0:T(8,128)}, f32[4,272,2048]{2,1,0:T(8,128)}) custom-call(f32[6]{0:T(128)} %stack.47.num_ref, s32[1]{0:T(128)} %bitcast.14.at_ref, f32[256,2048]{1,0:T(8,128)} %get-tuple-element.21.own.parts_in, f32[256,2048]{1,0:T(8,128)} %collective-permute-done.nxt, f32[256,2048]{1,0:T(8,128)} %collective-permute-done.1.prv, ...), custom_call_target="tpu_custom_call" | custom-call | flops 100000000 | bytes 17825792 | tf_op jit(solution)/shard_map/tv_first/pallas_call | solution.py:661
  247.3 5.3 %collective-permute-start.10 = (f32[272,2048]{1,0:T(8,128)}, f32[272,2048]{1,0:T(8,128)}, u32[]{:S(2)}, u32[]{:S(2)}) collective-permute-start(f32[272,2048]{1,0:T(8,128)} %get-tuple-element.27.own_in), channel_id=1, source_target_pairs={{8,0},{16,8},{24,16},{32,24},{40,32},{48,40},{56,48},{64,56},{72,6... | collective-permute-start | bytes 6684680 | tf_op jit(solution)/shard_map/ppermute | solution.py:803
  252.6 1.9 collective-permute-start.11
  254.5 0.0 collective-permute-done.6.nxt
  254.6 5.9 %collective-permute-done.7.prv = f32[256,2048]{1,0:T(8,128)} collective-permute-done((f32[256,2048]{1,0:T(8,128)}, f32[256,2048]{1,0:T(8,128)}, u32[]{:S(2)}, u32[]{:S(2)}) %collective-permute-start.7) | collective-permute-done | bytes 2097184 | tf_op jit(solution)/shard_map/ppermute | solution.py:803
  260.5 11.4 %tv_first.2 = (f32[272,2048]{1,0:T(8,128)}, f32[4,272,2048]{2,1,0:T(8,128)}) custom-call(f32[6]{0:T(128)} %stack.47.num_ref, s32[1]{0:T(128)} %bitcast.14.at_ref, f32[256,2048]{1,0:T(8,128)} %get-tuple-element.24.own.parts_in, f32[256,2048]{1,0:T(8,128)} %collective-permute-done.6.nxt, f32[256,2048]{1,0:T(8,128)} %collective-permute-done.7.prv, ...), custom_call_target="tpu_custom_call" | custom-call | flops 100000000 | bytes 17825792 | tf_op jit(solution)/shard_map/tv_first/pallas_call | solution.py:661
  271.9 1.9 collective-permute-start.8
  273.8 2.4 collective-permute-start.9
  276.3 2.2 collective-permute-done.10.nxt_in
  278.4 5.9 %collective-permute-done.11.prv_in = f32[272,2048]{1,0:T(8,128)} collective-permute-done((f32[272,2048]{1,0:T(8,128)}, f32[272,2048]{1,0:T(8,128)}, u32[]{:S(2)}, u32[]{:S(2)}) %collective-permute-start.11) | collective-permute-done | bytes 2228256 | tf_op jit(solution)/shard_map/ppermute | solution.py:803
  284.4 11.3 %tv_second.2.rest_0_ = f32[2,1,256,2048]{3,2,1,0:T(8,128)} custom-call(f32[6]{0:T(128)} %stack.47.num_ref, f32[272,2048]{1,0:T(8,128)} %get-tuple-element.27.own_in, f32[272,2048]{1,0:T(8,128)} %collective-permute-done.10.nxt_in, f32[272,2048]{1,0:T(8,128)} %collective-permute-done.11.prv_in, f32[4,272,2048]{2,1,0:T(8,128)} %get-tuple-element.28.dual_in, ...), custom_call_target="tpu_custom_call" | custom-call | flops 100000000 | bytes 24117248 | tf_op jit(solution)/shard_map/tv_second/pallas_call | solution.py:778
  295.7 6.6 %collective-permute-done.8.nxt_in = f32[272,2048]{1,0:T(8,128)} collective-permute-done((f32[272,2048]{1,0:T(8,128)}, f32[272,2048]{1,0:T(8,128)}, u32[]{:S(2)}, u32[]{:S(2)}) %collective-permute-start.8) | collective-permute-done | bytes 2228256 | tf_op jit(solution)/shard_map/ppermute | solution.py:803
  302.3 5.9 %collective-permute-done.9.prv_in = f32[272,2048]{1,0:T(8,128)} collective-permute-done((f32[272,2048]{1,0:T(8,128)}, f32[272,2048]{1,0:T(8,128)}, u32[]{:S(2)}, u32[]{:S(2)}) %collective-permute-start.9) | collective-permute-done | bytes 2228256 | tf_op jit(solution)/shard_map/ppermute | solution.py:803
  308.3 11.3 %tv_second.3 = f32[2,1,256,2048]{3,2,1,0:T(8,128)} custom-call(f32[6]{0:T(128)} %stack.47.num_ref, f32[272,2048]{1,0:T(8,128)} %get-tuple-element.25.own_in, f32[272,2048]{1,0:T(8,128)} %collective-permute-done.8.nxt_in, f32[272,2048]{1,0:T(8,128)} %collective-permute-done.9.prv_in, ...), custom_call_target="tpu_custom_call", output_to_operand_aliasing={{}: (8, {})} | custom-call | flops 100000000 | bytes 24117248 | tf_op jit(solution)/shard_map/tv_second/pallas_call | solution.py:778
  (4 shorter events, 0.0 us)
Async XLA Ops:
  9.6 23.5 %all-to-all-start.1 = ((f32[128,8,128]{2,1,0:T(8,128)}), f32[128,8,128]{2,1,0:T(8,128)S(1)}, u32[]{:S(2)}, u32[]{:S(2)}) async-start(f32[128,8,128]{2,1,0:T(8,128)} %bitcast.23), calls=%async_computation.1 | async-start | bytes 1048576 | tf_op jit(solution)/shard_map/all_to_all | solution.py:835
  33.0 8.5 %copy-start.3 = (f32[128,8,128]{2,1,0:T(8,128)}, f32[128,8,128]{2,1,0:T(8,128)S(1)}, u32[]{:S(2)}) copy-start(f32[128,8,128]{2,1,0:T(8,128)S(1)} %all-to-all-done.1) | copy-start | bytes 1572868
  33.0 57.8 %all-to-all-start = ((f32[128,2,16,256]{3,2,1,0:T(8,128)}), f32[128,2,16,256]{3,2,1,0:T(8,128)}, u32[]{:S(2)}, u32[]{:S(2)}) async-start(f32[128,2,16,256]{3,2,1,0:T(8,128)} %bitcast.22), calls=%async_computation | async-start | bytes 8388608 | tf_op jit(solution)/shard_map/all_to_all | solution.py:846
  189.9 38.8 %collective-permute-start = (f32[256,2048]{1,0:T(8,128)}, f32[256,2048]{1,0:T(8,128)}, u32[]{:S(2)}, u32[]{:S(2)}) collective-permute-start(f32[256,2048]{1,0:T(8,128)} %get-tuple-element.21.own.parts_in), channel_id=1, source_target_pairs={{8,0},{16,8},{24,16},{32,24},{40,32},{48,40},{56,48},{64,56},{72,6... | collective-permute-start | bytes 6291464 | tf_op jit(solution)/shard_map/ppermute | solution.py:803
  193.5 35.3 %collective-permute-start.1 = (f32[256,2048]{1,0:T(8,128)}, f32[256,2048]{1,0:T(8,128)}, u32[]{:S(2)}, u32[]{:S(2)}) collective-permute-start(f32[256,2048]{1,0:T(8,128)} %get-tuple-element.21.own.parts_in), channel_id=1, source_target_pairs={{0,8},{8,16},{16,24},{24,32},{32,40},{40,48},{48,56},{56,64},{64,7... | collective-permute-start | bytes 6291464 | tf_op jit(solution)/shard_map/ppermute | solution.py:803
  195.4 6.4 %collective-permute-start.2 = (f32[2,8,2048]{2,1,0:T(8,128)}, f32[2,8,2048]{2,1,0:T(8,128)S(1)}, u32[]{:S(2)}, u32[]{:S(2)}) collective-permute-start(f32[2,8,2048]{2,1,0:T(8,128)} %get-tuple-element.22), channel_id=1, source_target_pairs={{0,1},{1,2},{2,3},{3,4},{4,5},{5,6},{6,7},{8,9},{9,10},{10,11},{11... | collective-permute-start | bytes 393224 | tf_op jit(solution)/shard_map/ppermute | solution.py:803
  199.0 7.1 %collective-permute-start.3 = (f32[2,8,2048]{2,1,0:T(8,128)}, f32[2,8,2048]{2,1,0:T(8,128)S(1)}, u32[]{:S(2)}, u32[]{:S(2)}) collective-permute-start(f32[2,8,2048]{2,1,0:T(8,128)} %get-tuple-element.23), channel_id=1, source_target_pairs={{1,0},{2,1},{3,2},{4,3},{5,4},{6,5},{7,6},{9,8},{10,9},{11,10},{12... | collective-permute-start | bytes 393224 | tf_op jit(solution)/shard_map/ppermute | solution.py:803
  206.1 29.8 %copy-start = (f32[2,2,8,2048]{3,2,1,0:T(8,128)}, f32[2,2,8,2048]{3,2,1,0:T(8,128)S(1)}, u32[]{:S(2)}) copy-start(f32[2,2,8,2048]{3,2,1,0:T(8,128)S(1)} %pad_maximum_fusion.own_h) | copy-start | bytes 786436
  206.2 16.6 %collective-permute-start.4 = (f32[2,2,8,2048]{3,2,1,0:T(8,128)S(1)}, f32[2,2,8,2048]{3,2,1,0:T(8,128)S(1)}, u32[]{:S(2)}, u32[]{:S(2)}) collective-permute-start(f32[2,2,8,2048]{3,2,1,0:T(8,128)S(1)} %pad_maximum_fusion.own_h), channel_id=1, source_target_pairs={{8,0},{16,8},{24,16},{32,24},{40,32},{48,40},{56,48},{64,56},{72,6... | collective-permute-start | bytes 786440 | tf_op jit(solution)/shard_map/ppermute | solution.py:803
  210.9 17.9 %collective-permute-start.5 = (f32[2,2,8,2048]{3,2,1,0:T(8,128)S(1)}, f32[2,2,8,2048]{3,2,1,0:T(8,128)S(1)}, u32[]{:S(2)}, u32[]{:S(2)}) collective-permute-start(f32[2,2,8,2048]{3,2,1,0:T(8,128)S(1)} %pad_maximum_fusion.own_h), channel_id=1, source_target_pairs={{0,8},{8,16},{16,24},{24,32},{32,40},{40,48},{48,56},{56,64},{64,7... | collective-permute-start | bytes 786440 | tf_op jit(solution)/shard_map/ppermute | solution.py:803
  222.8 13.1 %copy-start.1 = (f32[2,2,8,2048]{3,2,1,0:T(8,128)}, f32[2,2,8,2048]{3,2,1,0:T(8,128)S(1)}, u32[]{:S(2)}) copy-start(f32[2,2,8,2048]{3,2,1,0:T(8,128)S(1)} %collective-permute-done.4.nxt_h) | copy-start | bytes 786436
  228.8 7.1 %copy-start.2 = (f32[2,2,8,2048]{3,2,1,0:T(8,128)}, f32[2,2,8,2048]{3,2,1,0:T(8,128)S(1)}, u32[]{:S(2)}) copy-start(f32[2,2,8,2048]{3,2,1,0:T(8,128)S(1)} %collective-permute-done.5.prv_h) | copy-start | bytes 786436
  228.8 25.8 %collective-permute-start.6 = (f32[256,2048]{1,0:T(8,128)}, f32[256,2048]{1,0:T(8,128)}, u32[]{:S(2)}, u32[]{:S(2)}) collective-permute-start(f32[256,2048]{1,0:T(8,128)} %get-tuple-element.24.own.parts_in), channel_id=1, source_target_pairs={{8,0},{16,8},{24,16},{32,24},{40,32},{48,40},{56,48},{64,56},{72,6... | collective-permute-start | bytes 6291464 | tf_op jit(solution)/shard_map/ppermute | solution.py:803
  230.7 29.8 %collective-permute-start.7 = (f32[256,2048]{1,0:T(8,128)}, f32[256,2048]{1,0:T(8,128)}, u32[]{:S(2)}, u32[]{:S(2)}) collective-permute-start(f32[256,2048]{1,0:T(8,128)} %get-tuple-element.24.own.parts_in), channel_id=1, source_target_pairs={{0,8},{8,16},{16,24},{24,32},{32,40},{40,48},{48,56},{56,64},{64,7... | collective-permute-start | bytes 6291464 | tf_op jit(solution)/shard_map/ppermute | solution.py:803
  247.3 31.1 %collective-permute-start.10 = (f32[272,2048]{1,0:T(8,128)}, f32[272,2048]{1,0:T(8,128)}, u32[]{:S(2)}, u32[]{:S(2)}) collective-permute-start(f32[272,2048]{1,0:T(8,128)} %get-tuple-element.27.own_in), channel_id=1, source_target_pairs={{8,0},{16,8},{24,16},{32,24},{40,32},{48,40},{56,48},{64,56},{72,6... | collective-permute-start | bytes 6684680 | tf_op jit(solution)/shard_map/ppermute | solution.py:803
  252.6 31.8 %collective-permute-start.11 = (f32[272,2048]{1,0:T(8,128)}, f32[272,2048]{1,0:T(8,128)}, u32[]{:S(2)}, u32[]{:S(2)}) collective-permute-start(f32[272,2048]{1,0:T(8,128)} %get-tuple-element.27.own_in), channel_id=1, source_target_pairs={{0,8},{8,16},{16,24},{24,32},{32,40},{40,48},{48,56},{56,64},{64,7... | collective-permute-start | bytes 6684680 | tf_op jit(solution)/shard_map/ppermute | solution.py:803
  271.9 30.4 %collective-permute-start.8 = (f32[272,2048]{1,0:T(8,128)}, f32[272,2048]{1,0:T(8,128)}, u32[]{:S(2)}, u32[]{:S(2)}) collective-permute-start(f32[272,2048]{1,0:T(8,128)} %get-tuple-element.25.own_in), channel_id=1, source_target_pairs={{8,0},{16,8},{24,16},{32,24},{40,32},{48,40},{56,48},{64,56},{72,6... | collective-permute-start | bytes 6684680 | tf_op jit(solution)/shard_map/ppermute | solution.py:803
  273.8 34.4 %collective-permute-start.9 = (f32[272,2048]{1,0:T(8,128)}, f32[272,2048]{1,0:T(8,128)}, u32[]{:S(2)}, u32[]{:S(2)}) collective-permute-start(f32[272,2048]{1,0:T(8,128)} %get-tuple-element.25.own_in), channel_id=1, source_target_pairs={{0,8},{8,16},{16,24},{24,32},{32,40},{40,48},{48,56},{56,64},{64,7... | collective-permute-start | bytes 6684680 | tf_op jit(solution)/shard_map/ppermute | solution.py:803

commit v3 on v2

--- a/solution.py
+++ b/solution.py
@@ -23,6 +23,7 @@
 RADIX = 8
 PART = 256
 EXT = ROWS + 16
+PACK = ROWS + 8
 F32 = jnp.float32
 BF16 = jnp.bfloat16
 MIB = 1024 * 1024
@@ -42,6 +43,11 @@
     forward = np.block([[cos, -sin], [sin, cos]])
     inverse = np.block([[cos, sin], [-sin, cos]])
     return forward, inverse
+
+
+def halo_table(inverse):
+    rows = inverse[:PART].reshape(16, 2, 8, 2 * PART)
+    return np.ascontiguousarray(rows.transpose(1, 0, 2, 3)).reshape(PART, 2 * PART)
 
 
 def twiddles():
@@ -129,11 +135,25 @@
     return pl.BlockSpec(shape, lambda *_: (0,) * len(shape))
 
 
-def rows_body(x_ref, gh_ref, gl_ref, tw_ref, y_ref, ss_ref, hi, lo):
+def stage_copies(pairs, sems):
+    copies = [pltpu.make_async_copy(a, b, sems.at[i]) for i, (a, b) in enumerate(pairs)]
+    for copy in copies:
+        copy.start()
+    return copies
+
+
+def quarter(q):
+    return pl.ds(q * (ROWS // 4), ROWS // 4)
+
+
+def rows_body(x_in, g_in, tw_ref, y_ref, ss_ref, hi, lo, x_ref, g_ref, sems):
     k = pl.program_id(0)
 
     @pl.when(k == 0)
     def _():
+        pairs = [(x_in.at[:, :, quarter(q), :], x_ref.at[:, :, quarter(q), :]) for q in range(4)]
+        copies = stage_copies(pairs + [(g_in, g_ref)], sems)
+
         def chunk(t, total):
             rows = pl.ds(pl.multiple_of(t * 16, 16), 16)
             for half in range(2):
@@ -148,9 +168,14 @@
                 forward_radix(lambda i: patches[i], tw_ref, hi, lo, rows, half)
             return total
 
-        ss_ref[...] = lax.fori_loop(0, ROWS // 16, chunk, jnp.zeros((16, 128), F32))
-
-    gh, gl = gh_ref, gl_ref
+        total = jnp.zeros((16, 128), F32)
+        for q in range(4):
+            copies[q].wait()
+            total = lax.fori_loop(q * 4, q * 4 + 4, chunk, total)
+        ss_ref[...] = total
+        copies[4].wait()
+
+    gh, gl = g_ref.at[0], g_ref.at[1]
     high, low = hi[k], lo[k]
     for part in range(2):
         at = slice(part * PART, part * PART + PART)
@@ -158,14 +183,14 @@
         y_ref[0, :, part] = out.reshape(16, 16, ROWS)
 
 
-def rows_forward(x_now, gt_high, gt_low, tw):
+def rows_forward(x_now, table, tw):
+    anywhere = pl.BlockSpec(memory_space=pl.ANY)
     return pl.pallas_call(
         rows_body,
         grid=(RADIX,),
         in_specs=[
-            whole((2, 1, ROWS, N)),
-            whole((2 * PART, 2 * PART)),
-            whole((2 * PART, 2 * PART)),
+            anywhere,
+            anywhere,
             whole((RADIX, 2, PART)),
         ],
         out_specs=[
@@ -179,16 +204,22 @@
         scratch_shapes=[
             pltpu.VMEM((RADIX, ROWS, 2 * PART), BF16),
             pltpu.VMEM((RADIX, ROWS, 2 * PART), BF16),
+            pltpu.VMEM((2, 1, ROWS, N), F32),
+            pltpu.VMEM((2, 2 * PART, 2 * PART), BF16),
+            pltpu.SemaphoreType.DMA((5,)),
         ],
         compiler_params=params(62),
         cost_estimate=pl.CostEstimate(
             flops=4 * 10**9, bytes_accessed=10 * MIB, transcendentals=0
         ),
         name="rows_forward",
-    )(x_now, gt_high, gt_low, tw)
-
-
-def holo_body(depth_ref, x_ref, gh_ref, gl_ref, tw_ref, y_ref, hi, lo):
+    )(x_now, table, tw)
+
+
+def holo_body(depth_ref, x_in, gh_ref, gl_ref, tw_ref, y_ref, hi, lo, x_ref, sems):
+    pairs = [(x_in.at[:, quarter(q), :], x_ref.at[:, quarter(q), :]) for q in range(4)]
+    copies = stage_copies(pairs, sems)
+
     def chunk(t, carry):
         rows = pl.ds(pl.multiple_of(t * 16, 16), 16)
         for half in range(2):
@@ -200,7 +231,9 @@
             forward_radix(load, tw_ref, hi, lo, rows, half)
         return carry
 
-    lax.fori_loop(0, ROWS // 16, chunk, 0)
+    for q in range(4):
+        copies[q].wait()
+        lax.fori_loop(q * 4, q * 4 + 4, chunk, 0)
     y_ref[...] = jnp.full(y_ref.shape, depth_ref[0], F32)
 
     def per_k(k, carry):
@@ -222,9 +255,14 @@
         scratch_shapes=[
             pltpu.VMEM((RADIX, ROWS, 2 * PART), BF16),
             pltpu.VMEM((RADIX, ROWS, 2 * PART), BF16),
-        ],
-        in_specs=[pl.BlockSpec(memory_space=pltpu.SMEM)]
-        + [pl.BlockSpec(memory_space=pltpu.VMEM)] * 4,
+            pltpu.VMEM((2, ROWS, N), F32),
+            pltpu.SemaphoreType.DMA((4,)),
+        ],
+        in_specs=[
+            pl.BlockSpec(memory_space=pltpu.SMEM),
+            pl.BlockSpec(memory_space=pl.ANY),
+        ]
+        + [pl.BlockSpec(memory_space=pltpu.VMEM)] * 3,
         out_specs=pl.BlockSpec(memory_space=pltpu.VMEM),
         compiler_params=params(62),
         cost_estimate=pl.CostEstimate(
@@ -291,15 +329,21 @@
 WITH_HOLO = COLS + 16
 
 
+def planes_of(q):
+    return pl.ds(q * 4, 4)
+
+
 def spectral_body(
-    z_ref, h_ref, t_ref, sq_ref, gh_ref, gl_ref, ih_ref, il_ref, tw_ref, o_ref, norm_ref,
-    hi, lo, spec, bhi, blo, back,
+    z_in, h_ref, t_ref, sq_ref, g_in, tw_ref, o_out, norm_ref,
+    hi, lo, spec, bhi, blo, back, z_ref, g_ref, o_ref, sems, out_sems,
 ):
     k = pl.program_id(0)
 
     @pl.when(k == 0)
     def _():
         norm_ref[...] = jnp.zeros_like(norm_ref)
+        pairs = [(z_in.at[:, planes_of(q)], z_ref.at[:, planes_of(q)]) for q in range(4)]
+        copies = stage_copies(pairs + [(g_in, g_ref)], sems)
 
         def chunk(p, carry):
             rows = pl.ds(pl.multiple_of(p * 16, 16), 16)
@@ -312,7 +356,10 @@
                 forward_radix(load, tw_ref, hi, lo, rows, half)
             return carry
 
-        lax.fori_loop(0, PLANES, chunk, 0)
+        for q in range(4):
+            copies[q].wait()
+            lax.fori_loop(q * 4, q * 4 + 4, chunk, 0)
+        copies[4].wait()
         for half in range(2):
 
             def load_holo(i):
@@ -320,7 +367,7 @@
 
             forward_radix(load_holo, tw_ref, hi, lo, slice(COLS, WITH_HOLO), half)
 
-    spec[...] = dot3(hi[k], lo[k], gh_ref[...], gl_ref[...], NN)
+    spec[...] = dot3(hi[k], lo[k], g_ref[0], g_ref[1], NN)
 
     for half in range(2):
         at = slice(half * 128, half * 128 + 128)
@@ -353,7 +400,7 @@
 
     c = tw_ref[k, 0:1, :]
     s = tw_ref[k, 1:2, :]
-    out = dot3(bhi[...], blo[...], ih_ref[...], il_ref[...], NN)
+    out = dot3(bhi[...], blo[...], g_ref[2], g_ref[3], NN)
     re, im = out[:, :PART], out[:, PART:]
     back[k, 0] = re * c + im * s
     back[k, 1] = im * c - re * s
@@ -362,39 +409,62 @@
     def _():
         square = sq_ref[...] + norm_ref[...] * (1.0 / PLANES)
         square = square[:8, :] + square[8:, :]
+        square = square + pltpu.roll(square, 64, 1)
+        lane = lax.broadcasted_iota(jnp.int32, (8, 128), 1)
+        square = jnp.where(lane < 64, 0.0, square)
 
         def chunk(p, carry):
             rows = pl.ds(pl.multiple_of(p * 16, 16), 16)
-            for i in range(RADIX):
-                o_ref[i, p, 64:MESSAGE, :] = square
             for half in range(2):
                 at = slice(half * 128, half * 128 + 128)
                 out = dft8([(back[i, 0, rows, at], back[i, 1, rows, at]) for i in range(RADIX)], 1)
                 for i in range(RADIX):
                     o_ref[i, p, half * 16 : half * 16 + 16, :] = out[i][0]
                     o_ref[i, p, half * 16 + 32 : half * 16 + 48, :] = out[i][1]
+            for i in range(RADIX):
+                tile = square
+                for high in range(2):
+                    for c in range(2):
+                        low_rows = slice(c * 32 + high * 8, c * 32 + high * 8 + 8)
+                        high_rows = slice(c * 32 + 16 + high * 8, c * 32 + 24 + high * 8)
+                        edge = jnp.where(
+                            lane < 2,
+                            o_ref[min(i + 1, RADIX - 1), p, low_rows, :],
+                            o_ref[max(i - 1, 0), p, high_rows, :],
+                        )
+                        base = high * 8 + c * 4
+                        edge = pltpu.roll(edge, base + 2, 1)
+                        tile = jnp.where((lane >= base) & (lane < base + 4), edge, tile)
+                o_ref[i, p, 64:MESSAGE, :] = tile
             return carry
 
-        lax.fori_loop(0, PLANES, chunk, 0)
-
-
-def spectral(z, holo, trans, squares, g_high, g_low, i_high, i_low, tw):
-    table = whole((2 * PART, 2 * PART))
+        sends = []
+        for q in range(4):
+            lax.fori_loop(q * 4, q * 4 + 4, chunk, 0)
+            sends.append(
+                pltpu.make_async_copy(
+                    o_ref.at[:, planes_of(q)], o_out.at[:, planes_of(q)], out_sems.at[q]
+                )
+            )
+            sends[-1].start()
+        for send in sends:
+            send.wait()
+
+
+def spectral(z, holo, trans, squares, table, tw):
+    anywhere = pl.BlockSpec(memory_space=pl.ANY)
     return pl.pallas_call(
         spectral_body,
         grid=(RADIX,),
         in_specs=[
-            whole((RADIX, PLANES, 2, 16, PART)),
+            anywhere,
             whole((RADIX, 16, 8, 128)),
             pl.BlockSpec((1, 2, COLS, PART), lambda k: (k, 0, 0, 0)),
             whole((16, 128)),
-            table,
-            table,
-            table,
-            table,
+            anywhere,
             whole((RADIX, 2, PART)),
         ],
-        out_specs=whole((RADIX, PLANES, MESSAGE, 128)),
+        out_specs=anywhere,
         out_shape=jax.ShapeDtypeStruct((RADIX, PLANES, MESSAGE, 128), F32),
         scratch_shapes=[
             pltpu.VMEM((16, 128), F32),
@@ -404,38 +474,73 @@
             pltpu.VMEM((COLS, 2 * PART), BF16),
             pltpu.VMEM((COLS, 2 * PART), BF16),
             pltpu.VMEM((RADIX, 2, COLS, PART), F32),
+            pltpu.VMEM((RADIX, PLANES, 2, 16, PART), F32),
+            pltpu.VMEM((4, 2 * PART, 2 * PART), BF16),
+            pltpu.VMEM((RADIX, PLANES, MESSAGE, 128), F32),
+            pltpu.SemaphoreType.DMA((5,)),
+            pltpu.SemaphoreType.DMA((4,)),
         ],
         compiler_params=params(62),
         cost_estimate=pl.CostEstimate(
             flops=8 * 10**9, bytes_accessed=14 * MIB, transcendentals=0
         ),
         name="spectral",
-    )(z, holo, trans, squares, g_high, g_low, i_high, i_low, tw)
+    )(z, holo, trans, squares, table, tw)
 
 
 def rows_back_body(
-    w_ref, x_ref, ih_ref, il_ref, tw_ref, re_ref, im_ref, top_ref, bot_ref, sum_ref, back
+    w_ref, x_in, xt_ref, xb_ref, ih_ref, il_ref, eh_ref, el_ref, tw_ref, re_out, im_out, sum_ref,
+    back, edge_back, x_ref, parts, x_sem, out_sems,
 ):
     k = pl.program_id(0)
+    fetch = pltpu.make_async_copy(x_in, x_ref, x_sem)
+
     @pl.when(k == 0)
     def _():
+        fetch.start()
         sum_ref[...] = jnp.zeros_like(sum_ref)
 
-    sum_ref[...] += jnp.sum(w_ref[0, :, 64:MESSAGE, :], axis=0)
-    parts = []
+    tiles = w_ref[0, :, 64:MESSAGE, :]
+    lane = lax.broadcasted_iota(jnp.int32, (8, 128), 1)
+    sum_ref[...] += jnp.where(lane < 64, 0.0, jnp.sum(tiles, axis=0))
+    turned = tiles.reshape(128, 128).T
+    edge = jnp.concatenate([turned[0:8, :], turned[8:16, :]], axis=1)
+    edge_high, edge_low = split(jnp.concatenate([edge, jnp.zeros_like(edge)], axis=0))
+    mixed = dot3(edge_high, edge_low, eh_ref[...], el_ref[...], NN)[0:8, :]
+    swapped = pltpu.roll(mixed, 4, 0)
+    edge_re = mixed[:, :PART] - swapped[:, PART:]
+    edge_im = mixed[:, PART:] + swapped[:, :PART]
+
+    halves = []
     for c in range(2):
-        halves = [w_ref[0, :, c * 32 + h * 16 : c * 32 + h * 16 + 16, :] for h in range(2)]
-        parts.append(jnp.concatenate([h.reshape(PART, 128).T for h in halves], axis=0))
-    high, low = split(jnp.concatenate(parts, axis=1))
+        for h in range(2):
+            rows = slice(c * 32 + h * 16, c * 32 + h * 16 + 16)
+            halves.append(w_ref[0, :, rows, :].reshape(PART, 128).T)
+    turned = [jnp.concatenate(halves[c * 2 : c * 2 + 2], axis=0) for c in range(2)]
+    high, low = split(jnp.concatenate(turned, axis=1))
     out = dot3(high, low, ih_ref[...], il_ref[...], NN)
     c = tw_ref[k, 0:1, :]
     s = tw_ref[k, 1:2, :]
     re, im = out[:, :PART], out[:, PART:]
     back[k, 0] = re * c + im * s
     back[k, 1] = im * c - re * s
+    edge_back[k, 0] = edge_re * c + edge_im * s
+    edge_back[k, 1] = edge_im * c - edge_re * s
 
     @pl.when(k == RADIX - 1)
     def _():
+        fetch.wait()
+        low_rows = lax.broadcasted_iota(jnp.int32, (8, 128), 0) < 4
+        for half in range(2):
+            at = slice(half * 128, half * 128 + 128)
+            out = dft8([(edge_back[i, 0, :, at], edge_back[i, 1, :, at]) for i in range(RADIX)], 1)
+            for i in range(RADIX):
+                to = slice(i * PART + half * 128, i * PART + half * 128 + 128)
+                for c in range(2):
+                    value = pltpu.roll(out[i][c], 6, 0)
+                    x = jnp.where(low_rows, xb_ref[c, 0, :, to], xt_ref[c, 0, :, to])
+                    parts[c, ROWS:PACK, to] = value + x
+
         def chunk(t, carry):
             rows = pl.ds(pl.multiple_of(t * 16, 16), 16)
             for half in range(2):
@@ -443,50 +548,63 @@
                 out = dft8([(back[i, 0, rows, at], back[i, 1, rows, at]) for i in range(RADIX)], 1)
                 for i in range(RADIX):
                     to = slice(i * PART + half * 128, i * PART + half * 128 + 128)
-                    re_ref[rows, to] = x_ref[0, 0, rows, to] + out[i][0]
-                    im_ref[rows, to] = x_ref[1, 0, rows, to] + out[i][1]
+                    for c in range(2):
+                        parts[c, rows, to] = x_ref[c, 0, rows, to] + out[i][c]
             return carry
 
-        lax.fori_loop(0, ROWS // 16, chunk, 0)
-        top_ref[0] = re_ref[0:8, :]
-        top_ref[1] = im_ref[0:8, :]
-        bot_ref[0] = re_ref[ROWS - 8 : ROWS, :]
-        bot_ref[1] = im_ref[ROWS - 8 : ROWS, :]
-
-
-def rows_back(w, x_now, i_high, i_low, tw):
+        sends = []
+        for q in range(4):
+            lax.fori_loop(q * 4, q * 4 + 4, chunk, 0)
+            span = pl.ds(q * 64, 72 if q == 3 else 64)
+            for c, target in enumerate((re_out, im_out)):
+                sends.append(
+                    pltpu.make_async_copy(
+                        parts.at[c, span, :], target.at[span, :], out_sems.at[c, q]
+                    )
+                )
+                sends[-1].start()
+        for send in sends:
+            send.wait()
+
+
+def rows_back(w, x_now, x_top, x_bottom, i_high, i_low, e_high, e_low, tw):
     table = whole((2 * PART, 2 * PART))
+    edge_table = whole((PART, 2 * PART))
+    anywhere = pl.BlockSpec(memory_space=pl.ANY)
     return pl.pallas_call(
         rows_back_body,
         grid=(RADIX,),
         in_specs=[
             pl.BlockSpec((1, 16, MESSAGE, 128), lambda k: (k, 0, 0, 0)),
-            whole((2, 1, ROWS, N)),
+            anywhere,
+            whole((2, 1, 8, N)),
+            whole((2, 1, 8, N)),
             table,
             table,
+            edge_table,
+            edge_table,
             whole((RADIX, 2, PART)),
         ],
-        out_specs=[
-            whole((ROWS, N)),
-            whole((ROWS, N)),
-            whole((2, 8, N)),
-            whole((2, 8, N)),
-            whole((8, 128)),
-        ],
+        out_specs=[anywhere, anywhere, whole((8, 128))],
         out_shape=[
-            jax.ShapeDtypeStruct((ROWS, N), F32),
-            jax.ShapeDtypeStruct((ROWS, N), F32),
-            jax.ShapeDtypeStruct((2, 8, N), F32),
-            jax.ShapeDtypeStruct((2, 8, N), F32),
+            jax.ShapeDtypeStruct((PACK, N), F32),
+            jax.ShapeDtypeStruct((PACK, N), F32),
             jax.ShapeDtypeStruct((8, 128), F32),
         ],
-        scratch_shapes=[pltpu.VMEM((RADIX, 2, ROWS, PART), F32)],
+        scratch_shapes=[
+            pltpu.VMEM((RADIX, 2, ROWS, PART), F32),
+            pltpu.VMEM((RADIX, 2, 8, PART), F32),
+            pltpu.VMEM((2, 1, ROWS, N), F32),
+            pltpu.VMEM((2, PACK, N), F32),
+            pltpu.SemaphoreType.DMA,
+            pltpu.SemaphoreType.DMA((2, 4)),
+        ],
         compiler_params=params(62),
         cost_estimate=pl.CostEstimate(
             flops=4 * 10**9, bytes_accessed=13 * MIB, transcendentals=0
         ),
         name="rows_back",
-    )(w, x_now, i_high, i_low, tw)
+    )(w, x_now, x_top, x_bottom, i_high, i_low, e_high, e_low, tw)
 
 
 TILES = EXT // 8
@@ -536,41 +654,44 @@
     return ref[lead + (rows, at)], after
 
 
+def arrivals(source, target, q, first, last, sems, edge_sems):
+    copies = [
+        pltpu.make_async_copy(
+            source.at[pl.ds(first, last - first), :],
+            target.at[pl.ds(first + 8, last - first), :],
+            sems.at[q],
+        )
+    ]
+    halo = source.at[pl.ds(ROWS, 8), :]
+    if q == 0:
+        copies.append(pltpu.make_async_copy(halo, target.at[pl.ds(0, 8), :], edge_sems.at[0]))
+    if q == STAGES - 1:
+        copies.append(
+            pltpu.make_async_copy(halo, target.at[pl.ds(ROWS + 8, 8), :], edge_sems.at[1])
+        )
+    return copies
+
+
 def tv_first_body(
-    comp, num_ref, at_ref, own, nxt, prv, own_h, nxt_h, prv_h, inner_out, dual_out,
-    ext, inner, dual, in_sems, halo_sems, out_sems,
+    num_ref, at_ref, own, nxt, prv, inner_out, dual_out,
+    ext, inner, dual, in_sems, edge_sems, out_sems,
 ):
     size = ROWS // STAGES
     mains = []
-    halos = []
-    for which, (main, halo) in enumerate(((own, own_h), (nxt, nxt_h), (prv, prv_h))):
-        mains.append(
-            [
-                pltpu.make_async_copy(
-                    main.at[pl.ds(q * size, size), :],
-                    ext.at[which, pl.ds(8 + q * size, size), :],
-                    in_sems.at[which, q],
-                )
-                for q in range(STAGES)
-            ]
-        )
-        halos.append(
-            [
-                pltpu.make_async_copy(
-                    halo.at[end, comp],
-                    ext.at[which, pl.ds(end * (ROWS + 8), 8), :],
-                    halo_sems.at[which, end],
-                )
-                for end in range(2)
-            ]
-        )
     for q in range(STAGES):
-        for which in range(3):
-            if q == 0:
-                halos[which][0].start()
-            mains[which][q].start()
-            if q == STAGES - 1:
-                halos[which][1].start()
+        mains.append([])
+        for which, main in enumerate((own, nxt, prv)):
+            mains[q] += arrivals(
+                main,
+                ext.at[which],
+                q,
+                q * size,
+                (q + 1) * size,
+                in_sems.at[which],
+                edge_sems.at[which],
+            )
+        for copy in mains[q]:
+            copy.start()
     scale = num_ref[0]
     inverse = num_ref[1]
     size_of = num_ref[5]
@@ -609,12 +730,8 @@
     outs = []
     done = 0
     for q in range(STAGES):
-        for which in range(3):
-            if q == 0:
-                halos[which][0].wait()
-            mains[which][q].wait()
-            if q == STAGES - 1:
-                halos[which][1].wait()
+        for copy in mains[q]:
+            copy.wait()
         if q == 0:
 
             @pl.when(band == 0)
@@ -643,9 +760,24 @@
             def _():
                 inner[ROWS + 8 : ROWS + 9, :] = inner[ROWS + 7 : ROWS + 8, :]
 
+            row = lax.broadcasted_iota(jnp.int32, (8, N), 0)
+            inner[0:8, :] = jnp.where(row < 4, inner[ROWS + 8 : EXT, :], inner[0:8, :])
+            outs.append(
+                pltpu.make_async_copy(
+                    inner.at[pl.ds(0, 8), :], inner_out.at[pl.ds(ROWS, 8), :], out_sems.at[2, 0]
+                )
+            )
+            outs[-1].start()
+
+        first = max(done, 1)
+        last = min(upto, TILES - 1)
         span = pl.ds(done * 8, (upto - done) * 8)
         outs += [
-            pltpu.make_async_copy(inner.at[span, :], inner_out.at[span, :], out_sems.at[0, q]),
+            pltpu.make_async_copy(
+                inner.at[pl.ds(first * 8, (last - first) * 8), :],
+                inner_out.at[pl.ds(first * 8 - 8, (last - first) * 8), :],
+                out_sems.at[0, q],
+            ),
             pltpu.make_async_copy(dual.at[:, span, :], dual_out.at[:, span, :], out_sems.at[1, q]),
         ]
         outs[-2].start()
@@ -655,15 +787,15 @@
         copy.wait()
 
 
-def tv_first(comp, numbers, place, own, nxt, prv, own_h, nxt_h, prv_h):
+def tv_first(numbers, place, own, nxt, prv):
     smem = pl.BlockSpec(memory_space=pltpu.SMEM)
     anywhere = pl.BlockSpec(memory_space=pl.ANY)
     return pl.pallas_call(
-        functools.partial(tv_first_body, comp),
-        in_specs=[smem, smem] + [anywhere] * 6,
+        tv_first_body,
+        in_specs=[smem, smem] + [anywhere] * 3,
         out_specs=[anywhere, anywhere],
         out_shape=[
-            jax.ShapeDtypeStruct((EXT, N), F32),
+            jax.ShapeDtypeStruct((PACK, N), F32),
             jax.ShapeDtypeStruct((4, EXT, N), F32),
         ],
         scratch_shapes=[
@@ -672,35 +804,40 @@
             pltpu.VMEM((4, EXT, N), F32),
             pltpu.SemaphoreType.DMA((3, STAGES)),
             pltpu.SemaphoreType.DMA((3, 2)),
-            pltpu.SemaphoreType.DMA((2, STAGES)),
+            pltpu.SemaphoreType.DMA((3, STAGES)),
         ],
         compiler_params=params(62),
         cost_estimate=pl.CostEstimate(
             flops=10**8, bytes_accessed=17 * MIB, transcendentals=2 * 10**6
         ),
         name="tv_first",
-    )(numbers, place, own, nxt, prv, own_h, nxt_h, prv_h)
+    )(numbers, place, own, nxt, prv)
 
 
 def tv_second_body(
     comp, num_ref, own_in, nxt_in, prv_in, dual_in, parts_in, x_prev_in, x_now_in, *rest
 ):
-    out_ref, inner, dual, plain, below, sems, out_sems = rest[-7:]
+    out_ref, inner, dual, plain, below, sems, edge_sems, out_sems = rest[-8:]
     size = ROWS // STAGES
     copies = []
     for q in range(STAGES):
         first = 0 if q == 0 else q * size + 16
         span = pl.ds(first, (q + 1) * size + 16 - first)
         main = pl.ds(q * size, size)
-        pairs = [(ref.at[span, :], inner.at[i, span, :]) for i, ref in enumerate((own_in, nxt_in, prv_in))]
-        pairs += [
+        begin = 0 if q == 0 else q * size + 8
+        end = min((q + 1) * size + 8, ROWS)
+        blocks = []
+        for i, ref in enumerate((own_in, nxt_in, prv_in)):
+            blocks += arrivals(ref, inner.at[i], q, begin, end, sems.at[i], edge_sems.at[i])
+        pairs = [
             (dual_in.at[:, span, :], dual.at[:, span, :]),
             (parts_in.at[main, :], plain.at[0, main, :]),
             (x_prev_in.at[comp, 0, main, :], plain.at[1, main, :]),
             (x_now_in.at[comp, 0, main, :], plain.at[2, main, :]),
         ]
         copies.append(
-            [pltpu.make_async_copy(a, b, sems.at[i, q]) for i, (a, b) in enumerate(pairs)]
+            blocks
+            + [pltpu.make_async_copy(a, b, sems.at[i + 3, q]) for i, (a, b) in enumerate(pairs)]
         )
         for copy in copies[-1]:
             copy.start()
@@ -786,6 +923,7 @@
             pltpu.VMEM((3, ROWS, N), F32),
             pltpu.VMEM((8, N), F32),
             pltpu.SemaphoreType.DMA((7, STAGES)),
+            pltpu.SemaphoreType.DMA((3, 2)),
             pltpu.SemaphoreType.DMA((STAGES,)),
         ],
         input_output_aliases=aliases,
@@ -803,10 +941,6 @@
     return lax.ppermute(x, axis, pairs)
 
 
-def tie(x, *after):
-    return lax.optimization_barrier((x,) + after)[0]
-
-
 def signed_freq(freq):
     signed = jnp.where(freq < N // 2, freq, freq - N)
     return signed.astype(F32) * (2.0 * math.pi / N)
@@ -824,6 +958,7 @@
     g_high, g_low = split_np(forward)
     i_high, i_low = split_np(inverse)
     p_high, p_low = split_np(inverse / PLANES)
+    e_high, e_low = split_np(halo_table(inverse / PLANES))
     t_high, t_low = split_np(forward.T)
     pick = np.stack([t_high, t_low]).reshape(2, 2, 16, 16, 2 * PART)
     pick = np.ascontiguousarray(pick.transpose(3, 0, 1, 2, 4)).reshape(16, 2, 32, 2 * PART)
@@ -842,25 +977,28 @@
     rate = phase_rate(signed_freq(kx)[None, :, None], signed_freq(ky)[:, None, :])
     trans = transfer(depth_all, rate)
 
-    sent, squares = rows_forward(x_now, jnp.asarray(t_high), jnp.asarray(t_low), tw)
+    sent, squares = rows_forward(x_now, jnp.asarray(np.stack([t_high, t_low])), tw)
     got = lax.all_to_all(sent.reshape(128, 2, 16, ROWS), both, 0, 0, tiled=True)
+    x_top = from_behind(x_now[:, :, ROWS - 8 :], "rows", 1)
+    x_bottom = from_behind(x_now[:, :, :8], "rows", -1)
     back = spectral(
         got.reshape(RADIX, PLANES, 2, 16, ROWS),
         holo.reshape(RADIX, PLANES, 8, 128),
         trans,
         squares,
-        jnp.asarray(g_high),
-        jnp.asarray(g_low),
-        jnp.asarray(i_high),
-        jnp.asarray(i_low),
+        jnp.asarray(np.stack([g_high, g_low, i_high, i_low])),
         tw,
     )
     ret = lax.all_to_all(back.reshape(128, MESSAGE, 128), both, 0, 0, tiled=True)
-    re, im, top, bot, sums = rows_back(
+    re, im, sums = rows_back(
         ret.reshape(RADIX, PLANES, MESSAGE, 128),
         x_now,
+        x_top,
+        x_bottom,
         jnp.asarray(p_high),
         jnp.asarray(p_low),
+        jnp.asarray(e_high),
+        jnp.asarray(e_low),
         tw,
     )
 
@@ -879,30 +1017,19 @@
     )
     place = jnp.stack([r])
 
-    halo = jnp.stack([from_behind(bot, "rows", 1), from_behind(top, "rows", -1)])
-    own = [re, im]
-    nxt = [from_behind(re, "depth", -1)]
-    prv = [from_behind(re, "depth", 1)]
-    halo_next = from_behind(halo, "depth", -1)
-    halo_prev = from_behind(halo, "depth", 1)
-    own[1] = tie(im, nxt[0], prv[0], halo_next, halo_prev)
-    nxt.append(from_behind(own[1], "depth", -1))
-    prv.append(from_behind(own[1], "depth", 1))
-
-    inner_re, dual_re = tv_first(0, numbers, place, re, nxt[0], prv[0], halo, halo_next, halo_prev)
-    nxt_re = from_behind(inner_re, "depth", -1)
-    prv_re = from_behind(inner_re, "depth", 1)
-    inner_im, dual_im = tv_first(
-        1, numbers, place, own[1], nxt[1], prv[1], halo, halo_next, halo_prev
-    )
-    nxt_im = from_behind(inner_im, "depth", -1)
-    prv_im = from_behind(inner_im, "depth", 1)
-    out = tv_second(
-        0, numbers, inner_re, nxt_re, prv_re, dual_re, re, x_prev, x_now, None
-    )
-    return tv_second(
-        1, numbers, inner_im, nxt_im, prv_im, dual_im, own[1], x_prev, x_now, out
-    )
+    own = (re, im)
+    nxt = [from_behind(part, "depth", -1) for part in own]
+    prv = [from_behind(part, "depth", 1) for part in own]
+    out = None
+    firsts = [tv_first(numbers, place, own[c], nxt[c], prv[c]) for c in range(2)]
+    ahead = [from_behind(inner, "depth", -1) for inner, _ in firsts]
+    behind = [from_behind(inner, "depth", 1) for inner, _ in firsts]
+    for c in range(2):
+        inner, dual = firsts[c]
+        out = tv_second(
+            c, numbers, inner, ahead[c], behind[c], dual, own[c], x_prev, x_now, out
+        )
+    return out
 
 
 def solution(mesh):

time: 321 us -> 307 us (0.956)
  blocking collectives: 66.8 us -> 0 us
  waiting for transfers between devices: 93.3 us -> 141 us
  starting transfers between devices: 50.7 us -> 54 us
    all_to_all x1 -> x0, blocking collectives: 66.8 us -> none  [shards(): lax.all_to_all(back.reshape(128, MESSAGE, 128), both, 0, 0, tiled=True)]
    ppermute x12 -> x10, waiting for transfers between devices: 48.4 us -> 94.7 us  [from_behind(): return lax.ppermute(x, axis, pairs)]
    all_to_all x0 -> x1, starting transfers between devices: none -> 8.81 us  [shards(): lax.all_to_all(back.reshape(128, MESSAGE, 128), both, 0, 0, tiled=True)]
    ppermute x12 -> x10, starting transfers between devices: 32.9 us -> 27.8 us  [from_behind(): return lax.ppermute(x, axis, pairs)]
  transfers between devices with their start and end apart: 14 -> 13, of which waited for: 11 -> 13; matrix products, arithmetic and copies ran while one was open for 1% -> 1% of each run, Pallas kernels for 16% -> 17%
where the time goes in v3:
time: 307 us; the launch traced here: 304 us
  waiting for transfers between devices  141 us (46%)
  Pallas kernels  101 us (33%)
  starting transfers between devices  54 us (18%)
  local copies, waits for them, and re-layouts  3.84 us (1%)
    ppermute x10, waiting for transfers between devices, from_behind(): return lax.ppermute(x, axis, pairs)  94.7 us
    all_to_all x1, waiting for transfers between devices, shards(): got = lax.all_to_all(sent.reshape(128, 2, 16, ROWS), both, 0, 0, tiled=True)  42.3 us
    ppermute x10, starting transfers between devices, from_behind(): return lax.ppermute(x, axis, pairs)  27.8 us
    pallas_call x2, Pallas kernels, tv_first(): pl.pallas_call(tv_first_body, in_specs=[smem, smem] + [anywhere] * 3, out...  22.8 us
    pallas_call x2, Pallas kernels, tv_second(): pl.pallas_call(functools.partial(tv_second_body, comp), in_specs=[smem] +...  22.7 us
    pallas_call x1, Pallas kernels, spectral(): pl.pallas_call(spectral_body, grid=(RADIX,), in_specs=[anywhere, whole((R...  19.8 us
    pallas_call x1, Pallas kernels, rows_back(): pl.pallas_call(rows_back_body, grid=(RADIX,), in_specs=[pl.BlockSpec((1,...  12.2 us
    all_to_all x1, starting transfers between devices, shards(): holo = lax.all_to_all(holo.reshape(128, 8, 128), both, 0, 0, tiled=True)  10.2 us
  transfers between devices with their start and end apart: 13, of which 13 were waited for; matrix products, arithmetic and copies ran while one was open for 1% of the time, Pallas kernels for 17%

profile of v3, /device:TPU:32, one launch (start us, length us, event | category | flops | bytes accessed | tf_op | source)
XLA Modules:
  0.0 303.8 jit_solution(16375588775355861311)
XLA Ops:
  0.7 1.4 dynamic-slice_bitcast_fusion
  2.1 7.3 %holo_forward.1 = f32[8,16,8,128]{3,2,1,0:T(8,128)} custom-call(f32[1]{0:T(128)S(6)} %copy.17.depth_ref, f32[2,256,2048]{2,1,0:T(8,128)} %x_in.4, bf16[32,512]{1,0:T(8,128)(2,1)} %get-tuple-element.26.gh_ref, bf16[32,512]{1,0:T(8,128)(2,1)} %get-tuple-element.25.gl_ref, f32[8,2,256]{2,1,0:T(2,128)} %constant.68.clone.tw_ref), custom_call_target="tpu_custom_call" | custom-call | flops 400000000 | bytes 5242880 | tf_op jit(solution)/shard_map/holo_forward/pallas_call | solution.py:252
  9.4 10.2 %all-to-all-start.1 = ((f32[128,8,128]{2,1,0:T(8,128)}), f32[128,8,128]{2,1,0:T(8,128)S(1)}, u32[]{:S(2)}, u32[]{:S(2)}) async-start(f32[128,8,128]{2,1,0:T(8,128)} %bitcast.20), calls=%async_computation.1 | async-start | bytes 1048576 | tf_op jit(solution)/shard_map/all_to_all | solution.py:970
  19.6 10.1 %rows_forward.1 = (f32[8,16,2,16,256]{4,3,2,1,0:T(8,128)}, f32[16,128]{1,0:T(8,128)}) custom-call(f32[2,1,256,2048]{3,2,1,0:T(8,128)} %x_now_in.3, bf16[2,512,512]{2,1,0:T(8,128)(2,1)} %constant.70.clone.g_in, f32[8,2,256]{2,1,0:T(2,128)} %constant.68.clone.tw_ref), custom_call_target="tpu_custom_call" | custom-call | flops 4000000000 | bytes 10485760 | tf_op jit(solution)/shard_map/rows_forward/pallas_call | solution.py:188
  29.8 3.1 %all-to-all-done.1 = f32[128,8,128]{2,1,0:T(8,128)S(1)} async-done(((f32[128,8,128]{2,1,0:T(8,128)}), f32[128,8,128]{2,1,0:T(8,128)S(1)}, u32[]{:S(2)}, u32[]{:S(2)}) %all-to-all-start.1) | async-done | bytes 524320 | tf_op jit(solution)/shard_map/all_to_all | solution.py:970
  32.9 0.0 copy-start
  32.9 7.2 %all-to-all-start = ((f32[128,2,16,256]{3,2,1,0:T(8,128)}), f32[128,2,16,256]{3,2,1,0:T(8,128)}, u32[]{:S(2)}, u32[]{:S(2)}) async-start(f32[128,2,16,256]{3,2,1,0:T(8,128)} %bitcast.19), calls=%async_computation | async-start | bytes 8388608 | tf_op jit(solution)/shard_map/all_to_all | solution.py:981
  40.1 0.8 fusion.rate_ref
  40.9 0.0 copy-done
  40.9 0.8 slice_reduce_fusion
  41.6 6.3 %transfer.1.t_ref = f32[8,2,256,256]{3,2,1,0:T(8,128)} custom-call(f32[1,16]{1,0:T(1,128)} %bitcast.22, f32[8,16,256]{2,1,0:T(8,128)} %fusion.rate_ref), custom_call_target="tpu_custom_call" | custom-call | flops 10000000 | bytes 4194304 | tf_op jit(solution)/shard_map/transfer/pallas_call | solution.py:310
  47.9 42.3 %all-to-all-done = f32[128,2,16,256]{3,2,1,0:T(8,128)} async-done(((f32[128,2,16,256]{3,2,1,0:T(8,128)}), f32[128,2,16,256]{3,2,1,0:T(8,128)}, u32[]{:S(2)}, u32[]{:S(2)}) %all-to-all-start) | async-done | bytes 4194336 | tf_op jit(solution)/shard_map/all_to_all | solution.py:981
  90.2 19.8 %spectral.1 = f32[8,16,72,128]{3,2,1,0:T(8,128)} custom-call(f32[8,16,2,16,256]{4,3,2,1,0:T(8,128)} %bitcast.1.z_in, f32[8,16,8,128]{3,2,1,0:T(8,128)} %bitcast.21, f32[8,2,256,256]{3,2,1,0:T(8,128)} %transfer.1.t_ref, f32[16,128]{1,0:T(8,128)} %get-tuple-element.15.sq_ref, bf16[4,512,512]{2,1,0:T(8,128)(2,1)} %constant.71.clone.g_in, ...), custom_call_target="tpu_custom_call" | custom-call | flops 8000000000 | bytes 14680064 | tf_op jit(solution)/shard_map/spectral/pallas_call | solution.py:456
  110.0 8.8 %all-to-all-start.2 = ((f32[128,72,128]{2,1,0:T(8,128)}), f32[128,72,128]{2,1,0:T(8,128)}, u32[]{:S(2)}, u32[]{:S(2)}) async-start(f32[128,72,128]{2,1,0:T(8,128)} %bitcast.18), calls=%async_computation.2 | async-start | bytes 9437184 | tf_op jit(solution)/shard_map/all_to_all | solution.py:992
  118.8 1.0 fusion.9
  119.8 3.4 %collective-permute-start = (f32[2,1,8,2048]{3,2,1,0:T(8,128)S(1)}, f32[2,1,8,2048]{3,2,1,0:T(8,128)S(1)}, u32[]{:S(2)}, u32[]{:S(2)}) collective-permute-start(f32[2,1,8,2048]{3,2,1,0:T(8,128)S(1)} %get-tuple-element.24), channel_id=1, source_target_pairs={{0,1},{1,2},{2,3},{3,4},{4,5},{5,6},{6,7},{8,9},{9,10},{10,11},{11... | collective-permute-start | bytes 393224 | tf_op jit(solution)/shard_map/ppermute | solution.py:941
  123.2 1.3 collective-permute-start.1
  124.5 47.4 %collective-permute-done.xt_ref = f32[2,1,8,2048]{3,2,1,0:T(8,128)S(1)} collective-permute-done((f32[2,1,8,2048]{3,2,1,0:T(8,128)S(1)}, f32[2,1,8,2048]{3,2,1,0:T(8,128)S(1)}, u32[]{:S(2)}, u32[]{:S(2)}) %collective-permute-start) | collective-permute-done | bytes 131104 | tf_op jit(solution)/shard_map/ppermute | solution.py:941
  171.9 0.0 copy-start.1
  171.9 2.6 collective-permute-done.1.xb_ref
  174.5 0.0 copy-start.2
  174.5 0.9 all-to-all-done.2
  175.4 0.0 copy-done.1
  175.4 0.0 copy-done.2
  175.4 12.2 %rows_back.1 = (f32[264,2048]{1,0:T(8,128)}, f32[264,2048]{1,0:T(8,128)}, f32[8,128]{1,0:T(8,128)}) custom-call(f32[8,16,72,128]{3,2,1,0:T(8,128)} %bitcast.7.w_ref, f32[2,1,256,2048]{3,2,1,0:T(8,128)} %x_now_in.3, f32[2,1,8,2048]{3,2,1,0:T(8,128)} %copy-done.1, f32[2,1,8,2048]{3,2,1,0:T(8,128)} %copy-done.2, bf16[512,512]{1,0:T(8,128)(2,1)} %constant.72.clone.ih_ref, ...), custom_call_target="tpu_custom_call" | custom-call | flops 4000000000 | bytes 13631488 | tf_op jit(solution)/shard_map/rows_back/pallas_call | solution.py:574
  187.7 4.8 %collective-permute-start.6 = (f32[264,2048]{1,0:T(8,128)}, f32[264,2048]{1,0:T(8,128)}, u32[]{:S(2)}, u32[]{:S(2)}) collective-permute-start(f32[264,2048]{1,0:T(8,128)} %get-tuple-element.20.own.parts_in), channel_id=1, source_target_pairs={{8,0},{16,8},{24,16},{32,24},{40,32},{48,40},{56,48},{64,56},{72,6... | collective-permute-start | bytes 6488072 | tf_op jit(solution)/shard_map/ppermute | solution.py:941
  192.5 1.9 collective-permute-start.7
  194.4 5.8 %collective-permute-start.2 = (f32[264,2048]{1,0:T(8,128)}, f32[264,2048]{1,0:T(8,128)}, u32[]{:S(2)}, u32[]{:S(2)}) collective-permute-start(f32[264,2048]{1,0:T(8,128)} %get-tuple-element.17.own.parts_in), channel_id=1, source_target_pairs={{8,0},{16,8},{24,16},{32,24},{40,32},{48,40},{56,48},{64,56},{72,6... | collective-permute-start | bytes 6488072 | tf_op jit(solution)/shard_map/ppermute | solution.py:941
  200.2 1.9 collective-permute-start.3
  202.1 1.3 reduce_sum.9
  204.2 0.7 stack.38.num_ref
  204.9 12.1 %collective-permute-done.6.nxt = f32[264,2048]{1,0:T(8,128)} collective-permute-done((f32[264,2048]{1,0:T(8,128)}, f32[264,2048]{1,0:T(8,128)}, u32[]{:S(2)}, u32[]{:S(2)}) %collective-permute-start.6) | collective-permute-done | bytes 2162720 | tf_op jit(solution)/shard_map/ppermute | solution.py:941
  217.0 5.9 %collective-permute-done.7.prv = f32[264,2048]{1,0:T(8,128)} collective-permute-done((f32[264,2048]{1,0:T(8,128)}, f32[264,2048]{1,0:T(8,128)}, u32[]{:S(2)}, u32[]{:S(2)}) %collective-permute-start.7) | collective-permute-done | bytes 2162720 | tf_op jit(solution)/shard_map/ppermute | solution.py:941
  223.0 11.4 %tv_first.3 = (f32[264,2048]{1,0:T(8,128)}, f32[4,272,2048]{2,1,0:T(8,128)}) custom-call(f32[6]{0:T(128)} %stack.38.num_ref, s32[1]{0:T(128)} %bitcast.14.at_ref, f32[264,2048]{1,0:T(8,128)} %get-tuple-element.20.own.parts_in, f32[264,2048]{1,0:T(8,128)} %collective-permute-done.6.nxt, f32[264,2048]{1,0:T(8,128)} %collective-permute-done.7.prv), custom_call_target="tpu_custom_call" | custom-call | flops 100000000 | bytes 17825792 | tf_op jit(solution)/shard_map/tv_first/pallas_call | solution.py:793
  234.4 1.9 collective-permute-start.8
  236.3 2.4 collective-permute-start.9
  238.7 1.5 collective-permute-done.2.nxt
  240.2 5.9 %collective-permute-done.3.prv = f32[264,2048]{1,0:T(8,128)} collective-permute-done((f32[264,2048]{1,0:T(8,128)}, f32[264,2048]{1,0:T(8,128)}, u32[]{:S(2)}, u32[]{:S(2)}) %collective-permute-start.3) | collective-permute-done | bytes 2162720 | tf_op jit(solution)/shard_map/ppermute | solution.py:941
  246.1 11.4 %tv_first.2 = (f32[264,2048]{1,0:T(8,128)}, f32[4,272,2048]{2,1,0:T(8,128)}) custom-call(f32[6]{0:T(128)} %stack.38.num_ref, s32[1]{0:T(128)} %bitcast.14.at_ref, f32[264,2048]{1,0:T(8,128)} %get-tuple-element.17.own.parts_in, f32[264,2048]{1,0:T(8,128)} %collective-permute-done.2.nxt, f32[264,2048]{1,0:T(8,128)} %collective-permute-done.3.prv), custom_call_target="tpu_custom_call" | custom-call | flops 100000000 | bytes 17825792 | tf_op jit(solution)/shard_map/tv_first/pallas_call | solution.py:793
  257.5 1.9 collective-permute-start.4
  259.5 2.4 collective-permute-start.5
  261.9 1.5 collective-permute-done.8.nxt_in
  263.4 5.9 %collective-permute-done.9.prv_in = f32[264,2048]{1,0:T(8,128)} collective-permute-done((f32[264,2048]{1,0:T(8,128)}, f32[264,2048]{1,0:T(8,128)}, u32[]{:S(2)}, u32[]{:S(2)}) %collective-permute-start.9) | collective-permute-done | bytes 2162720 | tf_op jit(solution)/shard_map/ppermute | solution.py:941
  269.3 11.4 %tv_second.2.rest_0_ = f32[2,1,256,2048]{3,2,1,0:T(8,128)} custom-call(f32[6]{0:T(128)} %stack.38.num_ref, f32[264,2048]{1,0:T(8,128)} %get-tuple-element.21.own_in, f32[264,2048]{1,0:T(8,128)} %collective-permute-done.8.nxt_in, f32[264,2048]{1,0:T(8,128)} %collective-permute-done.9.prv_in, f32[4,272,2048]{2,1,0:T(8,128)} %get-tuple-element.22.dual_in, ...), custom_call_target="tpu_custom_call" | custom-call | flops 100000000 | bytes 24117248 | tf_op jit(solution)/shard_map/tv_second/pallas_call | solution.py:915
  280.7 5.9 %collective-permute-done.4.nxt_in = f32[264,2048]{1,0:T(8,128)} collective-permute-done((f32[264,2048]{1,0:T(8,128)}, f32[264,2048]{1,0:T(8,128)}, u32[]{:S(2)}, u32[]{:S(2)}) %collective-permute-start.4) | collective-permute-done | bytes 2162720 | tf_op jit(solution)/shard_map/ppermute | solution.py:941
  286.5 5.9 %collective-permute-done.5.prv_in = f32[264,2048]{1,0:T(8,128)} collective-permute-done((f32[264,2048]{1,0:T(8,128)}, f32[264,2048]{1,0:T(8,128)}, u32[]{:S(2)}, u32[]{:S(2)}) %collective-permute-start.5) | collective-permute-done | bytes 2162720 | tf_op jit(solution)/shard_map/ppermute | solution.py:941
  292.5 11.4 %tv_second.3 = f32[2,1,256,2048]{3,2,1,0:T(8,128)} custom-call(f32[6]{0:T(128)} %stack.38.num_ref, f32[264,2048]{1,0:T(8,128)} %get-tuple-element.18.own_in, f32[264,2048]{1,0:T(8,128)} %collective-permute-done.4.nxt_in, f32[264,2048]{1,0:T(8,128)} %collective-permute-done.5.prv_in, ...), custom_call_target="tpu_custom_call", output_to_operand_aliasing={{}: (8, {})} | custom-call | flops 100000000 | bytes 24117248 | tf_op jit(solution)/shard_map/tv_second/pallas_call | solution.py:915
  (3 shorter events, 0.0 us)
Async XLA Ops:
  9.4 23.5 %all-to-all-start.1 = ((f32[128,8,128]{2,1,0:T(8,128)}), f32[128,8,128]{2,1,0:T(8,128)S(1)}, u32[]{:S(2)}, u32[]{:S(2)}) async-start(f32[128,8,128]{2,1,0:T(8,128)} %bitcast.20), calls=%async_computation.1 | async-start | bytes 1048576 | tf_op jit(solution)/shard_map/all_to_all | solution.py:970
  32.9 8.0 %copy-start = (f32[128,8,128]{2,1,0:T(8,128)}, f32[128,8,128]{2,1,0:T(8,128)S(1)}, u32[]{:S(2)}) copy-start(f32[128,8,128]{2,1,0:T(8,128)S(1)} %all-to-all-done.1) | copy-start | bytes 1572868
  32.9 57.3 %all-to-all-start = ((f32[128,2,16,256]{3,2,1,0:T(8,128)}), f32[128,2,16,256]{3,2,1,0:T(8,128)}, u32[]{:S(2)}, u32[]{:S(2)}) async-start(f32[128,2,16,256]{3,2,1,0:T(8,128)} %bitcast.19), calls=%async_computation | async-start | bytes 8388608 | tf_op jit(solution)/shard_map/all_to_all | solution.py:981
  110.0 65.5 %all-to-all-start.2 = ((f32[128,72,128]{2,1,0:T(8,128)}), f32[128,72,128]{2,1,0:T(8,128)}, u32[]{:S(2)}, u32[]{:S(2)}) async-start(f32[128,72,128]{2,1,0:T(8,128)} %bitcast.18), calls=%async_computation.2 | async-start | bytes 9437184 | tf_op jit(solution)/shard_map/all_to_all | solution.py:992
  119.8 52.1 %collective-permute-start = (f32[2,1,8,2048]{3,2,1,0:T(8,128)S(1)}, f32[2,1,8,2048]{3,2,1,0:T(8,128)S(1)}, u32[]{:S(2)}, u32[]{:S(2)}) collective-permute-start(f32[2,1,8,2048]{3,2,1,0:T(8,128)S(1)} %get-tuple-element.24), channel_id=1, source_target_pairs={{0,1},{1,2},{2,3},{3,4},{4,5},{5,6},{6,7},{8,9},{9,10},{10,11},{11... | collective-permute-start | bytes 393224 | tf_op jit(solution)/shard_map/ppermute | solution.py:941
  123.2 51.3 %collective-permute-start.1 = (f32[2,1,8,2048]{3,2,1,0:T(8,128)S(1)}, f32[2,1,8,2048]{3,2,1,0:T(8,128)S(1)}, u32[]{:S(2)}, u32[]{:S(2)}) collective-permute-start(f32[2,1,8,2048]{3,2,1,0:T(8,128)S(1)} %get-tuple-element.23), channel_id=1, source_target_pairs={{1,0},{2,1},{3,2},{4,3},{5,4},{6,5},{7,6},{9,8},{10,9},{11,10},{12... | collective-permute-start | bytes 393224 | tf_op jit(solution)/shard_map/ppermute | solution.py:941
  171.9 3.5 %copy-start.1 = (f32[2,1,8,2048]{3,2,1,0:T(8,128)}, f32[2,1,8,2048]{3,2,1,0:T(8,128)S(1)}, u32[]{:S(2)}) copy-start(f32[2,1,8,2048]{3,2,1,0:T(8,128)S(1)} %collective-permute-done.xt_ref) | copy-start | bytes 393220
  174.5 1.0 copy-start.2
  187.7 29.3 %collective-permute-start.6 = (f32[264,2048]{1,0:T(8,128)}, f32[264,2048]{1,0:T(8,128)}, u32[]{:S(2)}, u32[]{:S(2)}) collective-permute-start(f32[264,2048]{1,0:T(8,128)} %get-tuple-element.20.own.parts_in), channel_id=1, source_target_pairs={{8,0},{16,8},{24,16},{32,24},{40,32},{48,40},{56,48},{64,56},{72,6... | collective-permute-start | bytes 6488072 | tf_op jit(solution)/shard_map/ppermute | solution.py:941
  192.5 30.5 %collective-permute-start.7 = (f32[264,2048]{1,0:T(8,128)}, f32[264,2048]{1,0:T(8,128)}, u32[]{:S(2)}, u32[]{:S(2)}) collective-permute-start(f32[264,2048]{1,0:T(8,128)} %get-tuple-element.20.own.parts_in), channel_id=1, source_target_pairs={{0,8},{8,16},{16,24},{24,32},{32,40},{40,48},{48,56},{56,64},{64,7... | collective-permute-start | bytes 6488072 | tf_op jit(solution)/shard_map/ppermute | solution.py:941
  194.4 45.8 %collective-permute-start.2 = (f32[264,2048]{1,0:T(8,128)}, f32[264,2048]{1,0:T(8,128)}, u32[]{:S(2)}, u32[]{:S(2)}) collective-permute-start(f32[264,2048]{1,0:T(8,128)} %get-tuple-element.17.own.parts_in), channel_id=1, source_target_pairs={{8,0},{16,8},{24,16},{32,24},{40,32},{48,40},{56,48},{64,56},{72,6... | collective-permute-start | bytes 6488072 | tf_op jit(solution)/shard_map/ppermute | solution.py:941
  200.2 46.0 %collective-permute-start.3 = (f32[264,2048]{1,0:T(8,128)}, f32[264,2048]{1,0:T(8,128)}, u32[]{:S(2)}, u32[]{:S(2)}) collective-permute-start(f32[264,2048]{1,0:T(8,128)} %get-tuple-element.17.own.parts_in), channel_id=1, source_target_pairs={{0,8},{8,16},{16,24},{24,32},{32,40},{40,48},{48,56},{56,64},{64,7... | collective-permute-start | bytes 6488072 | tf_op jit(solution)/shard_map/ppermute | solution.py:941
  234.4 29.0 %collective-permute-start.8 = (f32[264,2048]{1,0:T(8,128)}, f32[264,2048]{1,0:T(8,128)}, u32[]{:S(2)}, u32[]{:S(2)}) collective-permute-start(f32[264,2048]{1,0:T(8,128)} %get-tuple-element.21.own_in), channel_id=1, source_target_pairs={{8,0},{16,8},{24,16},{32,24},{40,32},{48,40},{56,48},{64,56},{72,6... | collective-permute-start | bytes 6488072 | tf_op jit(solution)/shard_map/ppermute | solution.py:941
  236.3 33.0 %collective-permute-start.9 = (f32[264,2048]{1,0:T(8,128)}, f32[264,2048]{1,0:T(8,128)}, u32[]{:S(2)}, u32[]{:S(2)}) collective-permute-start(f32[264,2048]{1,0:T(8,128)} %get-tuple-element.21.own_in), channel_id=1, source_target_pairs={{0,8},{8,16},{16,24},{24,32},{32,40},{40,48},{48,56},{56,64},{64,7... | collective-permute-start | bytes 6488072 | tf_op jit(solution)/shard_map/ppermute | solution.py:941
  257.5 29.0 %collective-permute-start.4 = (f32[264,2048]{1,0:T(8,128)}, f32[264,2048]{1,0:T(8,128)}, u32[]{:S(2)}, u32[]{:S(2)}) collective-permute-start(f32[264,2048]{1,0:T(8,128)} %get-tuple-element.18.own_in), channel_id=1, source_target_pairs={{8,0},{16,8},{24,16},{32,24},{40,32},{48,40},{56,48},{64,56},{72,6... | collective-permute-start | bytes 6488072 | tf_op jit(solution)/shard_map/ppermute | solution.py:941
  259.5 33.0 %collective-permute-start.5 = (f32[264,2048]{1,0:T(8,128)}, f32[264,2048]{1,0:T(8,128)}, u32[]{:S(2)}, u32[]{:S(2)}) collective-permute-start(f32[264,2048]{1,0:T(8,128)} %get-tuple-element.18.own_in), channel_id=1, source_target_pairs={{0,8},{8,16},{16,24},{24,32},{32,40},{40,48},{48,56},{56,64},{64,7... | collective-permute-start | bytes 6488072 | tf_op jit(solution)/shard_map/ppermute | solution.py:941

commit v4 on v3

--- a/solution.py
+++ b/solution.py
@@ -24,6 +24,7 @@
 PART = 256
 EXT = ROWS + 16
 PACK = ROWS + 8
+HALF = ROWS // 2
 F32 = jnp.float32
 BF16 = jnp.bfloat16
 MIB = 1024 * 1024
@@ -146,57 +147,58 @@
     return pl.ds(q * (ROWS // 4), ROWS // 4)
 
 
-def rows_body(x_in, g_in, tw_ref, y_ref, ss_ref, hi, lo, x_ref, g_ref, sems):
-    k = pl.program_id(0)
-
-    @pl.when(k == 0)
-    def _():
-        pairs = [(x_in.at[:, :, quarter(q), :], x_ref.at[:, :, quarter(q), :]) for q in range(4)]
-        copies = stage_copies(pairs + [(g_in, g_ref)], sems)
-
-        def chunk(t, total):
-            rows = pl.ds(pl.multiple_of(t * 16, 16), 16)
-            for half in range(2):
-
-                def load(i):
-                    at = slice(i * PART + half * 128, i * PART + half * 128 + 128)
-                    return (x_ref[0, 0, rows, at], x_ref[1, 0, rows, at])
-
-                patches = [load(i) for i in range(RADIX)]
-                for re, im in patches:
-                    total = total + (re * re + im * im)
-                forward_radix(lambda i: patches[i], tw_ref, hi, lo, rows, half)
-            return total
-
-        total = jnp.zeros((16, 128), F32)
-        for q in range(4):
-            copies[q].wait()
-            total = lax.fori_loop(q * 4, q * 4 + 4, chunk, total)
-        ss_ref[...] = total
-        copies[4].wait()
-
-    gh, gl = g_ref.at[0], g_ref.at[1]
-    high, low = hi[k], lo[k]
-    for part in range(2):
-        at = slice(part * PART, part * PART + PART)
-        out = dot3(gh[at, :], gl[at, :], high, low, NT)
-        y_ref[0, :, part] = out.reshape(16, 16, ROWS)
+def rows_body(x_in, g_in, tw_ref, y_out, ss_ref, hi, lo, x_ref, g_ref, y_ref, sems, out_sems):
+    pairs = [(x_in.at[:, :, quarter(q), :], x_ref.at[:, :, quarter(q), :]) for q in range(4)]
+    copies = stage_copies(pairs + [(g_in, g_ref)], sems)
+
+    def chunk(t, total):
+        rows = pl.ds(pl.multiple_of(t * 16, 16), 16)
+        for half in range(2):
+
+            def load(i):
+                at = slice(i * PART + half * 128, i * PART + half * 128 + 128)
+                return (x_ref[0, 0, rows, at], x_ref[1, 0, rows, at])
+
+            patches = [load(i) for i in range(RADIX)]
+            for re, im in patches:
+                total = total + (re * re + im * im)
+            forward_radix(lambda i: patches[i], tw_ref, hi, lo, rows, half)
+        return total
+
+    total = jnp.zeros((16, 128), F32)
+    for q in range(4):
+        copies[q].wait()
+        total = lax.fori_loop(q * 4, q * 4 + 4, chunk, total)
+    ss_ref[...] = total
+    copies[4].wait()
+
+    def send(k):
+        return pltpu.make_async_copy(y_ref.at[k], y_out.at[k], out_sems.at[k])
+
+    def per_k(k, carry):
+        high, low = hi[k], lo[k]
+        for part in range(2):
+            at = slice(part * PART, part * PART + PART)
+            out = dot3(g_ref[0, at, :], g_ref[1, at, :], high, low, NT)
+            y_ref[k, :, part] = out.reshape(16, 16, ROWS)
+        send(k).start()
+        return carry
+
+    def finish(k, carry):
+        send(k).wait()
+        return carry
+
+    lax.fori_loop(0, RADIX, per_k, 0)
+    lax.fori_loop(0, RADIX, finish, 0)
 
 
 def rows_forward(x_now, table, tw):
     anywhere = pl.BlockSpec(memory_space=pl.ANY)
+    vmem = pl.BlockSpec(memory_space=pltpu.VMEM)
     return pl.pallas_call(
         rows_body,
-        grid=(RADIX,),
-        in_specs=[
-            anywhere,
-            anywhere,
-            whole((RADIX, 2, PART)),
-        ],
-        out_specs=[
-            pl.BlockSpec((1, 16, 2, 16, ROWS), lambda k: (k, 0, 0, 0, 0)),
-            whole((16, 128)),
-        ],
+        in_specs=[anywhere, anywhere, vmem],
+        out_specs=[anywhere, vmem],
         out_shape=[
             jax.ShapeDtypeStruct((RADIX, 16, 2, 16, ROWS), F32),
             jax.ShapeDtypeStruct((16, 128), F32),
@@ -206,7 +208,9 @@
             pltpu.VMEM((RADIX, ROWS, 2 * PART), BF16),
             pltpu.VMEM((2, 1, ROWS, N), F32),
             pltpu.VMEM((2, 2 * PART, 2 * PART), BF16),
+            pltpu.VMEM((RADIX, 16, 2, 16, ROWS), F32),
             pltpu.SemaphoreType.DMA((5,)),
+            pltpu.SemaphoreType.DMA((RADIX,)),
         ],
         compiler_params=params(62),
         cost_estimate=pl.CostEstimate(
@@ -334,136 +338,138 @@
 
 
 def spectral_body(
-    z_in, h_ref, t_ref, sq_ref, g_in, tw_ref, o_out, norm_ref,
-    hi, lo, spec, bhi, blo, back, z_ref, g_ref, o_ref, sems, out_sems,
+    z_in, h_in, t_in, sq_ref, g_in, tw_ref, o_out, norm_ref,
+    hi, lo, spec, bhi, blo, back, z_ref, g_ref, o_ref, h_ref, t_ref, sems, out_sems, t_sems,
 ):
-    k = pl.program_id(0)
-
-    @pl.when(k == 0)
-    def _():
-        norm_ref[...] = jnp.zeros_like(norm_ref)
-        pairs = [(z_in.at[:, planes_of(q)], z_ref.at[:, planes_of(q)]) for q in range(4)]
-        copies = stage_copies(pairs + [(g_in, g_ref)], sems)
-
-        def chunk(p, carry):
-            rows = pl.ds(pl.multiple_of(p * 16, 16), 16)
-            for half in range(2):
-                at = slice(half * 128, half * 128 + 128)
-
-                def load(i):
-                    return (z_ref[i, p, 0, :, at], z_ref[i, p, 1, :, at])
-
-                forward_radix(load, tw_ref, hi, lo, rows, half)
-            return carry
-
-        for q in range(4):
-            copies[q].wait()
-            lax.fori_loop(q * 4, q * 4 + 4, chunk, 0)
-        copies[4].wait()
+    norm_ref[...] = jnp.zeros_like(norm_ref)
+    pairs = [(z_in.at[:, planes_of(q)], z_ref.at[:, planes_of(q)]) for q in range(4)]
+    copies = stage_copies(pairs + [(h_in, h_ref), (g_in, g_ref)], sems)
+
+    def take(k):
+        return pltpu.make_async_copy(t_in.at[k], t_ref.at[k], t_sems.at[k])
+
+    def begin(k, carry):
+        take(k).start()
+        return carry
+
+    lax.fori_loop(0, RADIX, begin, 0)
+
+    def chunk(p, carry):
+        rows = pl.ds(pl.multiple_of(p * 16, 16), 16)
         for half in range(2):
-
-            def load_holo(i):
-                return (h_ref[i, :, half, :], h_ref[i, :, 2 + half, :])
-
-            forward_radix(load_holo, tw_ref, hi, lo, slice(COLS, WITH_HOLO), half)
-
-    spec[...] = dot3(hi[k], lo[k], g_ref[0], g_ref[1], NN)
-
+            at = slice(half * 128, half * 128 + 128)
+
+            def load(i):
+                return (z_ref[i, p, 0, :, at], z_ref[i, p, 1, :, at])
+
+            forward_radix(load, tw_ref, hi, lo, rows, half)
+        return carry
+
+    for q in range(4):
+        copies[q].wait()
+        lax.fori_loop(q * 4, q * 4 + 4, chunk, 0)
+    copies[4].wait()
     for half in range(2):
-        at = slice(half * 128, half * 128 + 128)
-        at_im = slice(PART + half * 128, PART + half * 128 + 128)
-
-        def gather(p, total):
-            rows = pl.ds(pl.multiple_of(p * 16, 16), 16)
-            xr, xi = spec[rows, at], spec[rows, at_im]
-            tr, ti = t_ref[0, 0, rows, at], t_ref[0, 1, rows, at]
-            return (total[0] + (tr * xr - ti * xi), total[1] + (tr * xi + ti * xr))
-
-        zero = jnp.zeros((16, 128), F32)
-        pred = lax.fori_loop(0, PLANES, gather, (zero, zero), unroll=4)
-        holo = (spec[COLS:WITH_HOLO, at], spec[COLS:WITH_HOLO, at_im])
-        res = (holo[0] - pred[0], holo[1] - pred[1])
-        norm_ref[...] += res[0] * (holo[0] + pred[0]) + res[1] * (holo[1] + pred[1])
-
-        def scatter(p, carry):
-            rows = pl.ds(pl.multiple_of(p * 16, 16), 16)
-            tr, ti = t_ref[0, 0, rows, at], t_ref[0, 1, rows, at]
-            br = tr * res[0] + ti * res[1]
-            bi = tr * res[1] - ti * res[0]
-            for where, value in ((at, br), (at_im, bi)):
-                high, low = split(value)
-                bhi[rows, where] = high
-                blo[rows, where] = low
-            return carry
-
-        lax.fori_loop(0, PLANES, scatter, 0, unroll=4)
-
-    c = tw_ref[k, 0:1, :]
-    s = tw_ref[k, 1:2, :]
-    out = dot3(bhi[...], blo[...], g_ref[2], g_ref[3], NN)
-    re, im = out[:, :PART], out[:, PART:]
-    back[k, 0] = re * c + im * s
-    back[k, 1] = im * c - re * s
-
-    @pl.when(k == RADIX - 1)
-    def _():
-        square = sq_ref[...] + norm_ref[...] * (1.0 / PLANES)
-        square = square[:8, :] + square[8:, :]
-        square = square + pltpu.roll(square, 64, 1)
-        lane = lax.broadcasted_iota(jnp.int32, (8, 128), 1)
-        square = jnp.where(lane < 64, 0.0, square)
-
-        def chunk(p, carry):
-            rows = pl.ds(pl.multiple_of(p * 16, 16), 16)
-            for half in range(2):
-                at = slice(half * 128, half * 128 + 128)
-                out = dft8([(back[i, 0, rows, at], back[i, 1, rows, at]) for i in range(RADIX)], 1)
-                for i in range(RADIX):
-                    o_ref[i, p, half * 16 : half * 16 + 16, :] = out[i][0]
-                    o_ref[i, p, half * 16 + 32 : half * 16 + 48, :] = out[i][1]
+
+        def load_holo(i):
+            return (h_ref[i, :, half, :], h_ref[i, :, 2 + half, :])
+
+        forward_radix(load_holo, tw_ref, hi, lo, slice(COLS, WITH_HOLO), half)
+    copies[5].wait()
+
+    def per_k(k, carry):
+        spec[...] = dot3(hi[k], lo[k], g_ref[0], g_ref[1], NN)
+        take(k).wait()
+
+        for half in range(2):
+            at = slice(half * 128, half * 128 + 128)
+            at_im = slice(PART + half * 128, PART + half * 128 + 128)
+
+            def gather(p, total):
+                rows = pl.ds(pl.multiple_of(p * 16, 16), 16)
+                xr, xi = spec[rows, at], spec[rows, at_im]
+                tr, ti = t_ref[k, 0, rows, at], t_ref[k, 1, rows, at]
+                return (total[0] + (tr * xr - ti * xi), total[1] + (tr * xi + ti * xr))
+
+            zero = jnp.zeros((16, 128), F32)
+            pred = lax.fori_loop(0, PLANES, gather, (zero, zero), unroll=4)
+            holo = (spec[COLS:WITH_HOLO, at], spec[COLS:WITH_HOLO, at_im])
+            res = (holo[0] - pred[0], holo[1] - pred[1])
+            norm_ref[...] += res[0] * (holo[0] + pred[0]) + res[1] * (holo[1] + pred[1])
+
+            def scatter(p, carry):
+                rows = pl.ds(pl.multiple_of(p * 16, 16), 16)
+                tr, ti = t_ref[k, 0, rows, at], t_ref[k, 1, rows, at]
+                br = tr * res[0] + ti * res[1]
+                bi = tr * res[1] - ti * res[0]
+                for where, value in ((at, br), (at_im, bi)):
+                    high, low = split(value)
+                    bhi[rows, where] = high
+                    blo[rows, where] = low
+                return carry
+
+            lax.fori_loop(0, PLANES, scatter, 0, unroll=4)
+
+        c = tw_ref[k, 0:1, :]
+        s = tw_ref[k, 1:2, :]
+        out = dot3(bhi[...], blo[...], g_ref[2], g_ref[3], NN)
+        re, im = out[:, :PART], out[:, PART:]
+        back[k, 0] = re * c + im * s
+        back[k, 1] = im * c - re * s
+        return carry
+
+    lax.fori_loop(0, RADIX, per_k, 0)
+
+    square = sq_ref[...] + norm_ref[...] * (1.0 / PLANES)
+    square = square[:8, :] + square[8:, :]
+    square = square + pltpu.roll(square, 64, 1)
+    lane = lax.broadcasted_iota(jnp.int32, (8, 128), 1)
+    square = jnp.where(lane < 64, 0.0, square)
+
+    def chunk(p, carry):
+        rows = pl.ds(pl.multiple_of(p * 16, 16), 16)
+        for half in range(2):
+            at = slice(half * 128, half * 128 + 128)
+            out = dft8([(back[i, 0, rows, at], back[i, 1, rows, at]) for i in range(RADIX)], 1)
             for i in range(RADIX):
-                tile = square
-                for high in range(2):
-                    for c in range(2):
-                        low_rows = slice(c * 32 + high * 8, c * 32 + high * 8 + 8)
-                        high_rows = slice(c * 32 + 16 + high * 8, c * 32 + 24 + high * 8)
-                        edge = jnp.where(
-                            lane < 2,
-                            o_ref[min(i + 1, RADIX - 1), p, low_rows, :],
-                            o_ref[max(i - 1, 0), p, high_rows, :],
-                        )
-                        base = high * 8 + c * 4
-                        edge = pltpu.roll(edge, base + 2, 1)
-                        tile = jnp.where((lane >= base) & (lane < base + 4), edge, tile)
-                o_ref[i, p, 64:MESSAGE, :] = tile
-            return carry
-
-        sends = []
-        for q in range(4):
-            lax.fori_loop(q * 4, q * 4 + 4, chunk, 0)
-            sends.append(
-                pltpu.make_async_copy(
-                    o_ref.at[:, planes_of(q)], o_out.at[:, planes_of(q)], out_sems.at[q]
-                )
+                o_ref[i, p, half * 16 : half * 16 + 16, :] = out[i][0]
+                o_ref[i, p, half * 16 + 32 : half * 16 + 48, :] = out[i][1]
+        for i in range(RADIX):
+            tile = square
+            for high in range(2):
+                for c in range(2):
+                    low_rows = slice(c * 32 + high * 8, c * 32 + high * 8 + 8)
+                    high_rows = slice(c * 32 + 16 + high * 8, c * 32 + 24 + high * 8)
+                    edge = jnp.where(
+                        lane < 2,
+                        o_ref[min(i + 1, RADIX - 1), p, low_rows, :],
+                        o_ref[max(i - 1, 0), p, high_rows, :],
+                    )
+                    base = high * 8 + c * 4
+                    edge = pltpu.roll(edge, base + 2, 1)
+                    tile = jnp.where((lane >= base) & (lane < base + 4), edge, tile)
+            o_ref[i, p, 64:MESSAGE, :] = tile
+        return carry
+
+    sends = []
+    for q in range(4):
+        lax.fori_loop(q * 4, q * 4 + 4, chunk, 0)
+        sends.append(
+            pltpu.make_async_copy(
+                o_ref.at[:, planes_of(q)], o_out.at[:, planes_of(q)], out_sems.at[q]
             )
-            sends[-1].start()
-        for send in sends:
-            send.wait()
+        )
+        sends[-1].start()
+    for send in sends:
+        send.wait()
 
 
 def spectral(z, holo, trans, squares, table, tw):
     anywhere = pl.BlockSpec(memory_space=pl.ANY)
+    vmem = pl.BlockSpec(memory_space=pltpu.VMEM)
     return pl.pallas_call(
         spectral_body,
-        grid=(RADIX,),
-        in_specs=[
-            anywhere,
-            whole((RADIX, 16, 8, 128)),
-            pl.BlockSpec((1, 2, COLS, PART), lambda k: (k, 0, 0, 0)),
-            whole((16, 128)),
-            anywhere,
-            whole((RADIX, 2, PART)),
-        ],
+        in_specs=[anywhere, anywhere, anywhere, vmem, anywhere, vmem],
         out_specs=anywhere,
         out_shape=jax.ShapeDtypeStruct((RADIX, PLANES, MESSAGE, 128), F32),
         scratch_shapes=[
@@ -477,8 +483,11 @@
             pltpu.VMEM((RADIX, PLANES, 2, 16, PART), F32),
             pltpu.VMEM((4, 2 * PART, 2 * PART), BF16),
             pltpu.VMEM((RADIX, PLANES, MESSAGE, 128), F32),
-            pltpu.SemaphoreType.DMA((5,)),
+            pltpu.VMEM((RADIX, 16, 8, 128), F32),
+            pltpu.VMEM((RADIX, 2, COLS, PART), F32),
+            pltpu.SemaphoreType.DMA((6,)),
             pltpu.SemaphoreType.DMA((4,)),
+            pltpu.SemaphoreType.DMA((RADIX,)),
         ],
         compiler_params=params(62),
         cost_estimate=pl.CostEstimate(
@@ -489,103 +498,101 @@
 
 
 def rows_back_body(
-    w_ref, x_in, xt_ref, xb_ref, ih_ref, il_ref, eh_ref, el_ref, tw_ref, re_out, im_out, sum_ref,
-    back, edge_back, x_ref, parts, x_sem, out_sems,
+    w_in, x_in, xt_ref, xb_ref, p_in, e_in, tw_ref, re_out, im_out, sum_ref,
+    back, edge_back, w_ref, x_ref, parts, p_ref, e_ref, w_sems, sems, out_sems,
 ):
-    k = pl.program_id(0)
-    fetch = pltpu.make_async_copy(x_in, x_ref, x_sem)
-
-    @pl.when(k == 0)
-    def _():
-        fetch.start()
-        sum_ref[...] = jnp.zeros_like(sum_ref)
-
-    tiles = w_ref[0, :, 64:MESSAGE, :]
-    lane = lax.broadcasted_iota(jnp.int32, (8, 128), 1)
-    sum_ref[...] += jnp.where(lane < 64, 0.0, jnp.sum(tiles, axis=0))
-    turned = tiles.reshape(128, 128).T
-    edge = jnp.concatenate([turned[0:8, :], turned[8:16, :]], axis=1)
-    edge_high, edge_low = split(jnp.concatenate([edge, jnp.zeros_like(edge)], axis=0))
-    mixed = dot3(edge_high, edge_low, eh_ref[...], el_ref[...], NN)[0:8, :]
-    swapped = pltpu.roll(mixed, 4, 0)
-    edge_re = mixed[:, :PART] - swapped[:, PART:]
-    edge_im = mixed[:, PART:] + swapped[:, :PART]
-
-    halves = []
-    for c in range(2):
-        for h in range(2):
-            rows = slice(c * 32 + h * 16, c * 32 + h * 16 + 16)
-            halves.append(w_ref[0, :, rows, :].reshape(PART, 128).T)
-    turned = [jnp.concatenate(halves[c * 2 : c * 2 + 2], axis=0) for c in range(2)]
-    high, low = split(jnp.concatenate(turned, axis=1))
-    out = dot3(high, low, ih_ref[...], il_ref[...], NN)
-    c = tw_ref[k, 0:1, :]
-    s = tw_ref[k, 1:2, :]
-    re, im = out[:, :PART], out[:, PART:]
-    back[k, 0] = re * c + im * s
-    back[k, 1] = im * c - re * s
-    edge_back[k, 0] = edge_re * c + edge_im * s
-    edge_back[k, 1] = edge_im * c - edge_re * s
-
-    @pl.when(k == RADIX - 1)
-    def _():
-        fetch.wait()
-        low_rows = lax.broadcasted_iota(jnp.int32, (8, 128), 0) < 4
+    tables = stage_copies([(p_in, p_ref), (e_in, e_ref)], sems)
+
+    def take(k):
+        return pltpu.make_async_copy(w_in.at[k], w_ref.at[k], w_sems.at[k])
+
+    def begin(k, carry):
+        take(k).start()
+        return carry
+
+    lax.fori_loop(0, RADIX, begin, 0)
+    fetch = pltpu.make_async_copy(x_in, x_ref, sems.at[2])
+    fetch.start()
+    sum_ref[...] = jnp.zeros_like(sum_ref)
+    for copy in tables:
+        copy.wait()
+
+    def per_k(k, carry):
+        take(k).wait()
+        tiles = w_ref[k, :, 64:MESSAGE, :]
+        lane = lax.broadcasted_iota(jnp.int32, (8, 128), 1)
+        sum_ref[...] += jnp.where(lane < 64, 0.0, jnp.sum(tiles, axis=0))
+        turned = tiles.reshape(128, 128).T
+        edge = jnp.concatenate([turned[0:8, :], turned[8:16, :]], axis=1)
+        edge_high, edge_low = split(jnp.concatenate([edge, jnp.zeros_like(edge)], axis=0))
+        mixed = dot3(edge_high, edge_low, e_ref[0], e_ref[1], NN)[0:8, :]
+        swapped = pltpu.roll(mixed, 4, 0)
+        edge_re = mixed[:, :PART] - swapped[:, PART:]
+        edge_im = mixed[:, PART:] + swapped[:, :PART]
+
+        halves = []
+        for c in range(2):
+            for h in range(2):
+                rows = slice(c * 32 + h * 16, c * 32 + h * 16 + 16)
+                halves.append(w_ref[k, :, rows, :].reshape(PART, 128).T)
+        turned = [jnp.concatenate(halves[c * 2 : c * 2 + 2], axis=0) for c in range(2)]
+        high, low = split(jnp.concatenate(turned, axis=1))
+        out = dot3(high, low, p_ref[0], p_ref[1], NN)
+        c = tw_ref[k, 0:1, :]
+        s = tw_ref[k, 1:2, :]
+        re, im = out[:, :PART], out[:, PART:]
+        back[k, 0] = re * c + im * s
+        back[k, 1] = im * c - re * s
+        edge_back[k, 0] = edge_re * c + edge_im * s
+        edge_back[k, 1] = edge_im * c - edge_re * s
+        return carry
+
+    lax.fori_loop(0, RADIX, per_k, 0)
+    fetch.wait()
+    low_rows = lax.broadcasted_iota(jnp.int32, (8, 128), 0) < 4
+    for half in range(2):
+        at = slice(half * 128, half * 128 + 128)
+        out = dft8([(edge_back[i, 0, :, at], edge_back[i, 1, :, at]) for i in range(RADIX)], 1)
+        for i in range(RADIX):
+            to = slice(i * PART + half * 128, i * PART + half * 128 + 128)
+            for c in range(2):
+                value = pltpu.roll(out[i][c], 6, 0)
+                x = jnp.where(low_rows, xb_ref[c, 0, :, to], xt_ref[c, 0, :, to])
+                parts[c, ROWS:PACK, to] = value + x
+
+    def chunk(t, carry):
+        rows = pl.ds(pl.multiple_of(t * 16, 16), 16)
         for half in range(2):
             at = slice(half * 128, half * 128 + 128)
-            out = dft8([(edge_back[i, 0, :, at], edge_back[i, 1, :, at]) for i in range(RADIX)], 1)
+            out = dft8([(back[i, 0, rows, at], back[i, 1, rows, at]) for i in range(RADIX)], 1)
             for i in range(RADIX):
                 to = slice(i * PART + half * 128, i * PART + half * 128 + 128)
                 for c in range(2):
-                    value = pltpu.roll(out[i][c], 6, 0)
-                    x = jnp.where(low_rows, xb_ref[c, 0, :, to], xt_ref[c, 0, :, to])
-                    parts[c, ROWS:PACK, to] = value + x
-
-        def chunk(t, carry):
-            rows = pl.ds(pl.multiple_of(t * 16, 16), 16)
-            for half in range(2):
-                at = slice(half * 128, half * 128 + 128)
-                out = dft8([(back[i, 0, rows, at], back[i, 1, rows, at]) for i in range(RADIX)], 1)
-                for i in range(RADIX):
-                    to = slice(i * PART + half * 128, i * PART + half * 128 + 128)
-                    for c in range(2):
-                        parts[c, rows, to] = x_ref[c, 0, rows, to] + out[i][c]
-            return carry
-
-        sends = []
-        for q in range(4):
-            lax.fori_loop(q * 4, q * 4 + 4, chunk, 0)
-            span = pl.ds(q * 64, 72 if q == 3 else 64)
-            for c, target in enumerate((re_out, im_out)):
-                sends.append(
-                    pltpu.make_async_copy(
-                        parts.at[c, span, :], target.at[span, :], out_sems.at[c, q]
-                    )
+                    parts[c, rows, to] = x_ref[c, 0, rows, to] + out[i][c]
+        return carry
+
+    sends = []
+    for q in range(4):
+        lax.fori_loop(q * 4, q * 4 + 4, chunk, 0)
+        span = pl.ds(q * 64, 72 if q == 3 else 64)
+        for c, target in enumerate((re_out, im_out)):
+            sends.append(
+                pltpu.make_async_copy(
+                    parts.at[c, span, :], target.at[span, :], out_sems.at[c, q]
                 )
-                sends[-1].start()
-        for send in sends:
-            send.wait()
-
-
-def rows_back(w, x_now, x_top, x_bottom, i_high, i_low, e_high, e_low, tw):
-    table = whole((2 * PART, 2 * PART))
-    edge_table = whole((PART, 2 * PART))
+            )
+            sends[-1].start()
+    for send in sends:
+        send.wait()
+
+
+def rows_back(w, x_now, x_top, x_bottom, table, edge_table, tw):
     anywhere = pl.BlockSpec(memory_space=pl.ANY)
+    vmem = pl.BlockSpec(memory_space=pltpu.VMEM)
     return pl.pallas_call(
         rows_back_body,
-        grid=(RADIX,),
-        in_specs=[
-            pl.BlockSpec((1, 16, MESSAGE, 128), lambda k: (k, 0, 0, 0)),
-            anywhere,
-            whole((2, 1, 8, N)),
-            whole((2, 1, 8, N)),
-            table,
-            table,
-            edge_table,
-            edge_table,
-            whole((RADIX, 2, PART)),
-        ],
-        out_specs=[anywhere, anywhere, whole((8, 128))],
+        in_specs=[anywhere, anywhere, vmem, vmem, anywhere, anywhere, vmem],
+        out_specs=[anywhere, anywhere, vmem],
         out_shape=[
             jax.ShapeDtypeStruct((PACK, N), F32),
             jax.ShapeDtypeStruct((PACK, N), F32),
@@ -594,9 +601,13 @@
         scratch_shapes=[
             pltpu.VMEM((RADIX, 2, ROWS, PART), F32),
             pltpu.VMEM((RADIX, 2, 8, PART), F32),
+            pltpu.VMEM((RADIX, 16, MESSAGE, 128), F32),
             pltpu.VMEM((2, 1, ROWS, N), F32),
             pltpu.VMEM((2, PACK, N), F32),
-            pltpu.SemaphoreType.DMA,
+            pltpu.VMEM((2, 2 * PART, 2 * PART), BF16),
+            pltpu.VMEM((2, PART, 2 * PART), BF16),
+            pltpu.SemaphoreType.DMA((RADIX,)),
+            pltpu.SemaphoreType.DMA((3,)),
             pltpu.SemaphoreType.DMA((2, 4)),
         ],
         compiler_params=params(62),
@@ -604,7 +615,7 @@
             flops=4 * 10**9, bytes_accessed=13 * MIB, transcendentals=0
         ),
         name="rows_back",
-    )(w, x_now, x_top, x_bottom, i_high, i_low, e_high, e_low, tw)
+    )(w, x_now, x_top, x_bottom, table, edge_table, tw)
 
 
 TILES = EXT // 8
@@ -673,9 +684,10 @@
 
 
 def tv_first_body(
-    num_ref, at_ref, own, nxt, prv, inner_out, dual_out,
-    ext, inner, dual, in_sems, edge_sems, out_sems,
+    halves, num_ref, at_ref, own, nxt, prv, inner_out, *rest
 ):
+    high_out = rest[0] if halves else None
+    dual_out, ext, inner, dual, in_sems, edge_sems, out_sems = rest[-7:]
     size = ROWS // STAGES
     mains = []
     for q in range(STAGES):
@@ -760,6 +772,7 @@
             def _():
                 inner[ROWS + 8 : ROWS + 9, :] = inner[ROWS + 7 : ROWS + 8, :]
 
+        if q == STAGES - 1 and not halves:
             row = lax.broadcasted_iota(jnp.int32, (8, N), 0)
             inner[0:8, :] = jnp.where(row < 4, inner[ROWS + 8 : EXT, :], inner[0:8, :])
             outs.append(
@@ -772,32 +785,43 @@
         first = max(done, 1)
         last = min(upto, TILES - 1)
         span = pl.ds(done * 8, (upto - done) * 8)
-        outs += [
-            pltpu.make_async_copy(
-                inner.at[pl.ds(first * 8, (last - first) * 8), :],
-                inner_out.at[pl.ds(first * 8 - 8, (last - first) * 8), :],
-                out_sems.at[0, q],
-            ),
-            pltpu.make_async_copy(dual.at[:, span, :], dual_out.at[:, span, :], out_sems.at[1, q]),
-        ]
-        outs[-2].start()
+        if halves:
+            moves = []
+            if done * 8 < HALF + 16:
+                moves.append((inner_out, 0, done * 8, min(upto * 8, HALF + 16), 0))
+            if upto * 8 > HALF:
+                moves.append((high_out, HALF, max(done * 8, HALF), upto * 8, 2))
+        else:
+            moves = [(inner_out, 8, first * 8, last * 8, 0)]
+        for target, shift, begin, end, lane in moves:
+            outs.append(
+                pltpu.make_async_copy(
+                    inner.at[pl.ds(begin, end - begin), :],
+                    target.at[pl.ds(begin - shift, end - begin), :],
+                    out_sems.at[lane, q],
+                )
+            )
+            outs[-1].start()
+        outs.append(
+            pltpu.make_async_copy(dual.at[:, span, :], dual_out.at[:, span, :], out_sems.at[1, q])
+        )
         outs[-1].start()
         done = upto
     for copy in outs:
         copy.wait()
 
 
-def tv_first(numbers, place, own, nxt, prv):
+def tv_first(halves, numbers, place, own, nxt, prv):
     smem = pl.BlockSpec(memory_space=pltpu.SMEM)
     anywhere = pl.BlockSpec(memory_space=pl.ANY)
+    inner = [jax.ShapeDtypeStruct((PACK, N), F32)]
+    if halves:
+        inner = [jax.ShapeDtypeStruct((HALF + 16, N), F32)] * 2
     return pl.pallas_call(
-        tv_first_body,
+        functools.partial(tv_first_body, halves),
         in_specs=[smem, smem] + [anywhere] * 3,
-        out_specs=[anywhere, anywhere],
-        out_shape=[
-            jax.ShapeDtypeStruct((PACK, N), F32),
-            jax.ShapeDtypeStruct((4, EXT, N), F32),
-        ],
+        out_specs=[anywhere] * (len(inner) + 1),
+        out_shape=inner + [jax.ShapeDtypeStruct((4, EXT, N), F32)],
         scratch_shapes=[
             pltpu.VMEM((3, EXT, N), F32),
             pltpu.VMEM((EXT, N), F32),
@@ -806,7 +830,7 @@
             pltpu.SemaphoreType.DMA((3, 2)),
             pltpu.SemaphoreType.DMA((3, STAGES)),
         ],
-        compiler_params=params(62),
+        compiler_params=params(63),
         cost_estimate=pl.CostEstimate(
             flops=10**8, bytes_accessed=17 * MIB, transcendentals=2 * 10**6
         ),
@@ -815,25 +839,35 @@
 
 
 def tv_second_body(
-    comp, num_ref, own_in, nxt_in, prv_in, dual_in, parts_in, x_prev_in, x_now_in, *rest
+    comp, half, num_ref, own_in, nxt_in, prv_in, dual_in, parts_in, x_prev_in, x_now_in, *rest
 ):
     out_ref, inner, dual, plain, below, sems, edge_sems, out_sems = rest[-8:]
+    count = ROWS if half is None else HALF
+    offset = 0 if half is None else HALF * half
     size = ROWS // STAGES
+    stages = count // size
     copies = []
-    for q in range(STAGES):
+    for q in range(stages):
         first = 0 if q == 0 else q * size + 16
         span = pl.ds(first, (q + 1) * size + 16 - first)
         main = pl.ds(q * size, size)
+        place = pl.ds(offset + q * size, size)
+        dual_span = pl.ds(offset + first, (q + 1) * size + 16 - first)
         begin = 0 if q == 0 else q * size + 8
         end = min((q + 1) * size + 8, ROWS)
         blocks = []
         for i, ref in enumerate((own_in, nxt_in, prv_in)):
-            blocks += arrivals(ref, inner.at[i], q, begin, end, sems.at[i], edge_sems.at[i])
+            if half is None:
+                blocks += arrivals(ref, inner.at[i], q, begin, end, sems.at[i], edge_sems.at[i])
+            else:
+                blocks.append(
+                    pltpu.make_async_copy(ref.at[span, :], inner.at[i, span, :], sems.at[i, q])
+                )
         pairs = [
-            (dual_in.at[:, span, :], dual.at[:, span, :]),
-            (parts_in.at[main, :], plain.at[0, main, :]),
-            (x_prev_in.at[comp, 0, main, :], plain.at[1, main, :]),
-            (x_now_in.at[comp, 0, main, :], plain.at[2, main, :]),
+            (dual_in.at[:, dual_span, :], dual.at[:, span, :]),
+            (parts_in.at[place, :], plain.at[0, main, :]),
+            (x_prev_in.at[comp, 0, place, :], plain.at[1, main, :]),
+            (x_now_in.at[comp, 0, place, :], plain.at[2, main, :]),
         ]
         copies.append(
             blocks
@@ -886,7 +920,7 @@
         below[:, at] = (dual[1, 0:8, at] + gy) * reciprocal(1.0 + norm(gz, gy, gx))
 
     outs = []
-    for q in range(STAGES):
+    for q in range(stages):
         for copy in copies[q]:
             copy.wait()
         if q == 0:
@@ -896,7 +930,9 @@
         main = pl.ds(q * size, size)
         outs.append(
             pltpu.make_async_copy(
-                plain.at[1, main, :], out_ref.at[comp, 0, main, :], out_sems.at[q]
+                plain.at[1, main, :],
+                out_ref.at[comp, 0, pl.ds(offset + q * size, size), :],
+                out_sems.at[q],
             )
         )
         outs[-1].start()
@@ -904,30 +940,31 @@
         copy.wait()
 
 
-def tv_second(comp, numbers, own, nxt, prv, dual, parts, x_prev, x_now, into):
+def tv_second(comp, half, numbers, own, nxt, prv, dual, parts, x_prev, x_now, into):
     smem = pl.BlockSpec(memory_space=pltpu.SMEM)
     anywhere = pl.BlockSpec(memory_space=pl.ANY)
+    count = ROWS if half is None else HALF
     args = [numbers, own, nxt, prv, dual, parts, x_prev, x_now]
     aliases = {}
     if into is not None:
         args.append(into)
         aliases = {len(args) - 1: 0}
     return pl.pallas_call(
-        functools.partial(tv_second_body, comp),
+        functools.partial(tv_second_body, comp, half),
         in_specs=[smem] + [anywhere] * (len(args) - 1),
         out_specs=anywhere,
         out_shape=jax.ShapeDtypeStruct((2, 1, ROWS, N), F32),
         scratch_shapes=[
-            pltpu.VMEM((3, EXT, N), F32),
-            pltpu.VMEM((4, EXT, N), F32),
-            pltpu.VMEM((3, ROWS, N), F32),
+            pltpu.VMEM((3, count + 16, N), F32),
+            pltpu.VMEM((4, count + 16, N), F32),
+            pltpu.VMEM((3, count, N), F32),
             pltpu.VMEM((8, N), F32),
             pltpu.SemaphoreType.DMA((7, STAGES)),
             pltpu.SemaphoreType.DMA((3, 2)),
             pltpu.SemaphoreType.DMA((STAGES,)),
         ],
         input_output_aliases=aliases,
-        compiler_params=params(62),
+        compiler_params=params(63),
         cost_estimate=pl.CostEstimate(
             flops=10**8, bytes_accessed=23 * MIB, transcendentals=2 * 10**6
         ),
@@ -995,10 +1032,8 @@
         x_now,
         x_top,
         x_bottom,
-        jnp.asarray(p_high),
-        jnp.asarray(p_low),
-        jnp.asarray(e_high),
-        jnp.asarray(e_low),
+        jnp.asarray(np.stack([p_high, p_low])),
+        jnp.asarray(np.stack([e_high, e_low])),
         tw,
     )
 
@@ -1020,14 +1055,15 @@
     own = (re, im)
     nxt = [from_behind(part, "depth", -1) for part in own]
     prv = [from_behind(part, "depth", 1) for part in own]
+    inner_re, dual_re = tv_first(False, numbers, place, own[0], nxt[0], prv[0])
+    inner_low, inner_high, dual_im = tv_first(True, numbers, place, own[1], nxt[1], prv[1])
+    steps = ((0, None, inner_re, dual_re), (1, 0, inner_low, dual_im), (1, 1, inner_high, dual_im))
     out = None
-    firsts = [tv_first(numbers, place, own[c], nxt[c], prv[c]) for c in range(2)]
-    ahead = [from_behind(inner, "depth", -1) for inner, _ in firsts]
-    behind = [from_behind(inner, "depth", 1) for inner, _ in firsts]
-    for c in range(2):
-        inner, dual = firsts[c]
+    for c, half, inner, dual in steps:
+        ahead = from_behind(inner, "depth", -1)
+        behind = from_behind(inner, "depth", 1)
         out = tv_second(
-            c, numbers, inner, ahead[c], behind[c], dual, own[c], x_prev, x_now, out
+            c, half, numbers, inner, ahead, behind, dual, own[c], x_prev, x_now, out
         )
     return out
 

time: 307 us -> 304 us (level)
  waiting for transfers between devices: 141 us -> 128 us
  starting transfers between devices: 54 us -> 61.2 us
  Pallas kernels: 101 us -> 105 us
    ppermute x10 -> x12, waiting for transfers between devices: 94.7 us -> 81.5 us  [from_behind(): return lax.ppermute(x, axis, pairs)]
    ppermute x10 -> x12, starting transfers between devices: 27.8 us -> 35 us  [from_behind(): return lax.ppermute(x, axis, pairs)]
    pallas_call x7 -> x8, Pallas kernels: 87.6 us -> 91 us  [the longest x3 27.3 us: tv_second(): pl.pallas_call(functools.partial(tv_second_body, comp, half), in_specs=[s...]
  transfers between devices with their start and end apart: 13 -> 15, of which waited for: 13 -> 12; matrix products, arithmetic and copies ran while one was open for 1% -> 1% of each run, Pallas kernels for 17% -> 19%
where the time goes in v4:
time: 304 us; the launch traced here: 301 us
  waiting for transfers between devices  128 us (42%)
  Pallas kernels  105 us (35%)
  starting transfers between devices  61.2 us (20%)
  local copies, waits for them, and re-layouts  3.8 us (1%)
    ppermute x12, waiting for transfers between devices, from_behind(): return lax.ppermute(x, axis, pairs)  81.5 us
    all_to_all x1, waiting for transfers between devices, shards(): got = lax.all_to_all(sent.reshape(128, 2, 16, ROWS), both, 0, 0, tiled=True)  42.3 us
    ppermute x12, starting transfers between devices, from_behind(): return lax.ppermute(x, axis, pairs)  35 us
    pallas_call x3, Pallas kernels, tv_second(): pl.pallas_call(functools.partial(tv_second_body, comp, half), in_specs=[s...  27.3 us
    pallas_call x2, Pallas kernels, tv_first(): pl.pallas_call(functools.partial(tv_first_body, halves), in_specs=[smem,...  22.8 us
    pallas_call x1, Pallas kernels, spectral(): pl.pallas_call(spectral_body, in_specs=[anywhere, anywhere, anywhere, vme...  19.3 us
    pallas_call x1, Pallas kernels, rows_back(): pl.pallas_call(rows_back_body, in_specs=[anywhere, anywhere, vmem, vmem,...  11.4 us
    all_to_all x1, starting transfers between devices, shards(): holo = lax.all_to_all(holo.reshape(128, 8, 128), both, 0, 0, tiled=True)  10.2 us
  transfers between devices with their start and end apart: 15, of which 12 were waited for; matrix products, arithmetic and copies ran while one was open for 1% of the time, Pallas kernels for 19%

profile of v4, /device:TPU:32, one launch (start us, length us, event | category | flops | bytes accessed | tf_op | source)
XLA Modules:
  0.0 301.3 jit_solution(14612988618347925243)
XLA Ops:
  0.7 1.4 dynamic-slice_bitcast_fusion
  2.1 7.3 %holo_forward.1 = f32[8,16,8,128]{3,2,1,0:T(8,128)} custom-call(f32[1]{0:T(128)S(6)} %copy.17.depth_ref, f32[2,256,2048]{2,1,0:T(8,128)} %x_in.4, bf16[32,512]{1,0:T(8,128)(2,1)} %get-tuple-element.28.gh_ref, bf16[32,512]{1,0:T(8,128)(2,1)} %get-tuple-element.27.gl_ref, f32[8,2,256]{2,1,0:T(2,128)} %constant.64.clone.tw_ref), custom_call_target="tpu_custom_call" | custom-call | flops 400000000 | bytes 5242880 | tf_op jit(solution)/shard_map/holo_forward/pallas_call | solution.py:256
  9.4 10.2 %all-to-all-start.1 = ((f32[128,8,128]{2,1,0:T(8,128)}), f32[128,8,128]{2,1,0:T(8,128)S(1)}, u32[]{:S(2)}, u32[]{:S(2)}) async-start(f32[128,8,128]{2,1,0:T(8,128)} %bitcast.20), calls=%async_computation.1 | async-start | bytes 1048576 | tf_op jit(solution)/shard_map/all_to_all | solution.py:1007
  19.6 10.2 %rows_forward.1 = (f32[8,16,2,16,256]{4,3,2,1,0:T(8,128)}, f32[16,128]{1,0:T(8,128)}) custom-call(f32[2,1,256,2048]{3,2,1,0:T(8,128)} %x_now_in.5, bf16[2,512,512]{2,1,0:T(8,128)(2,1)} %constant.66.clone.g_in, f32[8,2,256]{2,1,0:T(2,128)} %constant.64.clone.tw_ref), custom_call_target="tpu_custom_call" | custom-call | flops 4000000000 | bytes 10485760 | tf_op jit(solution)/shard_map/rows_forward/pallas_call | solution.py:198
  29.8 3.0 all-to-all-done.1
  32.9 0.0 copy-start
  32.9 7.2 %all-to-all-start = ((f32[128,2,16,256]{3,2,1,0:T(8,128)}), f32[128,2,16,256]{3,2,1,0:T(8,128)}, u32[]{:S(2)}, u32[]{:S(2)}) async-start(f32[128,2,16,256]{3,2,1,0:T(8,128)} %bitcast.19), calls=%async_computation | async-start | bytes 8388608 | tf_op jit(solution)/shard_map/all_to_all | solution.py:1018
  40.1 0.8 fusion.rate_ref
  40.9 0.0 copy-done
  40.9 0.7 slice_reduce_fusion
  41.7 6.3 %transfer.1.t_in = f32[8,2,256,256]{3,2,1,0:T(8,128)} custom-call(f32[1,16]{1,0:T(1,128)} %bitcast.22, f32[8,16,256]{2,1,0:T(8,128)} %fusion.rate_ref), custom_call_target="tpu_custom_call" | custom-call | flops 10000000 | bytes 4194304 | tf_op jit(solution)/shard_map/transfer/pallas_call | solution.py:314
  47.9 42.3 %all-to-all-done = f32[128,2,16,256]{3,2,1,0:T(8,128)} async-done(((f32[128,2,16,256]{3,2,1,0:T(8,128)}), f32[128,2,16,256]{3,2,1,0:T(8,128)}, u32[]{:S(2)}, u32[]{:S(2)}) %all-to-all-start) | async-done | bytes 4194336 | tf_op jit(solution)/shard_map/all_to_all | solution.py:1018
  90.3 19.3 %spectral.1 = f32[8,16,72,128]{3,2,1,0:T(8,128)} custom-call(f32[8,16,2,16,256]{4,3,2,1,0:T(8,128)} %bitcast.1.z_in, f32[8,16,8,128]{3,2,1,0:T(8,128)} %bitcast.21, f32[8,2,256,256]{3,2,1,0:T(8,128)} %transfer.1.t_in, f32[16,128]{1,0:T(8,128)} %get-tuple-element.16.sq_ref, bf16[4,512,512]{2,1,0:T(8,128)(2,1)} %constant.67.clone.g_in, ...), custom_call_target="tpu_custom_call" | custom-call | flops 8000000000 | bytes 14680064 | tf_op jit(solution)/shard_map/spectral/pallas_call | solution.py:470
  109.5 8.8 %all-to-all-start.2 = ((f32[128,72,128]{2,1,0:T(8,128)}), f32[128,72,128]{2,1,0:T(8,128)}, u32[]{:S(2)}, u32[]{:S(2)}) async-start(f32[128,72,128]{2,1,0:T(8,128)} %bitcast.18), calls=%async_computation.2 | async-start | bytes 9437184 | tf_op jit(solution)/shard_map/all_to_all | solution.py:1029
  118.3 1.0 fusion.9
  119.3 3.4 %collective-permute-start = (f32[2,1,8,2048]{3,2,1,0:T(8,128)S(1)}, f32[2,1,8,2048]{3,2,1,0:T(8,128)S(1)}, u32[]{:S(2)}, u32[]{:S(2)}) collective-permute-start(f32[2,1,8,2048]{3,2,1,0:T(8,128)S(1)} %get-tuple-element.26), channel_id=1, source_target_pairs={{0,1},{1,2},{2,3},{3,4},{4,5},{5,6},{6,7},{8,9},{9,10},{10,11},{11... | collective-permute-start | bytes 393224 | tf_op jit(solution)/shard_map/ppermute | solution.py:978
  122.8 1.3 collective-permute-start.1
  124.1 47.4 %collective-permute-done.xt_ref = f32[2,1,8,2048]{3,2,1,0:T(8,128)S(1)} collective-permute-done((f32[2,1,8,2048]{3,2,1,0:T(8,128)S(1)}, f32[2,1,8,2048]{3,2,1,0:T(8,128)S(1)}, u32[]{:S(2)}, u32[]{:S(2)}) %collective-permute-start) | collective-permute-done | bytes 131104 | tf_op jit(solution)/shard_map/ppermute | solution.py:978
  171.5 0.0 copy-start.1
  171.5 2.6 collective-permute-done.1.xb_ref
  174.1 0.0 copy-start.2
  174.1 0.9 all-to-all-done.2
  175.0 0.0 copy-done.1
  175.0 0.0 copy-done.2
  175.0 11.4 %rows_back.1 = (f32[264,2048]{1,0:T(8,128)}, f32[264,2048]{1,0:T(8,128)}, f32[8,128]{1,0:T(8,128)}) custom-call(f32[8,16,72,128]{3,2,1,0:T(8,128)} %bitcast.7.w_in, f32[2,1,256,2048]{3,2,1,0:T(8,128)} %x_now_in.5, f32[2,1,8,2048]{3,2,1,0:T(8,128)} %copy-done.1, f32[2,1,8,2048]{3,2,1,0:T(8,128)} %copy-done.2, bf16[2,512,512]{2,1,0:T(8,128)(2,1)} %constant.68.clone.p_in, ...), custom_call_target="tpu_custom_call" | custom-call | flops 4000000000 | bytes 13631488 | tf_op jit(solution)/shard_map/rows_back/pallas_call | solution.py:592
  186.4 4.8 %collective-permute-start.8 = (f32[264,2048]{1,0:T(8,128)}, f32[264,2048]{1,0:T(8,128)}, u32[]{:S(2)}, u32[]{:S(2)}) collective-permute-start(f32[264,2048]{1,0:T(8,128)} %get-tuple-element.22.own.parts_in), channel_id=1, source_target_pairs={{8,0},{16,8},{24,16},{32,24},{40,32},{48,40},{56,48},{64,56},{72,6... | collective-permute-start | bytes 6488072 | tf_op jit(solution)/shard_map/ppermute | solution.py:978
  191.2 1.9 collective-permute-start.9
  193.1 5.8 %collective-permute-start.2 = (f32[264,2048]{1,0:T(8,128)}, f32[264,2048]{1,0:T(8,128)}, u32[]{:S(2)}, u32[]{:S(2)}) collective-permute-start(f32[264,2048]{1,0:T(8,128)} %get-tuple-element.18.own.parts_in), channel_id=1, source_target_pairs={{8,0},{16,8},{24,16},{32,24},{40,32},{48,40},{56,48},{64,56},{72,6... | collective-permute-start | bytes 6488072 | tf_op jit(solution)/shard_map/ppermute | solution.py:978
  198.9 1.9 collective-permute-start.3
  200.8 1.3 reduce_sum.9
  202.9 0.7 stack.38.num_ref
  203.6 12.1 %collective-permute-done.8.nxt = f32[264,2048]{1,0:T(8,128)} collective-permute-done((f32[264,2048]{1,0:T(8,128)}, f32[264,2048]{1,0:T(8,128)}, u32[]{:S(2)}, u32[]{:S(2)}) %collective-permute-start.8) | collective-permute-done | bytes 2162720 | tf_op jit(solution)/shard_map/ppermute | solution.py:978
  215.7 5.9 %collective-permute-done.9.prv = f32[264,2048]{1,0:T(8,128)} collective-permute-done((f32[264,2048]{1,0:T(8,128)}, f32[264,2048]{1,0:T(8,128)}, u32[]{:S(2)}, u32[]{:S(2)}) %collective-permute-start.9) | collective-permute-done | bytes 2162720 | tf_op jit(solution)/shard_map/ppermute | solution.py:978
  221.7 11.4 %tv_first.3 = (f32[264,2048]{1,0:T(8,128)}, f32[4,272,2048]{2,1,0:T(8,128)}) custom-call(f32[6]{0:T(128)} %stack.38.num_ref, s32[1]{0:T(128)} %bitcast.14.at_ref, f32[264,2048]{1,0:T(8,128)} %get-tuple-element.22.own.parts_in, f32[264,2048]{1,0:T(8,128)} %collective-permute-done.8.nxt, f32[264,2048]{1,0:T(8,128)} %collective-permute-done.9.prv), custom_call_target="tpu_custom_call" | custom-call | flops 100000000 | bytes 17825792 | tf_op jit(solution)/shard_map/tv_first/pallas_call | solution.py:820
  233.1 1.9 collective-permute-start.10
  235.0 2.4 collective-permute-start.11
  237.4 1.5 collective-permute-done.2.nxt
  238.9 5.9 %collective-permute-done.3.prv = f32[264,2048]{1,0:T(8,128)} collective-permute-done((f32[264,2048]{1,0:T(8,128)}, f32[264,2048]{1,0:T(8,128)}, u32[]{:S(2)}, u32[]{:S(2)}) %collective-permute-start.3) | collective-permute-done | bytes 2162720 | tf_op jit(solution)/shard_map/ppermute | solution.py:978
  244.8 11.4 %tv_first.2 = (f32[144,2048]{1,0:T(8,128)}, f32[144,2048]{1,0:T(8,128)}, f32[4,272,2048]{2,1,0:T(8,128)}) custom-call(f32[6]{0:T(128)} %stack.38.num_ref, s32[1]{0:T(128)} %bitcast.14.at_ref, f32[264,2048]{1,0:T(8,128)} %get-tuple-element.18.own.parts_in, f32[264,2048]{1,0:T(8,128)} %collective-permute-done.2.nxt, f32[264,2048]{1,0:T(8,128)} %collective-permute-done.3.prv), custom_call_target="tpu_custom_call" | custom-call | flops 100000000 | bytes 17825792 | tf_op jit(solution)/shard_map/tv_first/pallas_call | solution.py:820
  256.2 1.9 collective-permute-start.6
  258.2 2.4 collective-permute-start.7
  260.6 5.3 %collective-permute-start.4 = (f32[144,2048]{1,0:T(8,128)}, f32[144,2048]{1,0:T(8,128)}, u32[]{:S(2)}, u32[]{:S(2)}) collective-permute-start(f32[144,2048]{1,0:T(8,128)} %get-tuple-element.19.own_in), channel_id=1, source_target_pairs={{8,0},{16,8},{24,16},{32,24},{40,32},{48,40},{56,48},{64,56},{72,6... | collective-permute-start | bytes 3538952 | tf_op jit(solution)/shard_map/ppermute | solution.py:978
  265.8 0.0 collective-permute-done.10.nxt_in
  265.9 1.9 collective-permute-start.5
  267.8 0.2 collective-permute-done.11.prv_in
  268.0 11.4 %tv_second.3.rest_0_ = f32[2,1,256,2048]{3,2,1,0:T(8,128)} custom-call(f32[6]{0:T(128)} %stack.38.num_ref, f32[264,2048]{1,0:T(8,128)} %get-tuple-element.23.own_in, f32[264,2048]{1,0:T(8,128)} %collective-permute-done.10.nxt_in, f32[264,2048]{1,0:T(8,128)} %collective-permute-done.11.prv_in, f32[4,272,2048]{2,1,0:T(8,128)} %get-tuple-element.24.dual_in, ...), custom_call_target="tpu_custom_call" | custom-call | flops 100000000 | bytes 24117248 | tf_op jit(solution)/shard_map/tv_second/pallas_call | solution.py:952
  279.4 0.0 collective-permute-done.6.nxt_in
  279.4 1.3 collective-permute-done.7.prv_in
  280.6 8.0 %tv_second.4.rest_0_ = f32[2,1,256,2048]{3,2,1,0:T(8,128)} custom-call(f32[6]{0:T(128)} %stack.38.num_ref, f32[144,2048]{1,0:T(8,128)} %get-tuple-element.21.own_in, f32[144,2048]{1,0:T(8,128)} %collective-permute-done.6.nxt_in, f32[144,2048]{1,0:T(8,128)} %collective-permute-done.7.prv_in, ...), custom_call_target="tpu_custom_call", output_to_operand_aliasing={{}: (8, {})} | custom-call | flops 100000000 | bytes 24117248 | tf_op jit(solution)/shard_map/tv_second/pallas_call | solution.py:952
  288.6 0.0 collective-permute-done.4.nxt_in
  288.6 4.6 %collective-permute-done.5.prv_in = f32[144,2048]{1,0:T(8,128)} collective-permute-done((f32[144,2048]{1,0:T(8,128)}, f32[144,2048]{1,0:T(8,128)}, u32[]{:S(2)}, u32[]{:S(2)}) %collective-permute-start.5) | collective-permute-done | bytes 1179680 | tf_op jit(solution)/shard_map/ppermute | solution.py:978
  293.3 8.0 %tv_second.5 = f32[2,1,256,2048]{3,2,1,0:T(8,128)} custom-call(f32[6]{0:T(128)} %stack.38.num_ref, f32[144,2048]{1,0:T(8,128)} %get-tuple-element.19.own_in, f32[144,2048]{1,0:T(8,128)} %collective-permute-done.4.nxt_in, f32[144,2048]{1,0:T(8,128)} %collective-permute-done.5.prv_in, ...), custom_call_target="tpu_custom_call", output_to_operand_aliasing={{}: (8, {})} | custom-call | flops 100000000 | bytes 24117248 | tf_op jit(solution)/shard_map/tv_second/pallas_call | solution.py:952
  (3 shorter events, 0.0 us)
Async XLA Ops:
  9.4 23.5 %all-to-all-start.1 = ((f32[128,8,128]{2,1,0:T(8,128)}), f32[128,8,128]{2,1,0:T(8,128)S(1)}, u32[]{:S(2)}, u32[]{:S(2)}) async-start(f32[128,8,128]{2,1,0:T(8,128)} %bitcast.20), calls=%async_computation.1 | async-start | bytes 1048576 | tf_op jit(solution)/shard_map/all_to_all | solution.py:1007
  32.9 8.1 %copy-start = (f32[128,8,128]{2,1,0:T(8,128)}, f32[128,8,128]{2,1,0:T(8,128)S(1)}, u32[]{:S(2)}) copy-start(f32[128,8,128]{2,1,0:T(8,128)S(1)} %all-to-all-done.1) | copy-start | bytes 1572868
  32.9 57.4 %all-to-all-start = ((f32[128,2,16,256]{3,2,1,0:T(8,128)}), f32[128,2,16,256]{3,2,1,0:T(8,128)}, u32[]{:S(2)}, u32[]{:S(2)}) async-start(f32[128,2,16,256]{3,2,1,0:T(8,128)} %bitcast.19), calls=%async_computation | async-start | bytes 8388608 | tf_op jit(solution)/shard_map/all_to_all | solution.py:1018
  109.5 65.5 %all-to-all-start.2 = ((f32[128,72,128]{2,1,0:T(8,128)}), f32[128,72,128]{2,1,0:T(8,128)}, u32[]{:S(2)}, u32[]{:S(2)}) async-start(f32[128,72,128]{2,1,0:T(8,128)} %bitcast.18), calls=%async_computation.2 | async-start | bytes 9437184 | tf_op jit(solution)/shard_map/all_to_all | solution.py:1029
  119.3 52.1 %collective-permute-start = (f32[2,1,8,2048]{3,2,1,0:T(8,128)S(1)}, f32[2,1,8,2048]{3,2,1,0:T(8,128)S(1)}, u32[]{:S(2)}, u32[]{:S(2)}) collective-permute-start(f32[2,1,8,2048]{3,2,1,0:T(8,128)S(1)} %get-tuple-element.26), channel_id=1, source_target_pairs={{0,1},{1,2},{2,3},{3,4},{4,5},{5,6},{6,7},{8,9},{9,10},{10,11},{11... | collective-permute-start | bytes 393224 | tf_op jit(solution)/shard_map/ppermute | solution.py:978
  122.8 51.3 %collective-permute-start.1 = (f32[2,1,8,2048]{3,2,1,0:T(8,128)S(1)}, f32[2,1,8,2048]{3,2,1,0:T(8,128)S(1)}, u32[]{:S(2)}, u32[]{:S(2)}) collective-permute-start(f32[2,1,8,2048]{3,2,1,0:T(8,128)S(1)} %get-tuple-element.25), channel_id=1, source_target_pairs={{1,0},{2,1},{3,2},{4,3},{5,4},{6,5},{7,6},{9,8},{10,9},{11,10},{12... | collective-permute-start | bytes 393224 | tf_op jit(solution)/shard_map/ppermute | solution.py:978
  171.5 3.5 %copy-start.1 = (f32[2,1,8,2048]{3,2,1,0:T(8,128)}, f32[2,1,8,2048]{3,2,1,0:T(8,128)S(1)}, u32[]{:S(2)}) copy-start(f32[2,1,8,2048]{3,2,1,0:T(8,128)S(1)} %collective-permute-done.xt_ref) | copy-start | bytes 393220
  174.1 1.0 copy-start.2
  186.4 29.3 %collective-permute-start.8 = (f32[264,2048]{1,0:T(8,128)}, f32[264,2048]{1,0:T(8,128)}, u32[]{:S(2)}, u32[]{:S(2)}) collective-permute-start(f32[264,2048]{1,0:T(8,128)} %get-tuple-element.22.own.parts_in), channel_id=1, source_target_pairs={{8,0},{16,8},{24,16},{32,24},{40,32},{48,40},{56,48},{64,56},{72,6... | collective-permute-start | bytes 6488072 | tf_op jit(solution)/shard_map/ppermute | solution.py:978
  191.2 30.5 %collective-permute-start.9 = (f32[264,2048]{1,0:T(8,128)}, f32[264,2048]{1,0:T(8,128)}, u32[]{:S(2)}, u32[]{:S(2)}) collective-permute-start(f32[264,2048]{1,0:T(8,128)} %get-tuple-element.22.own.parts_in), channel_id=1, source_target_pairs={{0,8},{8,16},{16,24},{24,32},{32,40},{40,48},{48,56},{56,64},{64,7... | collective-permute-start | bytes 6488072 | tf_op jit(solution)/shard_map/ppermute | solution.py:978
  193.1 45.8 %collective-permute-start.2 = (f32[264,2048]{1,0:T(8,128)}, f32[264,2048]{1,0:T(8,128)}, u32[]{:S(2)}, u32[]{:S(2)}) collective-permute-start(f32[264,2048]{1,0:T(8,128)} %get-tuple-element.18.own.parts_in), channel_id=1, source_target_pairs={{8,0},{16,8},{24,16},{32,24},{40,32},{48,40},{56,48},{64,56},{72,6... | collective-permute-start | bytes 6488072 | tf_op jit(solution)/shard_map/ppermute | solution.py:978
  198.9 46.0 %collective-permute-start.3 = (f32[264,2048]{1,0:T(8,128)}, f32[264,2048]{1,0:T(8,128)}, u32[]{:S(2)}, u32[]{:S(2)}) collective-permute-start(f32[264,2048]{1,0:T(8,128)} %get-tuple-element.18.own.parts_in), channel_id=1, source_target_pairs={{0,8},{8,16},{16,24},{24,32},{32,40},{40,48},{48,56},{56,64},{64,7... | collective-permute-start | bytes 6488072 | tf_op jit(solution)/shard_map/ppermute | solution.py:978
  233.1 32.8 %collective-permute-start.10 = (f32[264,2048]{1,0:T(8,128)}, f32[264,2048]{1,0:T(8,128)}, u32[]{:S(2)}, u32[]{:S(2)}) collective-permute-start(f32[264,2048]{1,0:T(8,128)} %get-tuple-element.23.own_in), channel_id=1, source_target_pairs={{8,0},{16,8},{24,16},{32,24},{40,32},{48,40},{56,48},{64,56},{72,6... | collective-permute-start | bytes 6488072 | tf_op jit(solution)/shard_map/ppermute | solution.py:978
  235.0 33.0 %collective-permute-start.11 = (f32[264,2048]{1,0:T(8,128)}, f32[264,2048]{1,0:T(8,128)}, u32[]{:S(2)}, u32[]{:S(2)}) collective-permute-start(f32[264,2048]{1,0:T(8,128)} %get-tuple-element.23.own_in), channel_id=1, source_target_pairs={{0,8},{8,16},{16,24},{24,32},{32,40},{40,48},{48,56},{56,64},{64,7... | collective-permute-start | bytes 6488072 | tf_op jit(solution)/shard_map/ppermute | solution.py:978
  256.2 23.1 %collective-permute-start.6 = (f32[144,2048]{1,0:T(8,128)}, f32[144,2048]{1,0:T(8,128)}, u32[]{:S(2)}, u32[]{:S(2)}) collective-permute-start(f32[144,2048]{1,0:T(8,128)} %get-tuple-element.21.own_in), channel_id=1, source_target_pairs={{8,0},{16,8},{24,16},{32,24},{40,32},{48,40},{56,48},{64,56},{72,6... | collective-permute-start | bytes 3538952 | tf_op jit(solution)/shard_map/ppermute | solution.py:978
  258.2 22.5 %collective-permute-start.7 = (f32[144,2048]{1,0:T(8,128)}, f32[144,2048]{1,0:T(8,128)}, u32[]{:S(2)}, u32[]{:S(2)}) collective-permute-start(f32[144,2048]{1,0:T(8,128)} %get-tuple-element.21.own_in), channel_id=1, source_target_pairs={{0,8},{8,16},{16,24},{24,32},{32,40},{40,48},{48,56},{56,64},{64,7... | collective-permute-start | bytes 3538952 | tf_op jit(solution)/shard_map/ppermute | solution.py:978
  260.6 28.1 %collective-permute-start.4 = (f32[144,2048]{1,0:T(8,128)}, f32[144,2048]{1,0:T(8,128)}, u32[]{:S(2)}, u32[]{:S(2)}) collective-permute-start(f32[144,2048]{1,0:T(8,128)} %get-tuple-element.19.own_in), channel_id=1, source_target_pairs={{8,0},{16,8},{24,16},{32,24},{40,32},{48,40},{56,48},{64,56},{72,6... | collective-permute-start | bytes 3538952 | tf_op jit(solution)/shard_map/ppermute | solution.py:978
  265.9 27.4 %collective-permute-start.5 = (f32[144,2048]{1,0:T(8,128)}, f32[144,2048]{1,0:T(8,128)}, u32[]{:S(2)}, u32[]{:S(2)}) collective-permute-start(f32[144,2048]{1,0:T(8,128)} %get-tuple-element.19.own_in), channel_id=1, source_target_pairs={{0,8},{8,16},{16,24},{24,32},{32,40},{40,48},{48,56},{56,64},{64,7... | collective-permute-start | bytes 3538952 | tf_op jit(solution)/shard_map/ppermute | solution.py:978

commit v5 on v4

--- a/solution.py
+++ b/solution.py
@@ -844,8 +844,8 @@
     out_ref, inner, dual, plain, below, sems, edge_sems, out_sems = rest[-8:]
     count = ROWS if half is None else HALF
     offset = 0 if half is None else HALF * half
-    size = ROWS // STAGES
-    stages = count // size
+    size = count // STAGES
+    stages = STAGES
     copies = []
     for q in range(stages):
         first = 0 if q == 0 else q * size + 16

time: 304 us -> 304 us (level)
  transfers between devices with their start and end apart: 15 -> 15, of which waited for: 12 -> 11; matrix products, arithmetic and copies ran while one was open for 1% -> 1% of each run, Pallas kernels for 19% -> 19%
where the time goes in v5:
time: 304 us; the launch traced here: 301 us
  waiting for transfers between devices  129 us (42%)
  Pallas kernels  103 us (34%)
  starting transfers between devices  61.4 us (20%)
  local copies, waits for them, and re-layouts  3.8 us (1%)
    ppermute x12, waiting for transfers between devices, from_behind(): return lax.ppermute(x, axis, pairs)  82.2 us
    all_to_all x1, waiting for transfers between devices, shards(): got = lax.all_to_all(sent.reshape(128, 2, 16, ROWS), both, 0, 0, tiled=True)  42.3 us
    ppermute x12, starting transfers between devices, from_behind(): return lax.ppermute(x, axis, pairs)  35.1 us
    pallas_call x3, Pallas kernels, tv_second(): pl.pallas_call(functools.partial(tv_second_body, comp, half), in_specs=[s...  25.6 us
    pallas_call x2, Pallas kernels, tv_first(): pl.pallas_call(functools.partial(tv_first_body, halves), in_specs=[smem,...  22.8 us
    pallas_call x1, Pallas kernels, spectral(): pl.pallas_call(spectral_body, in_specs=[anywhere, anywhere, anywhere, vme...  19.3 us
    pallas_call x1, Pallas kernels, rows_back(): pl.pallas_call(rows_back_body, in_specs=[anywhere, anywhere, vmem, vmem,...  11.4 us
    all_to_all x1, starting transfers between devices, shards(): holo = lax.all_to_all(holo.reshape(128, 8, 128), both, 0, 0, tiled=True)  10.2 us
  transfers between devices with their start and end apart: 15, of which 11 were waited for; matrix products, arithmetic and copies ran while one was open for 1% of the time, Pallas kernels for 19%

profile of v5, /device:TPU:32, one launch (start us, length us, event | category | flops | bytes accessed | tf_op | source)
XLA Modules:
  0.0 300.6 jit_solution(6126894275223478575)
XLA Ops:
  0.7 1.4 dynamic-slice_bitcast_fusion
  2.1 7.3 %holo_forward.1 = f32[8,16,8,128]{3,2,1,0:T(8,128)} custom-call(f32[1]{0:T(128)S(6)} %copy.17.depth_ref, f32[2,256,2048]{2,1,0:T(8,128)} %x_in.4, bf16[32,512]{1,0:T(8,128)(2,1)} %get-tuple-element.28.gh_ref, bf16[32,512]{1,0:T(8,128)(2,1)} %get-tuple-element.27.gl_ref, f32[8,2,256]{2,1,0:T(2,128)} %constant.64.clone.tw_ref), custom_call_target="tpu_custom_call" | custom-call | flops 400000000 | bytes 5242880 | tf_op jit(solution)/shard_map/holo_forward/pallas_call | solution.py:256
  9.4 10.2 %all-to-all-start.1 = ((f32[128,8,128]{2,1,0:T(8,128)}), f32[128,8,128]{2,1,0:T(8,128)S(1)}, u32[]{:S(2)}, u32[]{:S(2)}) async-start(f32[128,8,128]{2,1,0:T(8,128)} %bitcast.20), calls=%async_computation.1 | async-start | bytes 1048576 | tf_op jit(solution)/shard_map/all_to_all | solution.py:1007
  19.6 10.2 %rows_forward.1 = (f32[8,16,2,16,256]{4,3,2,1,0:T(8,128)}, f32[16,128]{1,0:T(8,128)}) custom-call(f32[2,1,256,2048]{3,2,1,0:T(8,128)} %x_now_in.5, bf16[2,512,512]{2,1,0:T(8,128)(2,1)} %constant.66.clone.g_in, f32[8,2,256]{2,1,0:T(2,128)} %constant.64.clone.tw_ref), custom_call_target="tpu_custom_call" | custom-call | flops 4000000000 | bytes 10485760 | tf_op jit(solution)/shard_map/rows_forward/pallas_call | solution.py:198
  29.9 3.0 all-to-all-done.1
  32.9 0.0 copy-start
  32.9 7.2 %all-to-all-start = ((f32[128,2,16,256]{3,2,1,0:T(8,128)}), f32[128,2,16,256]{3,2,1,0:T(8,128)}, u32[]{:S(2)}, u32[]{:S(2)}) async-start(f32[128,2,16,256]{3,2,1,0:T(8,128)} %bitcast.19), calls=%async_computation | async-start | bytes 8388608 | tf_op jit(solution)/shard_map/all_to_all | solution.py:1018
  40.1 0.8 fusion.rate_ref
  40.9 0.0 copy-done
  40.9 0.7 slice_reduce_fusion
  41.7 6.3 %transfer.1.t_in = f32[8,2,256,256]{3,2,1,0:T(8,128)} custom-call(f32[1,16]{1,0:T(1,128)} %bitcast.22, f32[8,16,256]{2,1,0:T(8,128)} %fusion.rate_ref), custom_call_target="tpu_custom_call" | custom-call | flops 10000000 | bytes 4194304 | tf_op jit(solution)/shard_map/transfer/pallas_call | solution.py:314
  47.9 42.3 %all-to-all-done = f32[128,2,16,256]{3,2,1,0:T(8,128)} async-done(((f32[128,2,16,256]{3,2,1,0:T(8,128)}), f32[128,2,16,256]{3,2,1,0:T(8,128)}, u32[]{:S(2)}, u32[]{:S(2)}) %all-to-all-start) | async-done | bytes 4194336 | tf_op jit(solution)/shard_map/all_to_all | solution.py:1018
  90.3 19.3 %spectral.1 = f32[8,16,72,128]{3,2,1,0:T(8,128)} custom-call(f32[8,16,2,16,256]{4,3,2,1,0:T(8,128)} %bitcast.1.z_in, f32[8,16,8,128]{3,2,1,0:T(8,128)} %bitcast.21, f32[8,2,256,256]{3,2,1,0:T(8,128)} %transfer.1.t_in, f32[16,128]{1,0:T(8,128)} %get-tuple-element.16.sq_ref, bf16[4,512,512]{2,1,0:T(8,128)(2,1)} %constant.67.clone.g_in, ...), custom_call_target="tpu_custom_call" | custom-call | flops 8000000000 | bytes 14680064 | tf_op jit(solution)/shard_map/spectral/pallas_call | solution.py:470
  109.5 8.8 %all-to-all-start.2 = ((f32[128,72,128]{2,1,0:T(8,128)}), f32[128,72,128]{2,1,0:T(8,128)}, u32[]{:S(2)}, u32[]{:S(2)}) async-start(f32[128,72,128]{2,1,0:T(8,128)} %bitcast.18), calls=%async_computation.2 | async-start | bytes 9437184 | tf_op jit(solution)/shard_map/all_to_all | solution.py:1029
  118.3 1.0 fusion.9
  119.3 3.4 %collective-permute-start = (f32[2,1,8,2048]{3,2,1,0:T(8,128)S(1)}, f32[2,1,8,2048]{3,2,1,0:T(8,128)S(1)}, u32[]{:S(2)}, u32[]{:S(2)}) collective-permute-start(f32[2,1,8,2048]{3,2,1,0:T(8,128)S(1)} %get-tuple-element.26), channel_id=1, source_target_pairs={{0,1},{1,2},{2,3},{3,4},{4,5},{5,6},{6,7},{8,9},{9,10},{10,11},{11... | collective-permute-start | bytes 393224 | tf_op jit(solution)/shard_map/ppermute | solution.py:978
  122.8 1.3 collective-permute-start.1
  124.1 47.4 %collective-permute-done.xt_ref = f32[2,1,8,2048]{3,2,1,0:T(8,128)S(1)} collective-permute-done((f32[2,1,8,2048]{3,2,1,0:T(8,128)S(1)}, f32[2,1,8,2048]{3,2,1,0:T(8,128)S(1)}, u32[]{:S(2)}, u32[]{:S(2)}) %collective-permute-start) | collective-permute-done | bytes 131104 | tf_op jit(solution)/shard_map/ppermute | solution.py:978
  171.5 0.0 copy-start.1
  171.5 2.6 collective-permute-done.1.xb_ref
  174.1 0.0 copy-start.2
  174.1 0.9 all-to-all-done.2
  175.0 0.0 copy-done.1
  175.0 0.0 copy-done.2
  175.0 11.4 %rows_back.1 = (f32[264,2048]{1,0:T(8,128)}, f32[264,2048]{1,0:T(8,128)}, f32[8,128]{1,0:T(8,128)}) custom-call(f32[8,16,72,128]{3,2,1,0:T(8,128)} %bitcast.7.w_in, f32[2,1,256,2048]{3,2,1,0:T(8,128)} %x_now_in.5, f32[2,1,8,2048]{3,2,1,0:T(8,128)} %copy-done.1, f32[2,1,8,2048]{3,2,1,0:T(8,128)} %copy-done.2, bf16[2,512,512]{2,1,0:T(8,128)(2,1)} %constant.68.clone.p_in, ...), custom_call_target="tpu_custom_call" | custom-call | flops 4000000000 | bytes 13631488 | tf_op jit(solution)/shard_map/rows_back/pallas_call | solution.py:592
  186.4 4.8 %collective-permute-start.8 = (f32[264,2048]{1,0:T(8,128)}, f32[264,2048]{1,0:T(8,128)}, u32[]{:S(2)}, u32[]{:S(2)}) collective-permute-start(f32[264,2048]{1,0:T(8,128)} %get-tuple-element.22.own.parts_in), channel_id=1, source_target_pairs={{8,0},{16,8},{24,16},{32,24},{40,32},{48,40},{56,48},{64,56},{72,6... | collective-permute-start | bytes 6488072 | tf_op jit(solution)/shard_map/ppermute | solution.py:978
  191.2 1.9 collective-permute-start.9
  193.1 5.8 %collective-permute-start.2 = (f32[264,2048]{1,0:T(8,128)}, f32[264,2048]{1,0:T(8,128)}, u32[]{:S(2)}, u32[]{:S(2)}) collective-permute-start(f32[264,2048]{1,0:T(8,128)} %get-tuple-element.18.own.parts_in), channel_id=1, source_target_pairs={{8,0},{16,8},{24,16},{32,24},{40,32},{48,40},{56,48},{64,56},{72,6... | collective-permute-start | bytes 6488072 | tf_op jit(solution)/shard_map/ppermute | solution.py:978
  198.9 1.9 collective-permute-start.3
  200.8 1.3 reduce_sum.9
  202.9 0.7 stack.38.num_ref
  203.6 12.1 %collective-permute-done.8.nxt = f32[264,2048]{1,0:T(8,128)} collective-permute-done((f32[264,2048]{1,0:T(8,128)}, f32[264,2048]{1,0:T(8,128)}, u32[]{:S(2)}, u32[]{:S(2)}) %collective-permute-start.8) | collective-permute-done | bytes 2162720 | tf_op jit(solution)/shard_map/ppermute | solution.py:978
  215.7 5.9 %collective-permute-done.9.prv = f32[264,2048]{1,0:T(8,128)} collective-permute-done((f32[264,2048]{1,0:T(8,128)}, f32[264,2048]{1,0:T(8,128)}, u32[]{:S(2)}, u32[]{:S(2)}) %collective-permute-start.9) | collective-permute-done | bytes 2162720 | tf_op jit(solution)/shard_map/ppermute | solution.py:978
  221.6 11.4 %tv_first.3 = (f32[264,2048]{1,0:T(8,128)}, f32[4,272,2048]{2,1,0:T(8,128)}) custom-call(f32[6]{0:T(128)} %stack.38.num_ref, s32[1]{0:T(128)} %bitcast.14.at_ref, f32[264,2048]{1,0:T(8,128)} %get-tuple-element.22.own.parts_in, f32[264,2048]{1,0:T(8,128)} %collective-permute-done.8.nxt, f32[264,2048]{1,0:T(8,128)} %collective-permute-done.9.prv), custom_call_target="tpu_custom_call" | custom-call | flops 100000000 | bytes 17825792 | tf_op jit(solution)/shard_map/tv_first/pallas_call | solution.py:820
  233.1 1.9 collective-permute-start.10
  235.0 2.4 collective-permute-start.11
  237.4 1.5 collective-permute-done.2.nxt
  238.9 5.9 %collective-permute-done.3.prv = f32[264,2048]{1,0:T(8,128)} collective-permute-done((f32[264,2048]{1,0:T(8,128)}, f32[264,2048]{1,0:T(8,128)}, u32[]{:S(2)}, u32[]{:S(2)}) %collective-permute-start.3) | collective-permute-done | bytes 2162720 | tf_op jit(solution)/shard_map/ppermute | solution.py:978
  244.8 11.4 %tv_first.2 = (f32[144,2048]{1,0:T(8,128)}, f32[144,2048]{1,0:T(8,128)}, f32[4,272,2048]{2,1,0:T(8,128)}) custom-call(f32[6]{0:T(128)} %stack.38.num_ref, s32[1]{0:T(128)} %bitcast.14.at_ref, f32[264,2048]{1,0:T(8,128)} %get-tuple-element.18.own.parts_in, f32[264,2048]{1,0:T(8,128)} %collective-permute-done.2.nxt, f32[264,2048]{1,0:T(8,128)} %collective-permute-done.3.prv), custom_call_target="tpu_custom_call" | custom-call | flops 100000000 | bytes 17825792 | tf_op jit(solution)/shard_map/tv_first/pallas_call | solution.py:820
  256.2 1.9 collective-permute-start.6
  258.2 2.4 collective-permute-start.7
  260.6 5.3 %collective-permute-start.4 = (f32[144,2048]{1,0:T(8,128)}, f32[144,2048]{1,0:T(8,128)}, u32[]{:S(2)}, u32[]{:S(2)}) collective-permute-start(f32[144,2048]{1,0:T(8,128)} %get-tuple-element.19.own_in), channel_id=1, source_target_pairs={{8,0},{16,8},{24,16},{32,24},{40,32},{48,40},{56,48},{64,56},{72,6... | collective-permute-start | bytes 3538952 | tf_op jit(solution)/shard_map/ppermute | solution.py:978
  265.8 0.0 collective-permute-done.10.nxt_in
  265.9 2.1 collective-permute-start.5
  268.0 0.0 collective-permute-done.11.prv_in
  268.0 11.4 %tv_second.3.rest_0_ = f32[2,1,256,2048]{3,2,1,0:T(8,128)} custom-call(f32[6]{0:T(128)} %stack.38.num_ref, f32[264,2048]{1,0:T(8,128)} %get-tuple-element.23.own_in, f32[264,2048]{1,0:T(8,128)} %collective-permute-done.10.nxt_in, f32[264,2048]{1,0:T(8,128)} %collective-permute-done.11.prv_in, f32[4,272,2048]{2,1,0:T(8,128)} %get-tuple-element.24.dual_in, ...), custom_call_target="tpu_custom_call" | custom-call | flops 100000000 | bytes 24117248 | tf_op jit(solution)/shard_map/tv_second/pallas_call | solution.py:952
  279.4 0.0 collective-permute-done.6.nxt_in
  279.4 1.3 collective-permute-done.7.prv_in
  280.6 7.1 %tv_second.4.rest_0_ = f32[2,1,256,2048]{3,2,1,0:T(8,128)} custom-call(f32[6]{0:T(128)} %stack.38.num_ref, f32[144,2048]{1,0:T(8,128)} %get-tuple-element.21.own_in, f32[144,2048]{1,0:T(8,128)} %collective-permute-done.6.nxt_in, f32[144,2048]{1,0:T(8,128)} %collective-permute-done.7.prv_in, ...), custom_call_target="tpu_custom_call", output_to_operand_aliasing={{}: (8, {})} | custom-call | flops 100000000 | bytes 24117248 | tf_op jit(solution)/shard_map/tv_second/pallas_call | solution.py:952
  287.8 0.0 collective-permute-done.4.nxt_in
  287.8 5.5 %collective-permute-done.5.prv_in = f32[144,2048]{1,0:T(8,128)} collective-permute-done((f32[144,2048]{1,0:T(8,128)}, f32[144,2048]{1,0:T(8,128)}, u32[]{:S(2)}, u32[]{:S(2)}) %collective-permute-start.5) | collective-permute-done | bytes 1179680 | tf_op jit(solution)/shard_map/ppermute | solution.py:978
  293.3 7.1 %tv_second.5 = f32[2,1,256,2048]{3,2,1,0:T(8,128)} custom-call(f32[6]{0:T(128)} %stack.38.num_ref, f32[144,2048]{1,0:T(8,128)} %get-tuple-element.19.own_in, f32[144,2048]{1,0:T(8,128)} %collective-permute-done.4.nxt_in, f32[144,2048]{1,0:T(8,128)} %collective-permute-done.5.prv_in, ...), custom_call_target="tpu_custom_call", output_to_operand_aliasing={{}: (8, {})} | custom-call | flops 100000000 | bytes 24117248 | tf_op jit(solution)/shard_map/tv_second/pallas_call | solution.py:952
  (3 shorter events, 0.0 us)
Async XLA Ops:
  9.4 23.5 %all-to-all-start.1 = ((f32[128,8,128]{2,1,0:T(8,128)}), f32[128,8,128]{2,1,0:T(8,128)S(1)}, u32[]{:S(2)}, u32[]{:S(2)}) async-start(f32[128,8,128]{2,1,0:T(8,128)} %bitcast.20), calls=%async_computation.1 | async-start | bytes 1048576 | tf_op jit(solution)/shard_map/all_to_all | solution.py:1007
  32.9 8.1 %copy-start = (f32[128,8,128]{2,1,0:T(8,128)}, f32[128,8,128]{2,1,0:T(8,128)S(1)}, u32[]{:S(2)}) copy-start(f32[128,8,128]{2,1,0:T(8,128)S(1)} %all-to-all-done.1) | copy-start | bytes 1572868
  32.9 57.4 %all-to-all-start = ((f32[128,2,16,256]{3,2,1,0:T(8,128)}), f32[128,2,16,256]{3,2,1,0:T(8,128)}, u32[]{:S(2)}, u32[]{:S(2)}) async-start(f32[128,2,16,256]{3,2,1,0:T(8,128)} %bitcast.19), calls=%async_computation | async-start | bytes 8388608 | tf_op jit(solution)/shard_map/all_to_all | solution.py:1018
  109.5 65.5 %all-to-all-start.2 = ((f32[128,72,128]{2,1,0:T(8,128)}), f32[128,72,128]{2,1,0:T(8,128)}, u32[]{:S(2)}, u32[]{:S(2)}) async-start(f32[128,72,128]{2,1,0:T(8,128)} %bitcast.18), calls=%async_computation.2 | async-start | bytes 9437184 | tf_op jit(solution)/shard_map/all_to_all | solution.py:1029
  119.3 52.1 %collective-permute-start = (f32[2,1,8,2048]{3,2,1,0:T(8,128)S(1)}, f32[2,1,8,2048]{3,2,1,0:T(8,128)S(1)}, u32[]{:S(2)}, u32[]{:S(2)}) collective-permute-start(f32[2,1,8,2048]{3,2,1,0:T(8,128)S(1)} %get-tuple-element.26), channel_id=1, source_target_pairs={{0,1},{1,2},{2,3},{3,4},{4,5},{5,6},{6,7},{8,9},{9,10},{10,11},{11... | collective-permute-start | bytes 393224 | tf_op jit(solution)/shard_map/ppermute | solution.py:978
  122.8 51.3 %collective-permute-start.1 = (f32[2,1,8,2048]{3,2,1,0:T(8,128)S(1)}, f32[2,1,8,2048]{3,2,1,0:T(8,128)S(1)}, u32[]{:S(2)}, u32[]{:S(2)}) collective-permute-start(f32[2,1,8,2048]{3,2,1,0:T(8,128)S(1)} %get-tuple-element.25), channel_id=1, source_target_pairs={{1,0},{2,1},{3,2},{4,3},{5,4},{6,5},{7,6},{9,8},{10,9},{11,10},{12... | collective-permute-start | bytes 393224 | tf_op jit(solution)/shard_map/ppermute | solution.py:978
  171.5 3.5 %copy-start.1 = (f32[2,1,8,2048]{3,2,1,0:T(8,128)}, f32[2,1,8,2048]{3,2,1,0:T(8,128)S(1)}, u32[]{:S(2)}) copy-start(f32[2,1,8,2048]{3,2,1,0:T(8,128)S(1)} %collective-permute-done.xt_ref) | copy-start | bytes 393220
  174.1 1.0 copy-start.2
  186.4 29.3 %collective-permute-start.8 = (f32[264,2048]{1,0:T(8,128)}, f32[264,2048]{1,0:T(8,128)}, u32[]{:S(2)}, u32[]{:S(2)}) collective-permute-start(f32[264,2048]{1,0:T(8,128)} %get-tuple-element.22.own.parts_in), channel_id=1, source_target_pairs={{8,0},{16,8},{24,16},{32,24},{40,32},{48,40},{56,48},{64,56},{72,6... | collective-permute-start | bytes 6488072 | tf_op jit(solution)/shard_map/ppermute | solution.py:978
  191.2 30.5 %collective-permute-start.9 = (f32[264,2048]{1,0:T(8,128)}, f32[264,2048]{1,0:T(8,128)}, u32[]{:S(2)}, u32[]{:S(2)}) collective-permute-start(f32[264,2048]{1,0:T(8,128)} %get-tuple-element.22.own.parts_in), channel_id=1, source_target_pairs={{0,8},{8,16},{16,24},{24,32},{32,40},{40,48},{48,56},{56,64},{64,7... | collective-permute-start | bytes 6488072 | tf_op jit(solution)/shard_map/ppermute | solution.py:978
  193.1 45.8 %collective-permute-start.2 = (f32[264,2048]{1,0:T(8,128)}, f32[264,2048]{1,0:T(8,128)}, u32[]{:S(2)}, u32[]{:S(2)}) collective-permute-start(f32[264,2048]{1,0:T(8,128)} %get-tuple-element.18.own.parts_in), channel_id=1, source_target_pairs={{8,0},{16,8},{24,16},{32,24},{40,32},{48,40},{56,48},{64,56},{72,6... | collective-permute-start | bytes 6488072 | tf_op jit(solution)/shard_map/ppermute | solution.py:978
  198.9 46.0 %collective-permute-start.3 = (f32[264,2048]{1,0:T(8,128)}, f32[264,2048]{1,0:T(8,128)}, u32[]{:S(2)}, u32[]{:S(2)}) collective-permute-start(f32[264,2048]{1,0:T(8,128)} %get-tuple-element.18.own.parts_in), channel_id=1, source_target_pairs={{0,8},{8,16},{16,24},{24,32},{32,40},{40,48},{48,56},{56,64},{64,7... | collective-permute-start | bytes 6488072 | tf_op jit(solution)/shard_map/ppermute | solution.py:978
  233.1 32.8 %collective-permute-start.10 = (f32[264,2048]{1,0:T(8,128)}, f32[264,2048]{1,0:T(8,128)}, u32[]{:S(2)}, u32[]{:S(2)}) collective-permute-start(f32[264,2048]{1,0:T(8,128)} %get-tuple-element.23.own_in), channel_id=1, source_target_pairs={{8,0},{16,8},{24,16},{32,24},{40,32},{48,40},{56,48},{64,56},{72,6... | collective-permute-start | bytes 6488072 | tf_op jit(solution)/shard_map/ppermute | solution.py:978
  235.0 33.0 %collective-permute-start.11 = (f32[264,2048]{1,0:T(8,128)}, f32[264,2048]{1,0:T(8,128)}, u32[]{:S(2)}, u32[]{:S(2)}) collective-permute-start(f32[264,2048]{1,0:T(8,128)} %get-tuple-element.23.own_in), channel_id=1, source_target_pairs={{0,8},{8,16},{16,24},{24,32},{32,40},{40,48},{48,56},{56,64},{64,7... | collective-permute-start | bytes 6488072 | tf_op jit(solution)/shard_map/ppermute | solution.py:978
  256.2 23.1 %collective-permute-start.6 = (f32[144,2048]{1,0:T(8,128)}, f32[144,2048]{1,0:T(8,128)}, u32[]{:S(2)}, u32[]{:S(2)}) collective-permute-start(f32[144,2048]{1,0:T(8,128)} %get-tuple-element.21.own_in), channel_id=1, source_target_pairs={{8,0},{16,8},{24,16},{32,24},{40,32},{48,40},{56,48},{64,56},{72,6... | collective-permute-start | bytes 3538952 | tf_op jit(solution)/shard_map/ppermute | solution.py:978
  258.2 22.5 %collective-permute-start.7 = (f32[144,2048]{1,0:T(8,128)}, f32[144,2048]{1,0:T(8,128)}, u32[]{:S(2)}, u32[]{:S(2)}) collective-permute-start(f32[144,2048]{1,0:T(8,128)} %get-tuple-element.21.own_in), channel_id=1, source_target_pairs={{0,8},{8,16},{16,24},{24,32},{32,40},{40,48},{48,56},{56,64},{64,7... | collective-permute-start | bytes 3538952 | tf_op jit(solution)/shard_map/ppermute | solution.py:978
  260.6 27.2 %collective-permute-start.4 = (f32[144,2048]{1,0:T(8,128)}, f32[144,2048]{1,0:T(8,128)}, u32[]{:S(2)}, u32[]{:S(2)}) collective-permute-start(f32[144,2048]{1,0:T(8,128)} %get-tuple-element.19.own_in), channel_id=1, source_target_pairs={{8,0},{16,8},{24,16},{32,24},{40,32},{48,40},{56,48},{64,56},{72,6... | collective-permute-start | bytes 3538952 | tf_op jit(solution)/shard_map/ppermute | solution.py:978
  265.9 27.4 %collective-permute-start.5 = (f32[144,2048]{1,0:T(8,128)}, f32[144,2048]{1,0:T(8,128)}, u32[]{:S(2)}, u32[]{:S(2)}) collective-permute-start(f32[144,2048]{1,0:T(8,128)} %get-tuple-element.19.own_in), channel_id=1, source_target_pairs={{0,8},{8,16},{16,24},{24,32},{32,40},{40,48},{48,56},{56,64},{64,7... | collective-permute-start | bytes 3538952 | tf_op jit(solution)/shard_map/ppermute | solution.py:978

commit v6 on v5

--- a/solution.py
+++ b/solution.py
@@ -143,12 +143,15 @@
     return copies
 
 
-def quarter(q):
-    return pl.ds(q * (ROWS // 4), ROWS // 4)
+PIECES = 8
+
+
+def piece(q):
+    return pl.ds(q * (ROWS // PIECES), ROWS // PIECES)
 
 
 def rows_body(x_in, g_in, tw_ref, y_out, ss_ref, hi, lo, x_ref, g_ref, y_ref, sems, out_sems):
-    pairs = [(x_in.at[:, :, quarter(q), :], x_ref.at[:, :, quarter(q), :]) for q in range(4)]
+    pairs = [(x_in.at[:, :, piece(q), :], x_ref.at[:, :, piece(q), :]) for q in range(PIECES)]
     copies = stage_copies(pairs + [(g_in, g_ref)], sems)
 
     def chunk(t, total):
@@ -166,11 +169,11 @@
         return total
 
     total = jnp.zeros((16, 128), F32)
-    for q in range(4):
+    for q in range(PIECES):
         copies[q].wait()
-        total = lax.fori_loop(q * 4, q * 4 + 4, chunk, total)
+        total = lax.fori_loop(q * 2, q * 2 + 2, chunk, total)
     ss_ref[...] = total
-    copies[4].wait()
+    copies[PIECES].wait()
 
     def send(k):
         return pltpu.make_async_copy(y_ref.at[k], y_out.at[k], out_sems.at[k])
@@ -209,7 +212,7 @@
             pltpu.VMEM((2, 1, ROWS, N), F32),
             pltpu.VMEM((2, 2 * PART, 2 * PART), BF16),
             pltpu.VMEM((RADIX, 16, 2, 16, ROWS), F32),
-            pltpu.SemaphoreType.DMA((5,)),
+            pltpu.SemaphoreType.DMA((PIECES + 1,)),
             pltpu.SemaphoreType.DMA((RADIX,)),
         ],
         compiler_params=params(62),
@@ -221,7 +224,7 @@
 
 
 def holo_body(depth_ref, x_in, gh_ref, gl_ref, tw_ref, y_ref, hi, lo, x_ref, sems):
-    pairs = [(x_in.at[:, quarter(q), :], x_ref.at[:, quarter(q), :]) for q in range(4)]
+    pairs = [(x_in.at[:, piece(q), :], x_ref.at[:, piece(q), :]) for q in range(PIECES)]
     copies = stage_copies(pairs, sems)
 
     def chunk(t, carry):
@@ -235,9 +238,9 @@
             forward_radix(load, tw_ref, hi, lo, rows, half)
         return carry
 
-    for q in range(4):
+    for q in range(PIECES):
         copies[q].wait()
-        lax.fori_loop(q * 4, q * 4 + 4, chunk, 0)
+        lax.fori_loop(q * 2, q * 2 + 2, chunk, 0)
     y_ref[...] = jnp.full(y_ref.shape, depth_ref[0], F32)
 
     def per_k(k, carry):
@@ -260,7 +263,7 @@
             pltpu.VMEM((RADIX, ROWS, 2 * PART), BF16),
             pltpu.VMEM((RADIX, ROWS, 2 * PART), BF16),
             pltpu.VMEM((2, ROWS, N), F32),
-            pltpu.SemaphoreType.DMA((4,)),
+            pltpu.SemaphoreType.DMA((PIECES,)),
         ],
         in_specs=[
             pl.BlockSpec(memory_space=pltpu.SMEM),

time: 304 us -> 303 us (level)
  no operation moved by 1% of the time
where the time goes in v6:
time: 303 us; the launch traced here: 300 us
  waiting for transfers between devices  129 us (43%)
  Pallas kernels  103 us (34%)
  starting transfers between devices  61.3 us (20%)
  local copies, waits for them, and re-layouts  3.8 us (1%)
    ppermute x12, waiting for transfers between devices, from_behind(): return lax.ppermute(x, axis, pairs)  82.2 us
    all_to_all x1, waiting for transfers between devices, shards(): got = lax.all_to_all(sent.reshape(128, 2, 16, ROWS), both, 0, 0, tiled=True)  42.3 us
    ppermute x12, starting transfers between devices, from_behind(): return lax.ppermute(x, axis, pairs)  35.1 us
    pallas_call x3, Pallas kernels, tv_second(): pl.pallas_call(functools.partial(tv_second_body, comp, half), in_specs=[s...  25.6 us
    pallas_call x2, Pallas kernels, tv_first(): pl.pallas_call(functools.partial(tv_first_body, halves), in_specs=[smem,...  22.8 us
    pallas_call x1, Pallas kernels, spectral(): pl.pallas_call(spectral_body, in_specs=[anywhere, anywhere, anywhere, vme...  19.3 us
    pallas_call x1, Pallas kernels, rows_back(): pl.pallas_call(rows_back_body, in_specs=[anywhere, anywhere, vmem, vmem,...  11.4 us
    all_to_all x1, starting transfers between devices, shards(): holo = lax.all_to_all(holo.reshape(128, 8, 128), both, 0, 0, tiled=True)  10.2 us
  transfers between devices with their start and end apart: 15, of which 11 were waited for; matrix products, arithmetic and copies ran while one was open for 1% of the time, Pallas kernels for 19%

profile of v6, /device:TPU:32, one launch (start us, length us, event | category | flops | bytes accessed | tf_op | source)
XLA Modules:
  0.0 300.3 jit_solution(7724968772150654860)
XLA Ops:
  0.7 1.4 dynamic-slice_bitcast_fusion
  2.1 7.2 %holo_forward.1 = f32[8,16,8,128]{3,2,1,0:T(8,128)} custom-call(f32[1]{0:T(128)S(6)} %copy.17.depth_ref, f32[2,256,2048]{2,1,0:T(8,128)} %x_in.4, bf16[32,512]{1,0:T(8,128)(2,1)} %get-tuple-element.28.gh_ref, bf16[32,512]{1,0:T(8,128)(2,1)} %get-tuple-element.27.gl_ref, f32[8,2,256]{2,1,0:T(2,128)} %constant.64.clone.tw_ref), custom_call_target="tpu_custom_call" | custom-call | flops 400000000 | bytes 5242880 | tf_op jit(solution)/shard_map/holo_forward/pallas_call | solution.py:259
  9.2 10.2 %all-to-all-start.1 = ((f32[128,8,128]{2,1,0:T(8,128)}), f32[128,8,128]{2,1,0:T(8,128)S(1)}, u32[]{:S(2)}, u32[]{:S(2)}) async-start(f32[128,8,128]{2,1,0:T(8,128)} %bitcast.20), calls=%async_computation.1 | async-start | bytes 1048576 | tf_op jit(solution)/shard_map/all_to_all | solution.py:1010
  19.5 10.1 %rows_forward.1 = (f32[8,16,2,16,256]{4,3,2,1,0:T(8,128)}, f32[16,128]{1,0:T(8,128)}) custom-call(f32[2,1,256,2048]{3,2,1,0:T(8,128)} %x_now_in.5, bf16[2,512,512]{2,1,0:T(8,128)(2,1)} %constant.66.clone.g_in, f32[8,2,256]{2,1,0:T(2,128)} %constant.64.clone.tw_ref), custom_call_target="tpu_custom_call" | custom-call | flops 4000000000 | bytes 10485760 | tf_op jit(solution)/shard_map/rows_forward/pallas_call | solution.py:201
  29.6 3.2 %all-to-all-done.1 = f32[128,8,128]{2,1,0:T(8,128)S(1)} async-done(((f32[128,8,128]{2,1,0:T(8,128)}), f32[128,8,128]{2,1,0:T(8,128)S(1)}, u32[]{:S(2)}, u32[]{:S(2)}) %all-to-all-start.1) | async-done | bytes 524320 | tf_op jit(solution)/shard_map/all_to_all | solution.py:1010
  32.7 0.0 copy-start
  32.7 7.1 %all-to-all-start = ((f32[128,2,16,256]{3,2,1,0:T(8,128)}), f32[128,2,16,256]{3,2,1,0:T(8,128)}, u32[]{:S(2)}, u32[]{:S(2)}) async-start(f32[128,2,16,256]{3,2,1,0:T(8,128)} %bitcast.19), calls=%async_computation | async-start | bytes 8388608 | tf_op jit(solution)/shard_map/all_to_all | solution.py:1021
  39.9 0.8 fusion.rate_ref
  40.6 0.0 copy-done
  40.6 0.7 slice_reduce_fusion
  41.4 6.3 %transfer.1.t_in = f32[8,2,256,256]{3,2,1,0:T(8,128)} custom-call(f32[1,16]{1,0:T(1,128)} %bitcast.22, f32[8,16,256]{2,1,0:T(8,128)} %fusion.rate_ref), custom_call_target="tpu_custom_call" | custom-call | flops 10000000 | bytes 4194304 | tf_op jit(solution)/shard_map/transfer/pallas_call | solution.py:317
  47.6 42.3 %all-to-all-done = f32[128,2,16,256]{3,2,1,0:T(8,128)} async-done(((f32[128,2,16,256]{3,2,1,0:T(8,128)}), f32[128,2,16,256]{3,2,1,0:T(8,128)}, u32[]{:S(2)}, u32[]{:S(2)}) %all-to-all-start) | async-done | bytes 4194336 | tf_op jit(solution)/shard_map/all_to_all | solution.py:1021
  90.0 19.3 %spectral.1 = f32[8,16,72,128]{3,2,1,0:T(8,128)} custom-call(f32[8,16,2,16,256]{4,3,2,1,0:T(8,128)} %bitcast.1.z_in, f32[8,16,8,128]{3,2,1,0:T(8,128)} %bitcast.21, f32[8,2,256,256]{3,2,1,0:T(8,128)} %transfer.1.t_in, f32[16,128]{1,0:T(8,128)} %get-tuple-element.16.sq_ref, bf16[4,512,512]{2,1,0:T(8,128)(2,1)} %constant.67.clone.g_in, ...), custom_call_target="tpu_custom_call" | custom-call | flops 8000000000 | bytes 14680064 | tf_op jit(solution)/shard_map/spectral/pallas_call | solution.py:473
  109.2 8.8 %all-to-all-start.2 = ((f32[128,72,128]{2,1,0:T(8,128)}), f32[128,72,128]{2,1,0:T(8,128)}, u32[]{:S(2)}, u32[]{:S(2)}) async-start(f32[128,72,128]{2,1,0:T(8,128)} %bitcast.18), calls=%async_computation.2 | async-start | bytes 9437184 | tf_op jit(solution)/shard_map/all_to_all | solution.py:1032
  118.1 1.0 fusion.9
  119.1 3.4 %collective-permute-start = (f32[2,1,8,2048]{3,2,1,0:T(8,128)S(1)}, f32[2,1,8,2048]{3,2,1,0:T(8,128)S(1)}, u32[]{:S(2)}, u32[]{:S(2)}) collective-permute-start(f32[2,1,8,2048]{3,2,1,0:T(8,128)S(1)} %get-tuple-element.26), channel_id=1, source_target_pairs={{0,1},{1,2},{2,3},{3,4},{4,5},{5,6},{6,7},{8,9},{9,10},{10,11},{11... | collective-permute-start | bytes 393224 | tf_op jit(solution)/shard_map/ppermute | solution.py:981
  122.5 1.3 collective-permute-start.1
  123.8 47.4 %collective-permute-done.xt_ref = f32[2,1,8,2048]{3,2,1,0:T(8,128)S(1)} collective-permute-done((f32[2,1,8,2048]{3,2,1,0:T(8,128)S(1)}, f32[2,1,8,2048]{3,2,1,0:T(8,128)S(1)}, u32[]{:S(2)}, u32[]{:S(2)}) %collective-permute-start) | collective-permute-done | bytes 131104 | tf_op jit(solution)/shard_map/ppermute | solution.py:981
  171.2 0.0 copy-start.1
  171.2 2.6 collective-permute-done.1.xb_ref
  173.8 0.0 copy-start.2
  173.8 0.9 all-to-all-done.2
  174.7 0.0 copy-done.1
  174.7 0.0 copy-done.2
  174.7 11.4 %rows_back.1 = (f32[264,2048]{1,0:T(8,128)}, f32[264,2048]{1,0:T(8,128)}, f32[8,128]{1,0:T(8,128)}) custom-call(f32[8,16,72,128]{3,2,1,0:T(8,128)} %bitcast.7.w_in, f32[2,1,256,2048]{3,2,1,0:T(8,128)} %x_now_in.5, f32[2,1,8,2048]{3,2,1,0:T(8,128)} %copy-done.1, f32[2,1,8,2048]{3,2,1,0:T(8,128)} %copy-done.2, bf16[2,512,512]{2,1,0:T(8,128)(2,1)} %constant.68.clone.p_in, ...), custom_call_target="tpu_custom_call" | custom-call | flops 4000000000 | bytes 13631488 | tf_op jit(solution)/shard_map/rows_back/pallas_call | solution.py:595
  186.1 4.8 %collective-permute-start.8 = (f32[264,2048]{1,0:T(8,128)}, f32[264,2048]{1,0:T(8,128)}, u32[]{:S(2)}, u32[]{:S(2)}) collective-permute-start(f32[264,2048]{1,0:T(8,128)} %get-tuple-element.22.own.parts_in), channel_id=1, source_target_pairs={{8,0},{16,8},{24,16},{32,24},{40,32},{48,40},{56,48},{64,56},{72,6... | collective-permute-start | bytes 6488072 | tf_op jit(solution)/shard_map/ppermute | solution.py:981
  190.9 1.9 collective-permute-start.9
  192.8 5.8 %collective-permute-start.2 = (f32[264,2048]{1,0:T(8,128)}, f32[264,2048]{1,0:T(8,128)}, u32[]{:S(2)}, u32[]{:S(2)}) collective-permute-start(f32[264,2048]{1,0:T(8,128)} %get-tuple-element.18.own.parts_in), channel_id=1, source_target_pairs={{8,0},{16,8},{24,16},{32,24},{40,32},{48,40},{56,48},{64,56},{72,6... | collective-permute-start | bytes 6488072 | tf_op jit(solution)/shard_map/ppermute | solution.py:981
  198.6 1.9 collective-permute-start.3
  200.5 1.3 reduce_sum.9
  202.6 0.7 stack.38.num_ref
  203.3 12.1 %collective-permute-done.8.nxt = f32[264,2048]{1,0:T(8,128)} collective-permute-done((f32[264,2048]{1,0:T(8,128)}, f32[264,2048]{1,0:T(8,128)}, u32[]{:S(2)}, u32[]{:S(2)}) %collective-permute-start.8) | collective-permute-done | bytes 2162720 | tf_op jit(solution)/shard_map/ppermute | solution.py:981
  215.4 5.9 %collective-permute-done.9.prv = f32[264,2048]{1,0:T(8,128)} collective-permute-done((f32[264,2048]{1,0:T(8,128)}, f32[264,2048]{1,0:T(8,128)}, u32[]{:S(2)}, u32[]{:S(2)}) %collective-permute-start.9) | collective-permute-done | bytes 2162720 | tf_op jit(solution)/shard_map/ppermute | solution.py:981
  221.4 11.4 %tv_first.3 = (f32[264,2048]{1,0:T(8,128)}, f32[4,272,2048]{2,1,0:T(8,128)}) custom-call(f32[6]{0:T(128)} %stack.38.num_ref, s32[1]{0:T(128)} %bitcast.14.at_ref, f32[264,2048]{1,0:T(8,128)} %get-tuple-element.22.own.parts_in, f32[264,2048]{1,0:T(8,128)} %collective-permute-done.8.nxt, f32[264,2048]{1,0:T(8,128)} %collective-permute-done.9.prv), custom_call_target="tpu_custom_call" | custom-call | flops 100000000 | bytes 17825792 | tf_op jit(solution)/shard_map/tv_first/pallas_call | solution.py:823
  232.8 1.9 collective-permute-start.10
  234.7 2.4 collective-permute-start.11
  237.1 1.5 collective-permute-done.2.nxt
  238.6 5.9 %collective-permute-done.3.prv = f32[264,2048]{1,0:T(8,128)} collective-permute-done((f32[264,2048]{1,0:T(8,128)}, f32[264,2048]{1,0:T(8,128)}, u32[]{:S(2)}, u32[]{:S(2)}) %collective-permute-start.3) | collective-permute-done | bytes 2162720 | tf_op jit(solution)/shard_map/ppermute | solution.py:981
  244.5 11.4 %tv_first.2 = (f32[144,2048]{1,0:T(8,128)}, f32[144,2048]{1,0:T(8,128)}, f32[4,272,2048]{2,1,0:T(8,128)}) custom-call(f32[6]{0:T(128)} %stack.38.num_ref, s32[1]{0:T(128)} %bitcast.14.at_ref, f32[264,2048]{1,0:T(8,128)} %get-tuple-element.18.own.parts_in, f32[264,2048]{1,0:T(8,128)} %collective-permute-done.2.nxt, f32[264,2048]{1,0:T(8,128)} %collective-permute-done.3.prv), custom_call_target="tpu_custom_call" | custom-call | flops 100000000 | bytes 17825792 | tf_op jit(solution)/shard_map/tv_first/pallas_call | solution.py:823
  255.9 1.9 collective-permute-start.6
  257.9 2.4 collective-permute-start.7
  260.3 5.3 %collective-permute-start.4 = (f32[144,2048]{1,0:T(8,128)}, f32[144,2048]{1,0:T(8,128)}, u32[]{:S(2)}, u32[]{:S(2)}) collective-permute-start(f32[144,2048]{1,0:T(8,128)} %get-tuple-element.19.own_in), channel_id=1, source_target_pairs={{8,0},{16,8},{24,16},{32,24},{40,32},{48,40},{56,48},{64,56},{72,6... | collective-permute-start | bytes 3538952 | tf_op jit(solution)/shard_map/ppermute | solution.py:981
  265.6 0.0 collective-permute-done.10.nxt_in
  265.6 2.1 collective-permute-start.5
  267.7 0.0 collective-permute-done.11.prv_in
  267.7 11.4 %tv_second.3.rest_0_ = f32[2,1,256,2048]{3,2,1,0:T(8,128)} custom-call(f32[6]{0:T(128)} %stack.38.num_ref, f32[264,2048]{1,0:T(8,128)} %get-tuple-element.23.own_in, f32[264,2048]{1,0:T(8,128)} %collective-permute-done.10.nxt_in, f32[264,2048]{1,0:T(8,128)} %collective-permute-done.11.prv_in, f32[4,272,2048]{2,1,0:T(8,128)} %get-tuple-element.24.dual_in, ...), custom_call_target="tpu_custom_call" | custom-call | flops 100000000 | bytes 24117248 | tf_op jit(solution)/shard_map/tv_second/pallas_call | solution.py:955
  279.1 0.0 collective-permute-done.6.nxt_in
  279.1 1.3 collective-permute-done.7.prv_in
  280.3 7.1 %tv_second.4.rest_0_ = f32[2,1,256,2048]{3,2,1,0:T(8,128)} custom-call(f32[6]{0:T(128)} %stack.38.num_ref, f32[144,2048]{1,0:T(8,128)} %get-tuple-element.21.own_in, f32[144,2048]{1,0:T(8,128)} %collective-permute-done.6.nxt_in, f32[144,2048]{1,0:T(8,128)} %collective-permute-done.7.prv_in, ...), custom_call_target="tpu_custom_call", output_to_operand_aliasing={{}: (8, {})} | custom-call | flops 100000000 | bytes 24117248 | tf_op jit(solution)/shard_map/tv_second/pallas_call | solution.py:955
  287.5 0.0 collective-permute-done.4.nxt_in
  287.5 5.5 %collective-permute-done.5.prv_in = f32[144,2048]{1,0:T(8,128)} collective-permute-done((f32[144,2048]{1,0:T(8,128)}, f32[144,2048]{1,0:T(8,128)}, u32[]{:S(2)}, u32[]{:S(2)}) %collective-permute-start.5) | collective-permute-done | bytes 1179680 | tf_op jit(solution)/shard_map/ppermute | solution.py:981
  293.0 7.1 %tv_second.5 = f32[2,1,256,2048]{3,2,1,0:T(8,128)} custom-call(f32[6]{0:T(128)} %stack.38.num_ref, f32[144,2048]{1,0:T(8,128)} %get-tuple-element.19.own_in, f32[144,2048]{1,0:T(8,128)} %collective-permute-done.4.nxt_in, f32[144,2048]{1,0:T(8,128)} %collective-permute-done.5.prv_in, ...), custom_call_target="tpu_custom_call", output_to_operand_aliasing={{}: (8, {})} | custom-call | flops 100000000 | bytes 24117248 | tf_op jit(solution)/shard_map/tv_second/pallas_call | solution.py:955
  (3 shorter events, 0.0 us)
Async XLA Ops:
  9.2 23.5 %all-to-all-start.1 = ((f32[128,8,128]{2,1,0:T(8,128)}), f32[128,8,128]{2,1,0:T(8,128)S(1)}, u32[]{:S(2)}, u32[]{:S(2)}) async-start(f32[128,8,128]{2,1,0:T(8,128)} %bitcast.20), calls=%async_computation.1 | async-start | bytes 1048576 | tf_op jit(solution)/shard_map/all_to_all | solution.py:1010
  32.7 7.9 %copy-start = (f32[128,8,128]{2,1,0:T(8,128)}, f32[128,8,128]{2,1,0:T(8,128)S(1)}, u32[]{:S(2)}) copy-start(f32[128,8,128]{2,1,0:T(8,128)S(1)} %all-to-all-done.1) | copy-start | bytes 1572868
  32.7 57.3 %all-to-all-start = ((f32[128,2,16,256]{3,2,1,0:T(8,128)}), f32[128,2,16,256]{3,2,1,0:T(8,128)}, u32[]{:S(2)}, u32[]{:S(2)}) async-start(f32[128,2,16,256]{3,2,1,0:T(8,128)} %bitcast.19), calls=%async_computation | async-start | bytes 8388608 | tf_op jit(solution)/shard_map/all_to_all | solution.py:1021
  109.2 65.5 %all-to-all-start.2 = ((f32[128,72,128]{2,1,0:T(8,128)}), f32[128,72,128]{2,1,0:T(8,128)}, u32[]{:S(2)}, u32[]{:S(2)}) async-start(f32[128,72,128]{2,1,0:T(8,128)} %bitcast.18), calls=%async_computation.2 | async-start | bytes 9437184 | tf_op jit(solution)/shard_map/all_to_all | solution.py:1032
  119.1 52.1 %collective-permute-start = (f32[2,1,8,2048]{3,2,1,0:T(8,128)S(1)}, f32[2,1,8,2048]{3,2,1,0:T(8,128)S(1)}, u32[]{:S(2)}, u32[]{:S(2)}) collective-permute-start(f32[2,1,8,2048]{3,2,1,0:T(8,128)S(1)} %get-tuple-element.26), channel_id=1, source_target_pairs={{0,1},{1,2},{2,3},{3,4},{4,5},{5,6},{6,7},{8,9},{9,10},{10,11},{11... | collective-permute-start | bytes 393224 | tf_op jit(solution)/shard_map/ppermute | solution.py:981
  122.5 51.3 %collective-permute-start.1 = (f32[2,1,8,2048]{3,2,1,0:T(8,128)S(1)}, f32[2,1,8,2048]{3,2,1,0:T(8,128)S(1)}, u32[]{:S(2)}, u32[]{:S(2)}) collective-permute-start(f32[2,1,8,2048]{3,2,1,0:T(8,128)S(1)} %get-tuple-element.25), channel_id=1, source_target_pairs={{1,0},{2,1},{3,2},{4,3},{5,4},{6,5},{7,6},{9,8},{10,9},{11,10},{12... | collective-permute-start | bytes 393224 | tf_op jit(solution)/shard_map/ppermute | solution.py:981
  171.2 3.5 %copy-start.1 = (f32[2,1,8,2048]{3,2,1,0:T(8,128)}, f32[2,1,8,2048]{3,2,1,0:T(8,128)S(1)}, u32[]{:S(2)}) copy-start(f32[2,1,8,2048]{3,2,1,0:T(8,128)S(1)} %collective-permute-done.xt_ref) | copy-start | bytes 393220
  173.8 1.0 copy-start.2
  186.1 29.3 %collective-permute-start.8 = (f32[264,2048]{1,0:T(8,128)}, f32[264,2048]{1,0:T(8,128)}, u32[]{:S(2)}, u32[]{:S(2)}) collective-permute-start(f32[264,2048]{1,0:T(8,128)} %get-tuple-element.22.own.parts_in), channel_id=1, source_target_pairs={{8,0},{16,8},{24,16},{32,24},{40,32},{48,40},{56,48},{64,56},{72,6... | collective-permute-start | bytes 6488072 | tf_op jit(solution)/shard_map/ppermute | solution.py:981
  190.9 30.5 %collective-permute-start.9 = (f32[264,2048]{1,0:T(8,128)}, f32[264,2048]{1,0:T(8,128)}, u32[]{:S(2)}, u32[]{:S(2)}) collective-permute-start(f32[264,2048]{1,0:T(8,128)} %get-tuple-element.22.own.parts_in), channel_id=1, source_target_pairs={{0,8},{8,16},{16,24},{24,32},{32,40},{40,48},{48,56},{56,64},{64,7... | collective-permute-start | bytes 6488072 | tf_op jit(solution)/shard_map/ppermute | solution.py:981
  192.8 45.8 %collective-permute-start.2 = (f32[264,2048]{1,0:T(8,128)}, f32[264,2048]{1,0:T(8,128)}, u32[]{:S(2)}, u32[]{:S(2)}) collective-permute-start(f32[264,2048]{1,0:T(8,128)} %get-tuple-element.18.own.parts_in), channel_id=1, source_target_pairs={{8,0},{16,8},{24,16},{32,24},{40,32},{48,40},{56,48},{64,56},{72,6... | collective-permute-start | bytes 6488072 | tf_op jit(solution)/shard_map/ppermute | solution.py:981
  198.6 46.0 %collective-permute-start.3 = (f32[264,2048]{1,0:T(8,128)}, f32[264,2048]{1,0:T(8,128)}, u32[]{:S(2)}, u32[]{:S(2)}) collective-permute-start(f32[264,2048]{1,0:T(8,128)} %get-tuple-element.18.own.parts_in), channel_id=1, source_target_pairs={{0,8},{8,16},{16,24},{24,32},{32,40},{40,48},{48,56},{56,64},{64,7... | collective-permute-start | bytes 6488072 | tf_op jit(solution)/shard_map/ppermute | solution.py:981
  232.8 32.8 %collective-permute-start.10 = (f32[264,2048]{1,0:T(8,128)}, f32[264,2048]{1,0:T(8,128)}, u32[]{:S(2)}, u32[]{:S(2)}) collective-permute-start(f32[264,2048]{1,0:T(8,128)} %get-tuple-element.23.own_in), channel_id=1, source_target_pairs={{8,0},{16,8},{24,16},{32,24},{40,32},{48,40},{56,48},{64,56},{72,6... | collective-permute-start | bytes 6488072 | tf_op jit(solution)/shard_map/ppermute | solution.py:981
  234.7 33.0 %collective-permute-start.11 = (f32[264,2048]{1,0:T(8,128)}, f32[264,2048]{1,0:T(8,128)}, u32[]{:S(2)}, u32[]{:S(2)}) collective-permute-start(f32[264,2048]{1,0:T(8,128)} %get-tuple-element.23.own_in), channel_id=1, source_target_pairs={{0,8},{8,16},{16,24},{24,32},{32,40},{40,48},{48,56},{56,64},{64,7... | collective-permute-start | bytes 6488072 | tf_op jit(solution)/shard_map/ppermute | solution.py:981
  255.9 23.1 %collective-permute-start.6 = (f32[144,2048]{1,0:T(8,128)}, f32[144,2048]{1,0:T(8,128)}, u32[]{:S(2)}, u32[]{:S(2)}) collective-permute-start(f32[144,2048]{1,0:T(8,128)} %get-tuple-element.21.own_in), channel_id=1, source_target_pairs={{8,0},{16,8},{24,16},{32,24},{40,32},{48,40},{56,48},{64,56},{72,6... | collective-permute-start | bytes 3538952 | tf_op jit(solution)/shard_map/ppermute | solution.py:981
  257.9 22.5 %collective-permute-start.7 = (f32[144,2048]{1,0:T(8,128)}, f32[144,2048]{1,0:T(8,128)}, u32[]{:S(2)}, u32[]{:S(2)}) collective-permute-start(f32[144,2048]{1,0:T(8,128)} %get-tuple-element.21.own_in), channel_id=1, source_target_pairs={{0,8},{8,16},{16,24},{24,32},{32,40},{40,48},{48,56},{56,64},{64,7... | collective-permute-start | bytes 3538952 | tf_op jit(solution)/shard_map/ppermute | solution.py:981
  260.3 27.2 %collective-permute-start.4 = (f32[144,2048]{1,0:T(8,128)}, f32[144,2048]{1,0:T(8,128)}, u32[]{:S(2)}, u32[]{:S(2)}) collective-permute-start(f32[144,2048]{1,0:T(8,128)} %get-tuple-element.19.own_in), channel_id=1, source_target_pairs={{8,0},{16,8},{24,16},{32,24},{40,32},{48,40},{56,48},{64,56},{72,6... | collective-permute-start | bytes 3538952 | tf_op jit(solution)/shard_map/ppermute | solution.py:981
  265.6 27.4 %collective-permute-start.5 = (f32[144,2048]{1,0:T(8,128)}, f32[144,2048]{1,0:T(8,128)}, u32[]{:S(2)}, u32[]{:S(2)}) collective-permute-start(f32[144,2048]{1,0:T(8,128)} %get-tuple-element.19.own_in), channel_id=1, source_target_pairs={{0,8},{8,16},{16,24},{24,32},{32,40},{40,48},{48,56},{56,64},{64,7... | collective-permute-start | bytes 3538952 | tf_op jit(solution)/shard_map/ppermute | solution.py:981
